TPU v7x, 32 devices: a whole 2x2x4 slice. The times are simulated.
32 devices in a mesh: seq: 4 (over z), batch: 8 (over y, x, core).
Axes of the slice: x: 2, y: 2, z: 4, core: 2. Of those that a mesh axis runs over, the one named last changes fastest.
Arguments:
- tokens: bfloat16 [16, 1024, 2048], P('batch', 'seq'), may hold values from -6 to 6
- segments: int32 [16, 1024], P('batch', 'seq'), may hold values from 0 to 5, as said below
- norm1_gain: float32 [2048], replicated, may hold values from 0.1 to 1.9
- w_query: bfloat16 [2048, 2048], replicated, may hold values from -0.125 to 0.125
- w_key: bfloat16 [2048, 128], replicated, may hold values from -0.125 to 0.125
- w_value: bfloat16 [2048, 128], replicated, may hold values from -0.125 to 0.125
- w_output: bfloat16 [2048, 2048], replicated, may hold values from -1 to 1
- norm2_gain: float32 [2048], replicated, may hold values from 0.1 to 1.9
- w_gate: bfloat16 [2048, 5632], replicated, may hold values from -0.125 to 0.125
- w_up: bfloat16 [2048, 5632], replicated, may hold values from -0.125 to 0.125
- w_down: bfloat16 [5632, 2048], replicated, may hold values from -0.15625 to 0.15625
- cotangent: bfloat16 [16, 1024, 2048], P('batch', 'seq'), may hold values from -6 to 6
Outputs:
- output: bfloat16 [16, 1024, 2048], P('batch', 'seq')
- grad_tokens: float32 [16, 1024, 2048], P('batch', 'seq')
- grad_norm1: float32 [2048], P(('seq', 'batch'))
- grad_query: float32 [2048, 2048], P(('seq', 'batch'))
- grad_key: float32 [2048, 128], P(('seq', 'batch'))
- grad_value: float32 [2048, 128], P(('seq', 'batch'))
- grad_output: float32 [2048, 2048], P(('seq', 'batch'))
- grad_norm2: float32 [2048], P(('seq', 'batch'))
- grad_gate: float32 [2048, 5632], P(('seq', 'batch'))
- grad_up: float32 [2048, 5632], P(('seq', 'batch'))
- grad_down: float32 [5632, 2048], P(('seq', 'batch'))
Inputs may be any that keep to these rules, and one draw needn't show every extreme that they name: `segments`: segment ids number the documents of a sequence from 0 upward and never fall along it. Of the 2 sequences on one index of batch, one, drawn from the seed, is a single document; each other one holds 6 documents of random lengths.
All inputs are finite; a program needn't handle non-finite values.
Results may differ from a plain program's by a relative error of at most 0.015.
Values may be sent and summed in bfloat16 or wider, within the bound.
No kernel may reach another device: no remote copies, remote signals or barrier semaphores. Data moves between devices by JAX's collectives and lax.ppermute only.
A program may use at most 448 MiB of HBM per device.

v0:
```python
import math

import jax
import jax.numpy as jnp
from jax import lax
from jax.sharding import PartitionSpec as P

WINDOW = 512


eps = 1e-05
rope_base = 10000.0
masked = -1e30
big_index = 1 << 30


def carried_in(shard, axis, combine, identity):
    size, here = (lax.axis_size(axis), lax.axis_index(axis))
    everything = jax.tree.map(lambda part: lax.all_gather(part, axis), shard)
    start = jax.tree.map(
        lambda part, zero: jnp.broadcast_to(jnp.asarray(zero, part.dtype), part.shape),
        shard,
        identity,
    )

    def step(k, before):
        reached = k < here
        new = combine(before, jax.tree.map(lambda part: part[k], everything))
        return jax.tree.map(lambda a, b: jnp.where(reached, a, b), new, before)

    return lax.fori_loop(0, size, step, start)


def passed_along(block, axis, distance):
    devices = range(lax.axis_size(axis))
    route = [(i - distance, i) for i in devices if i - distance in devices]
    return lax.ppermute(block, axis, route)


def rope_turn(tensor, positions, sign):
    half = tensor.shape[-1] // 2
    freq = jnp.exp(-math.log(rope_base) * jnp.arange(half, dtype=jnp.float32) / half)
    angle = positions[..., None] * freq
    cosine = jnp.cos(angle)
    sine = sign * jnp.sin(angle)
    first_half = tensor[..., :half]
    second_half = tensor[..., half:]
    return jnp.concatenate(
        [first_half * cosine - second_half * sine, first_half * sine + second_half * cosine],
        axis=-1,
    )


def norm_back(grad_rows, rows, inverse):
    return inverse * (
        grad_rows - rows * inverse * inverse * jnp.mean(grad_rows * rows, axis=1, keepdims=True)
    )


def join_docs(earlier, later):
    early_begin, early_seg, early_start = earlier
    late_begin, late_seg, late_start = later
    vacant = late_seg < 0
    follows = (late_seg == early_seg) & (late_start == late_begin)
    begin_all = jnp.minimum(early_begin, late_begin)
    seg_all = jnp.where(vacant, early_seg, late_seg)
    start_all = jnp.where(vacant | follows, early_start, late_start)
    return (begin_all, seg_all, start_all)


def score_block(q_block, k_block, query_index, key_index, start_block, score_scale):
    raw = jnp.einsum("sqhd,skd->shqk", q_block, k_block, preferred_element_type=jnp.float32)
    allow = (
        (key_index[None, None, :] <= query_index[None, :, None])
        & (query_index[None, :, None] - key_index[None, None, :] < WINDOW)
        & (key_index[None, None, :] >= start_block[:, :, None])
    )
    allow = allow[:, None]
    return (jnp.where(allow, raw * score_scale, masked), allow)


def shards(
    tokens,
    segments,
    norm1_gain,
    w_query,
    w_key,
    w_value,
    w_output,
    norm2_gain,
    w_gate,
    w_up,
    w_down,
    cotangent,
):
    groups, stretch_len, width = tokens.shape
    head_dim = w_key.shape[1]
    head_count = w_query.shape[1] // head_dim
    hop_count = (WINDOW + stretch_len - 1) // stretch_len
    block_rows = min(stretch_len, 512)
    blocks = stretch_len // block_rows
    key_span = block_rows + WINDOW
    key_base = hop_count * stretch_len - WINDOW
    score_scale = 1.0 / math.sqrt(head_dim)
    total_rows = groups * stretch_len
    seq_rank = lax.axis_index("seq")
    offset = seq_rank * stretch_len
    token_index = offset + jnp.arange(stretch_len, dtype=jnp.int32)
    last_seg = segments[:, -1]
    first_of_last = jnp.min(
        jnp.where(segments == last_seg[:, None], token_index[None, :], big_index), axis=1
    )
    begins = jnp.zeros((groups,), jnp.int32) + offset
    identity = (
        jnp.full((groups,), big_index, jnp.int32),
        jnp.full((groups,), -1, jnp.int32),
        jnp.zeros((groups,), jnp.int32),
    )
    before_begin, before_seg, before_start = carried_in(
        (begins, last_seg, first_of_last), "seq", join_docs, identity
    )
    previous = jnp.concatenate([before_seg[:, None], segments[:, :-1]], axis=1)
    marks = jnp.where(segments != previous, token_index[None, :], -1)
    starts = lax.cummax(marks, axis=1)
    starts = jnp.where(starts >= 0, starts, before_start[:, None])
    positions = (token_index[None, :] - starts).astype(jnp.float32)
    x_rows = tokens.reshape(total_rows, width).astype(jnp.float32)
    inverse_one = lax.rsqrt(jnp.mean(x_rows * x_rows, axis=1, keepdims=True) + eps)
    normed = (x_rows * inverse_one * norm1_gain).astype(jnp.bfloat16)
    query_lin = jnp.dot(normed, w_query, preferred_element_type=jnp.float32).reshape(
        groups, stretch_len, head_count, head_dim
    )
    queries = rope_turn(query_lin, positions[:, :, None], 1.0).astype(jnp.bfloat16)
    key_lin = jnp.dot(normed, w_key, preferred_element_type=jnp.float32).reshape(
        groups, stretch_len, head_dim
    )
    key_rot = rope_turn(key_lin, positions, 1.0).astype(jnp.bfloat16)
    value_rot = (
        jnp.dot(normed, w_value, preferred_element_type=jnp.float32)
        .reshape(groups, stretch_len, head_dim)
        .astype(jnp.bfloat16)
    )
    earlier = [
        passed_along((key_rot, value_rot), "seq", distance) for distance in range(hop_count, 0, -1)
    ]
    key_all = jnp.concatenate([piece[0] for piece in earlier] + [key_rot], axis=1)
    value_all = jnp.concatenate([piece[1] for piece in earlier] + [value_rot], axis=1)
    key_first = (seq_rank - hop_count) * stretch_len + key_base

    def block_views(block_index):
        first = block_index * block_rows
        query_index = offset + first + jnp.arange(block_rows, dtype=jnp.int32)
        key_index = key_first + first + jnp.arange(key_span, dtype=jnp.int32)
        scores, allow = score_block(queries, key_all, query_index, key_index, starts, score_scale)
        return (first, queries, key_all, value_all, scores, allow)

    def attend(block_index):
        first, q_block, k_block, v_block, scores, allow = block_views(block_index)
        top = jnp.max(scores, axis=-1, keepdims=True)
        expo = jnp.exp(scores - top)
        total = jnp.sum(expo, axis=-1, keepdims=True)
        probs_low = (expo / total).astype(jnp.bfloat16)
        attended_block = jnp.einsum(
            "shqk,skd->sqhd", probs_low, v_block, preferred_element_type=jnp.float32
        ).astype(jnp.bfloat16)
        return (attended_block, top + jnp.log(total))

    block_list = jnp.arange(blocks, dtype=jnp.int32)
    attended_parts, log_totals = lax.map(attend, block_list)
    attended = attended_parts.transpose(1, 0, 2, 3, 4).reshape(total_rows, head_count * head_dim)
    mid = x_rows + jnp.dot(attended, w_output, preferred_element_type=jnp.float32)
    inverse_two = lax.rsqrt(jnp.mean(mid * mid, axis=1, keepdims=True) + eps)
    normed_two = (mid * inverse_two * norm2_gain).astype(jnp.bfloat16)
    gate_lin = jnp.dot(normed_two, w_gate, preferred_element_type=jnp.float32)
    up_lin = jnp.dot(normed_two, w_up, preferred_element_type=jnp.float32)
    sigmoid_gate = jax.nn.sigmoid(gate_lin)
    silu_gate = gate_lin * sigmoid_gate
    hidden = (silu_gate * up_lin).astype(jnp.bfloat16)
    result = mid + jnp.dot(hidden, w_down, preferred_element_type=jnp.float32)
    output = result.astype(jnp.bfloat16).reshape(groups, stretch_len, width)
    d_result = cotangent.reshape(total_rows, width)
    grad_down = jnp.einsum("tf,td->fd", hidden, d_result, preferred_element_type=jnp.float32)
    d_hidden = jnp.einsum("td,fd->tf", d_result, w_down, preferred_element_type=jnp.float32)
    d_gate = (d_hidden * up_lin * sigmoid_gate * (1.0 + gate_lin * (1.0 - sigmoid_gate))).astype(
        jnp.bfloat16
    )
    d_up = (d_hidden * silu_gate).astype(jnp.bfloat16)
    grad_gate = jnp.einsum("td,tf->df", normed_two, d_gate, preferred_element_type=jnp.float32)
    grad_up = jnp.einsum("td,tf->df", normed_two, d_up, preferred_element_type=jnp.float32)
    d_normed_two = jnp.einsum(
        "tf,df->td", d_gate, w_gate, preferred_element_type=jnp.float32
    ) + jnp.einsum("tf,df->td", d_up, w_up, preferred_element_type=jnp.float32)
    grad_norm2 = jnp.sum(d_normed_two * mid * inverse_two, axis=0)
    d_mid = d_result.astype(jnp.float32) + norm_back(d_normed_two * norm2_gain, mid, inverse_two)
    d_branch = d_mid.astype(jnp.bfloat16)
    grad_output = jnp.einsum("tc,td->cd", attended, d_branch, preferred_element_type=jnp.float32)
    d_attended = jnp.einsum(
        "td,cd->tc", d_branch, w_output, preferred_element_type=jnp.float32
    ).astype(jnp.bfloat16)
    d_attended = d_attended.reshape(groups, stretch_len, head_count, head_dim)

    def attend_back(carried, block_input):
        key_grad, value_grad = carried
        block_index, log_total = block_input
        first, q_block, k_block, v_block, scores, allow = block_views(block_index)
        probs = jnp.where(allow, jnp.exp(scores - log_total), 0.0)
        probs_low = probs.astype(jnp.bfloat16)
        d_probs = jnp.einsum(
            "sqhd,skd->shqk", d_attended, v_block, preferred_element_type=jnp.float32
        )
        value_piece = jnp.einsum(
            "shqk,sqhd->skd", probs_low, d_attended, preferred_element_type=jnp.float32
        )
        inner = jnp.sum(probs * d_probs, axis=-1, keepdims=True)
        d_scores = (probs * (d_probs - inner) * score_scale).astype(jnp.bfloat16)
        query_piece = jnp.einsum(
            "shqk,skd->sqhd", d_scores, k_block, preferred_element_type=jnp.float32
        )
        key_piece = jnp.einsum(
            "shqk,sqhd->skd", d_scores, q_block, preferred_element_type=jnp.float32
        )
        key_grad = key_grad + key_piece
        value_grad = value_grad + value_piece
        return ((key_grad, value_grad), query_piece)

    zero_keys = jnp.zeros(key_all.shape, jnp.float32)
    (key_grad, value_grad), query_parts = lax.scan(
        attend_back, (zero_keys, zero_keys), (block_list, log_totals)
    )
    d_queries = query_parts.transpose(1, 0, 2, 3, 4).reshape(
        groups, stretch_len, head_count, head_dim
    )
    own_key = key_grad[:, hop_count * stretch_len :]
    own_value = value_grad[:, hop_count * stretch_len :]
    for distance in range(1, hop_count + 1):
        lower = (hop_count - distance) * stretch_len
        back_key, back_value = (
            passed_along(
                key_grad[:, lower : lower + stretch_len].astype(jnp.bfloat16), "seq", -distance
            ).astype(jnp.float32),
            passed_along(
                value_grad[:, lower : lower + stretch_len].astype(jnp.bfloat16), "seq", -distance
            ).astype(jnp.float32),
        )
        own_key = own_key + back_key
        own_value = own_value + back_value
    d_query = (
        rope_turn(d_queries, positions[:, :, None], -1.0)
        .astype(jnp.bfloat16)
        .reshape(total_rows, head_count * head_dim)
    )
    d_key = rope_turn(own_key, positions, -1.0).astype(jnp.bfloat16).reshape(total_rows, head_dim)
    d_value = own_value.astype(jnp.bfloat16).reshape(total_rows, head_dim)
    grad_query = jnp.einsum("td,tc->dc", normed, d_query, preferred_element_type=jnp.float32)
    grad_key = jnp.einsum("td,tc->dc", normed, d_key, preferred_element_type=jnp.float32)
    grad_value = jnp.einsum("td,tc->dc", normed, d_value, preferred_element_type=jnp.float32)
    d_normed = jnp.einsum("tc,dc->td", d_query, w_query, preferred_element_type=jnp.float32)
    d_normed = d_normed + jnp.einsum("tc,dc->td", d_key, w_key, preferred_element_type=jnp.float32)
    d_normed = d_normed + jnp.einsum(
        "tc,dc->td", d_value, w_value, preferred_element_type=jnp.float32
    )
    grad_norm1 = jnp.sum(d_normed * x_rows * inverse_one, axis=0)
    grad_tokens = (d_mid + norm_back(d_normed * norm1_gain, x_rows, inverse_one)).reshape(
        groups, stretch_len, width
    )
    summed = (
        lax.psum_scatter(grad_norm1, ("seq", "batch"), scatter_dimension=0, tiled=True),
        lax.psum_scatter(grad_query, ("seq", "batch"), scatter_dimension=0, tiled=True),
        lax.psum_scatter(grad_key, ("seq", "batch"), scatter_dimension=0, tiled=True),
        lax.psum_scatter(grad_value, ("seq", "batch"), scatter_dimension=0, tiled=True),
        lax.psum_scatter(grad_output, ("seq", "batch"), scatter_dimension=0, tiled=True),
        lax.psum_scatter(grad_norm2, ("seq", "batch"), scatter_dimension=0, tiled=True),
        lax.psum_scatter(grad_gate, ("seq", "batch"), scatter_dimension=0, tiled=True),
        lax.psum_scatter(grad_up, ("seq", "batch"), scatter_dimension=0, tiled=True),
        lax.psum_scatter(grad_down, ("seq", "batch"), scatter_dimension=0, tiled=True),
    )
    return (
        output,
        grad_tokens,
        summed[0],
        summed[1],
        summed[2],
        summed[3],
        summed[4],
        summed[5],
        summed[6],
        summed[7],
        summed[8],
    )


def solution(mesh):
    placed = (
        P("batch", "seq", None),
        P("batch", "seq"),
        P(),
        P(),
        P(),
        P(),
        P(),
        P(),
        P(),
        P(),
        P(),
        P("batch", "seq", None),
    )
    return jax.shard_map(
        shards,
        mesh=mesh,
        in_specs=placed,
        out_specs=(
            P("batch", "seq", None),
            P("batch", "seq", None),
            P(("seq", "batch")),
            P(("seq", "batch"), None),
            P(("seq", "batch"), None),
            P(("seq", "batch"), None),
            P(("seq", "batch"), None),
            P(("seq", "batch")),
            P(("seq", "batch"), None),
            P(("seq", "batch"), None),
            P(("seq", "batch"), None),
        ),
        check_vma=False,
    )
```

profile of v0, /device:TPU:5, one launch (start us, length us, event | category | flops | bytes accessed | tf_op | source)
XLA Modules:
  0.0 2473.7 jit_solution(1074377607935075986)
XLA Ops:
  7.3 2.1 fusion.26
  9.4 2.1 fusion.28
  12.3 3.2 collective-permute-start.1
  15.5 4.9 collective-permute-start
  23.3 4.0 all-reduce.5
  31.2 2.4 collective-permute-start.3
  33.6 5.0 collective-permute-start.2
  39.4 12.4 copy.85
  51.8 7.0 fusion.40
  59.9 11.8 fusion.15
  71.7 11.0 fusion.8
  83.3 12.7 convert_bitcast_fusion
  96.0 4.7 copy.58
  100.7 7.9 multiply_reduce_fusion.2
  108.7 2.0 copy-done.6
  111.1 19.8 fusion.112
  130.9 19.2 fusion.111
  150.1 26.9 %multiply_convert_fusion = (bf16[512,5632]{1,0:T(8,128)(2,1)}, bf16[512,5632]{1,0:T(8,128)(2,1)}, bf16[512,5632]{1,0:T(8,128)(2,1)}) fusion(f32[512,5632]{1,0:T(8,128)} %fusion.111, f32[512,5632]{1,0:T(8,128)} %fusion.112, bf16[512,2048]{1,0:T(8,128)(2,1)S(1)} %bitcast.256, bf16[5632,2048]{1,0:T(8,128)(2,1)} %param.24), kind=kOutput, calls=%fused_computation.28 | convolution fusion | flops 11854413824 | bytes 65536000 | tf_op jit(solution)/shard_map/td,fd->tf/dot_general | solution.py:183
  177.0 19.5 fusion.113
  196.5 19.5 multiply_reduce_fusion
  217.5 9.7 fusion.49
  228.2 12.5 fusion.110
  244.2 12.7 fusion.47
  256.8 35.6 %fusion.109 = (bf16[2,768,128]{1,2,0:T(8,128)(2,1)S(1)}, f32[2,768,128]{1,2,0:T(8,128)}) fusion(bf16[2,256,16,64]{1,3,2,0:T(8,128)(2,1)S(1)} %copy-done.23, bf16[2,256,16,64]{1,3,2,0:T(8,128)(2,1)S(1)} %copy-done.21, f32[2,768,256,16]{2,1,3,0:T(8,128)} %fusion.47, f32[2,16,256]{2,1,0:T(8,128)} %log_add_fusion, pred[2,256,768]{1,2,0:T(8,128)(4,1)S(1)} %copy-done.17, ...), kind=kOutput, calls=%fused_computation.167 | convolution fusion | flops 1696801536 | bytes 54034432 | tf_op jit(solution)/shard_map/while/body/eval_jaxpr/shqk,sqhd->skd/dot_general | solution.py:219
  295.9 36.9 %fusion.32 = f32[2,256,16,128]{1,3,2,0:T(8,128)} fusion(f32[2,768,256,16]{2,1,3,0:T(8,128)} %fusion.47, f32[2,16,256]{2,1,0:T(8,128)} %log_add_fusion, pred[2,256,768]{1,2,0:T(8,128)(4,1)S(1)} %copy-done.17, f32[2,768,256,16]{2,1,3,0:T(8,128)} %get-tuple-element.274, bf16[2,256,64]{1,2,0:T(8,128)(2,1)S(1)} %copy-done.29, ...), kind=kOutput, calls=%fused_computation.67 | convolution fusion | flops 1693983488 | bytes 55345152 | tf_op jit(solution)/shard_map/while/body/eval_jaxpr/shqk,skd->sqhd/dot_general | solution.py:216
  334.0 1.7 convolution_bitcast_fusion
  337.4 2.9 multiply_subtract_fusion
  340.4 1.5 maximum_convert_fusion
  341.9 4.9 copy.61
  348.4 7.1 fusion.35
  355.6 4.1 fusion.31
  359.6 1.7 fusion.115
  361.5 13.2 fusion.37
  374.7 9.9 fusion.33
  384.7 1.5 copy-done.10
  386.2 21.1 fusion.117
  407.5 20.9 fusion.116
  428.4 1.5 copy-done.15
  429.9 20.9 fusion.118
  450.9 19.9 add_convert_fusion
  470.9 44.8 %all-reduce.6 = (f32[2048]{0:T(1024)S(1)}, f32[2048]{0:T(1024)S(1)}) all-reduce(f32[2048]{0:T(1024)S(1)} %copy-done.35, f32[2048]{0:T(1024)S(1)} %copy-done.43), channel_id=5, replica_groups=mesh['seq'=4,'batch'=8] {'seq','batch'}, use_global_device_ids=true, to_apply=%region_13.14.clone | all-reduce | flops 4096 | bytes 32768
  516.9 6.7 fusion.24
  523.6 72.8 %reduce-scatter.10.cloned.1.call-done = f32[64,128]{1,0:T(8,128)} async-done(((f32[2048,128]{1,0:T(8,128)}), f32[64,128]{1,0:T(8,128)}) %reduce-scatter.10.cloned.1.call-update) | async-done | bytes 32784 | tf_op jit(solution)/shard_map/reduce_scatter | solution.py:269
  596.4 197.5 %reduce-scatter.14.cloned.1.call-done = f32[64,2048]{1,0:T(8,128)} async-done(((f32[2048,2048]{1,0:T(8,128)}), f32[64,2048]{1,0:T(8,128)}) %reduce-scatter.14.cloned.1.call-update) | async-done | bytes 524304 | tf_op jit(solution)/shard_map/reduce_scatter | solution.py:271
  793.9 187.2 %reduce-scatter.8.cloned.1.call-done = f32[64,2048]{1,0:T(8,128)} async-done(((f32[2048,2048]{1,0:T(8,128)}), f32[64,2048]{1,0:T(8,128)}) %reduce-scatter.8.cloned.1.call-update) | async-done | bytes 524304 | tf_op jit(solution)/shard_map/reduce_scatter | solution.py:268
  981.1 493.8 %reduce-scatter.18.cloned.1.call-done = f32[64,5632]{1,0:T(8,128)} async-done(((f32[2048,5632]{1,0:T(8,128)}), f32[64,5632]{1,0:T(8,128)}) %reduce-scatter.18.cloned.1.call-update) | async-done | bytes 1441808 | tf_op jit(solution)/shard_map/reduce_scatter | solution.py:274
  1474.9 495.8 %reduce-scatter.16.cloned.1.call-done = f32[64,5632]{1,0:T(8,128)} async-done(((f32[2048,5632]{1,0:T(8,128)}), f32[64,5632]{1,0:T(8,128)}) %reduce-scatter.16.cloned.1.call-update) | async-done | bytes 1441808 | tf_op jit(solution)/shard_map/reduce_scatter | solution.py:273
  1970.7 496.0 %reduce-scatter.20.cloned.1.call-done = f32[176,2048]{1,0:T(8,128)} async-done(((f32[5632,2048]{1,0:T(8,128)}), f32[176,2048]{1,0:T(8,128)}) %reduce-scatter.20.cloned.1.call-update) | async-done | bytes 1441808 | tf_op jit(solution)/shard_map/reduce_scatter | solution.py:275
  (176 shorter events, 25.1 us)
Async XLA Ops:
  7.2 13.4 copy-start.46
  7.2 13.2 copy-start.39
  7.2 21.7 copy-start.12
  7.2 516.4 %reduce-scatter.12.cloned.1.call-start = ((), (), s32[]{:S(2)}) async-start(), calls=%async_computation.9 | async-start | bytes 1081344 | tf_op jit(solution)/shard_map/reduce_scatter | solution.py:270
  11.6 40.2 %copy-start.1 = (bf16[2,256,2048]{2,1,0:T(8,128)(2,1)}, bf16[2,256,2048]{2,1,0:T(8,128)(2,1)S(1)}, u32[]{:S(2)}) copy-start(bf16[2,256,2048]{2,1,0:T(8,128)(2,1)S(1)} %fusion.28) | copy-start | bytes 6291460
  12.3 71.0 %copy-start.24 = (bf16[2,256,128]{2,1,0:T(8,128)(2,1)}, bf16[2,256,128]{2,1,0:T(8,128)(2,1)S(1)}, u32[]{:S(2)}) copy-start(bf16[2,256,128]{2,1,0:T(8,128)(2,1)S(1)} %convolution_convert_fusion.1) | copy-start | bytes 393220
  12.3 71.0 %collective-permute-start.1 = (bf16[2,256,128]{2,1,0:T(8,128)(2,1)S(1)}, bf16[2,256,128]{2,1,0:T(8,128)(2,1)S(1)}, u32[]{:S(2)}, u32[]{:S(2)}) collective-permute-start(bf16[2,256,128]{2,1,0:T(8,128)(2,1)S(1)} %convolution_convert_fusion.1), channel_id=1, source_target_pairs={{0,8},{8,16},{16,24},{1,9},{9,17},{17,25},{2,10},{10,18},{18,26},{... | collective-permute-start | bytes 393224 | tf_op jit(solution)/shard_map/ppermute | solution.py:37
  15.5 67.8 %collective-permute-start = (bf16[2,256,128]{2,1,0:T(8,128)(2,1)S(1)}, bf16[2,256,128]{2,1,0:T(8,128)(2,1)}, u32[]{:S(2)}, u32[]{:S(2)}) collective-permute-start(bf16[2,256,128]{2,1,0:T(8,128)(2,1)S(1)} %convolution_convert_fusion.1), channel_id=1, source_target_pairs={{0,16},{8,24},{1,17},{9,25},{2,18},{10,26},{3,19},{11,27},{4,20},{... | collective-permute-start | bytes 393224 | tf_op jit(solution)/shard_map/ppermute | solution.py:37
  20.4 31.4 %copy-start.44 = (f32[64]{0:T(128)}, f32[64]{0:T(128)S(1)}, u32[]{:S(2)}) copy-start(f32[64]{0:T(128)S(1)} %multiply_exponential_fusion) | copy-start | bytes 772
  29.8 9.3 copy-start.37
  30.4 28.3 %copy-start.18 = (f32[2,256,64]{1,2,0:T(8,128)}, f32[2,256,64]{1,2,0:T(8,128)S(1)}, u32[]{:S(2)}) copy-start(f32[2,256,64]{1,2,0:T(8,128)S(1)} %get-tuple-element.270) | copy-start | bytes 393220
  30.4 29.5 %copy-start.26 = (bf16[2,256,64]{1,2,0:T(8,128)(2,1)}, bf16[2,256,64]{1,2,0:T(8,128)(2,1)S(1)}, u32[]{:S(2)}) copy-start(bf16[2,256,64]{1,2,0:T(8,128)(2,1)S(1)} %get-tuple-element.266) | copy-start | bytes 196612
  30.4 29.5 %copy-start.28 = (bf16[2,256,64]{1,2,0:T(8,128)(2,1)}, bf16[2,256,64]{1,2,0:T(8,128)(2,1)S(1)}, u32[]{:S(2)}) copy-start(bf16[2,256,64]{1,2,0:T(8,128)(2,1)S(1)} %get-tuple-element.267) | copy-start | bytes 196612
  31.2 28.7 %collective-permute-start.3 = (bf16[2,256,128]{1,2,0:T(8,128)(2,1)}, bf16[2,256,128]{1,2,0:T(8,128)(2,1)}, u32[]{:S(2)}, u32[]{:S(2)}) collective-permute-start(bf16[2,256,128]{1,2,0:T(8,128)(2,1)} %pad_maximum_fusion.5), channel_id=1, source_target_pairs={{0,8},{8,16},{16,24},{1,9},{9,17},{17,25},{2,10},{10,18},{18,26},{... | collective-permute-start | bytes 393224 | tf_op jit(solution)/shard_map/ppermute | solution.py:37
  33.6 26.3 %collective-permute-start.2 = (bf16[2,256,128]{1,2,0:T(8,128)(2,1)}, bf16[2,256,128]{1,2,0:T(8,128)(2,1)}, u32[]{:S(2)}, u32[]{:S(2)}) collective-permute-start(bf16[2,256,128]{1,2,0:T(8,128)(2,1)} %pad_maximum_fusion.5), channel_id=1, source_target_pairs={{0,16},{8,24},{1,17},{9,25},{2,18},{10,26},{3,19},{11,27},{4,20},{... | collective-permute-start | bytes 393224 | tf_op jit(solution)/shard_map/ppermute | solution.py:37
  59.5 12.2 copy-start.20
  59.5 12.2 copy-start.22
  59.9 23.4 copy-start.16
  83.3 12.7 copy-start.30
  100.7 10.0 copy-start.34
  111.1 19.8 copy-start.9
  130.9 19.2 copy-start.14
  196.5 19.5 copy-start.7
  217.5 9.7 copy-start.8
  228.2 15.9 copy-start.25
  228.2 16.0 copy-start.31
  241.4 91.5 %collective-permute-start.6 = (bf16[2,256,128]{2,1,0:T(8,128)(2,1)}, bf16[2,256,128]{2,1,0:T(8,128)(2,1)}, u32[]{:S(2)}, u32[]{:S(2)}) collective-permute-start(bf16[2,256,128]{2,1,0:T(8,128)(2,1)} %get-tuple-element.260), channel_id=1, source_target_pairs={{8,0},{16,8},{24,16},{9,1},{17,9},{25,17},{10,2},{18,10},{26,18},{... | collective-permute-start | bytes 393224 | tf_op jit(solution)/shard_map/ppermute | solution.py:37
  242.7 14.1 copy-start.21
  242.7 14.1 copy-start.23
  242.7 90.2 %collective-permute-start.7 = (bf16[2,256,128]{2,1,0:T(8,128)(2,1)}, bf16[2,256,128]{2,1,0:T(8,128)(2,1)}, u32[]{:S(2)}, u32[]{:S(2)}) collective-permute-start(bf16[2,256,128]{2,1,0:T(8,128)(2,1)} %get-tuple-element.261), channel_id=1, source_target_pairs={{16,0},{24,8},{17,1},{25,9},{18,2},{26,10},{19,3},{27,11},{20,4},{... | collective-permute-start | bytes 393224 | tf_op jit(solution)/shard_map/ppermute | solution.py:37
  256.8 39.1 %copy-start.27 = (bf16[2,256,64]{1,2,0:T(8,128)(2,1)S(1)}, bf16[2,256,64]{1,2,0:T(8,128)(2,1)}, u32[]{:S(2)}) copy-start(bf16[2,256,64]{1,2,0:T(8,128)(2,1)} %copy-done.26) | copy-start | bytes 196612
  256.8 39.1 %copy-start.29 = (bf16[2,256,64]{1,2,0:T(8,128)(2,1)S(1)}, bf16[2,256,64]{1,2,0:T(8,128)(2,1)}, u32[]{:S(2)}) copy-start(bf16[2,256,64]{1,2,0:T(8,128)(2,1)} %copy-done.28) | copy-start | bytes 196612
  293.2 42.7 %collective-permute-start.4 = (bf16[2,256,128]{1,2,0:T(8,128)(2,1)}, bf16[2,256,128]{1,2,0:T(8,128)(2,1)S(1)}, u32[]{:S(2)}, u32[]{:S(2)}) collective-permute-start(bf16[2,256,128]{1,2,0:T(8,128)(2,1)} %get-tuple-element.262), channel_id=1, source_target_pairs={{8,0},{16,8},{24,16},{9,1},{17,9},{25,17},{10,2},{18,10},{26,18},{... | collective-permute-start | bytes 393224 | tf_op jit(solution)/shard_map/ppermute | solution.py:37
  294.5 39.6 %copy-start.2 = (bf16[2,256,2048]{2,1,0:T(8,128)(2,1)S(1)}, bf16[2,256,2048]{2,1,0:T(8,128)(2,1)}, u32[]{:S(2)}) copy-start(bf16[2,256,2048]{2,1,0:T(8,128)(2,1)} %copy-done.1) | copy-start | bytes 6291460
  294.5 41.4 %collective-permute-start.5 = (bf16[2,256,128]{1,2,0:T(8,128)(2,1)}, bf16[2,256,128]{1,2,0:T(8,128)(2,1)S(1)}, u32[]{:S(2)}, u32[]{:S(2)}) collective-permute-start(bf16[2,256,128]{1,2,0:T(8,128)(2,1)} %get-tuple-element.263), channel_id=1, source_target_pairs={{16,0},{24,8},{17,1},{25,9},{18,2},{26,10},{19,3},{27,11},{20,4},{... | collective-permute-start | bytes 393224 | tf_op jit(solution)/shard_map/ppermute | solution.py:37
  335.8 260.6 %reduce-scatter.10.cloned.1.call-start = ((), (), s32[]{:S(2)}) async-start(), calls=%async_computation.8 | async-start | bytes 1081344 | tf_op jit(solution)/shard_map/reduce_scatter | solution.py:269
  348.4 7.2 copy-start.40
  361.4 432.5 %reduce-scatter.14.cloned.1.call-start = ((), (), s32[]{:S(2)}) async-start(), calls=%async_computation.10 | async-start | bytes 17301504 | tf_op jit(solution)/shard_map/reduce_scatter | solution.py:271
  374.7 606.4 %reduce-scatter.8.cloned.1.call-start = ((), (), s32[]{:S(2)}) async-start(), calls=%async_computation.7 | async-start | bytes 17301504 | tf_op jit(solution)/shard_map/reduce_scatter | solution.py:268
  384.7 1090.2 %reduce-scatter.18.cloned.1.call-start = ((), (), s32[]{:S(2)}) async-start(), calls=%async_computation.12 | async-start | bytes 47579136 | tf_op jit(solution)/shard_map/reduce_scatter | solution.py:274
  407.4 1563.3 %reduce-scatter.16.cloned.1.call-start = ((), (), s32[]{:S(2)}) async-start(), calls=%async_computation.11 | async-start | bytes 47579136 | tf_op jit(solution)/shard_map/reduce_scatter | solution.py:273
  428.3 2038.3 %reduce-scatter.20.cloned.1.call-start = ((), (), s32[]{:S(2)}) async-start(), calls=%async_computation.13 | async-start | bytes 47579136 | tf_op jit(solution)/shard_map/reduce_scatter | solution.py:275
  450.9 20.0 copy-start.35
  450.9 20.0 copy-start.43
  450.9 66.0 %copy-start.42 = (f32[512]{0:T(512)S(1)}, f32[512]{0:T(512)}, u32[]{:S(2)}) copy-start(f32[512]{0:T(512)} %get-tuple-element.228) | copy-start | bytes 6148
  450.9 66.0 %copy-start.5 = (bf16[2,256,2048]{2,1,0:T(8,128)(2,1)S(1)}, bf16[2,256,2048]{2,1,0:T(8,128)(2,1)}, u32[]{:S(2)}) copy-start(bf16[2,256,2048]{2,1,0:T(8,128)(2,1)} %param.14) | copy-start | bytes 6291460
  450.9 66.0 %copy-start.33 = (f32[2048]{0:T(1024)S(1)}, f32[2048]{0:T(1024)}, u32[]{:S(2)}) copy-start(f32[2048]{0:T(1024)} %param.16) | copy-start | bytes 24580
  450.9 66.0 %copy-start.41 = (f32[1,2,2,128]{3,1,2,0:T(2,128)S(1)}, f32[1,2,2,128]{3,1,2,0:T(2,128)}, u32[]{:S(2)}) copy-start(f32[1,2,2,128]{3,1,2,0:T(2,128)} %copy.90) | copy-start | bytes 6148
  (14 other events, 51.3 us)
Sparse Core Ops, SparseCore 0:
  335.9 126.5 reduce-scatter.11
  465.4 130.9 reduce-scatter.9
  599.3 194.5 reduce-scatter.13
  796.6 184.4 reduce-scatter.7
  983.9 490.9 reduce-scatter.17
  1477.6 493.0 reduce-scatter.15
  1973.6 493.0 reduce-scatter.19
where the time goes:
time: 2480 us; the launch traced here: 2470 us
  waiting for transfers between devices  1940 us (78%)
  matrix products  374 us (15%)
  blocking collectives  48.8 us (2%)
  other arithmetic  35.5 us (1%)
  local copies, waits for them, and re-layouts  34.7 us (1%)
    reduce_scatter x1, waiting for transfers between devices, shards(): lax.psum_scatter(grad_down, ('seq', 'batch'), scatter_dimension=0, tiled=...  496 us
    reduce_scatter x1, waiting for transfers between devices, shards(): lax.psum_scatter(grad_gate, ('seq', 'batch'), scatter_dimension=0, tiled=...  496 us
    reduce_scatter x1, waiting for transfers between devices, shards(): lax.psum_scatter(grad_up, ('seq', 'batch'), scatter_dimension=0, tiled=True)  494 us
    reduce_scatter x1, waiting for transfers between devices, shards(): lax.psum_scatter(grad_output, ('seq', 'batch'), scatter_dimension=0, tile...  198 us
    reduce_scatter x1, waiting for transfers between devices, shards(): lax.psum_scatter(grad_query, ('seq', 'batch'), scatter_dimension=0, tiled...  187 us
    reduce_scatter x1, waiting for transfers between devices, shards(): lax.psum_scatter(grad_key, ('seq', 'batch'), scatter_dimension=0, tiled=T...  72.8 us
  transfers between devices with their start and end apart: 15, of which 6 were waited for; matrix products, arithmetic and copies ran while one was open for 11% of the time, Pallas kernels for 0%

commit v1 on v0

v1 whole, which is shorter than its diff:
```python
import functools
import math

import jax
import jax.numpy as jnp
from jax import lax
from jax.experimental import pallas as pl
from jax.experimental.pallas import tpu as pltpu
from jax.sharding import PartitionSpec as P

WINDOW = 512
eps = 1e-05
rope_base = 10000.0
masked = -1e30
big = 1 << 30
AXES = ("seq", "batch")
GROUP = 4
f32 = jnp.float32
bf16 = jnp.bfloat16


MIB = 2**20
ONCE = pl.Buffered(1)
ANY = pl.BlockSpec(memory_space=pl.ANY)
SCALE = 1.0
COST = dict(
    norm_keys=5, query=9, attend=30, project_out=11, down_back=20, feed=21, gate_send=11, up_send=11, down_send=11,
    gate_keep=12, up_keep=12, down_keep=12, dn2_away=20, dn2_near=22, out_away=11, out_near=13, mid_back=14,
    attend_back=29, w_out_send=7, w_out_keep=7, w_query_send=7, w_query_keep=7, tokens_back=14, output=5,
)


def call(kernel, name, args, deps=(), scalars=(), grid=(1,), in_specs=(), out_specs=None, out_shape=None, scratch=(), vmem=56, passes=()):
    n_s, n_a, n_d, n_p = len(scalars), len(args), len(deps), len(passes)
    several = isinstance(out_shape, (list, tuple))
    shapes, specs = (list(out_shape), list(out_specs)) if several else ([out_shape], [out_specs])
    n_o = len(shapes)

    def body(*refs):
        at = n_s + n_a + n_d + n_p
        kernel(*refs[: n_s + n_a], *refs[at : at + n_o], *refs[at + n_o + n_p :])

    out = pl.pallas_call(
        body,
        grid_spec=pltpu.PrefetchScalarGridSpec(
            num_scalar_prefetch=n_s,
            grid=grid,
            in_specs=list(in_specs) + [ANY] * (n_d + n_p),
            out_specs=specs + [ANY] * n_p,
            scratch_shapes=list(scratch),
        ),
        out_shape=shapes + [jax.ShapeDtypeStruct(p.shape, p.dtype) for p in passes],
        input_output_aliases={n_s + n_a + n_d + i: n_o + i for i in range(n_p)},
        compiler_params=pltpu.CompilerParams(vmem_limit_bytes=vmem * MIB),
        cost_estimate=pl.CostEstimate(flops=int(SCALE * COST[name] * 10**9), bytes_accessed=1, transcendentals=0),
        name=name,
    )(*scalars, *args, *deps, *passes)
    return out if several or passes else out[0]


def dot(a, b, ca, cb, out=f32):
    return lax.dot_general(a, b, (((ca,), (cb,)), ((), ())), preferred_element_type=f32).astype(out)


class Moves:
    def __init__(self):
        self.nz, self.nb = lax.axis_size("seq"), lax.axis_size("batch")
        self.z, self.b = lax.axis_index("seq"), lax.axis_index("batch")
        self.ny = self.nb // GROUP
        self.y = self.b // GROUP

    def flip(self, value, mask):
        nz, nb = self.nz, self.nb
        pairs = [(z * nb + b, z * nb + (b ^ mask)) for z in range(nz) for b in range(nb)]
        return lax.ppermute(value, AXES, pairs)

    def shift(self, value, axis, sources, step):
        nz, ny, nb = self.nz, self.ny, self.nb
        pairs = []
        for z in range(nz):
            for b in range(nb):
                y, q = b // GROUP, b % GROUP
                at, size = (z, nz) if axis == "z" else (y, ny)
                if at in sources and 0 <= at + step < size:
                    to = (z + step, y) if axis == "z" else (z, y + step)
                    pairs.append((z * nb + b, to[0] * nb + to[1] * GROUP + q))
        return lax.ppermute(value, AXES, pairs)

    def bit(self, mask):
        return (self.b // mask) % 2


def turn(u, cosine, sine):
    return u * cosine + pltpu.roll(u, 64, 1) * sine


def mask_bias(starts, rows, first_row, keys, first_key, hop):
    qi = lax.broadcasted_iota(jnp.int32, (rows, keys), 0) + (first_row + hop)
    kj = lax.broadcasted_iota(jnp.int32, (rows, keys), 1) + first_key
    allow = (kj <= qi) & (qi - kj < WINDOW) & (kj >= starts)
    return jnp.where(allow, 0.0, masked)


def fwd_kernel(q_ref, cos_ref, sin_ref, start_ref, k_ref, v_ref, o_ref, qr_ref, lse_ref, *, heads, rb, hop):
    rows = q_ref.shape[0]
    scale = 1.0 / math.sqrt(128)
    lses = []
    for r in range(rows // rb):
        sl = pl.ds(r * rb, rb)
        k0 = max(0, r * rb + hop - WINDOW)
        k0 -= k0 % 128
        k1 = (r + 1) * rb + hop
        bias = mask_bias(start_ref[sl, :], rb, r * rb, k1 - k0, k0, hop)
        cosine, sine = cos_ref[sl, :], sin_ref[sl, :]
        kk = k_ref[0, pl.ds(k0, k1 - k0), :]
        vv = v_ref[0, pl.ds(k0, k1 - k0), :]
        lse_row = []
        for h in range(heads):
            hs = pl.ds(h * 128, 128)
            qr = turn(q_ref[sl, hs], cosine, sine).astype(bf16)
            qr_ref[sl, hs] = qr
            s = dot(qr, kk, 1, 1) * scale + bias
            top = jnp.max(s, axis=1, keepdims=True)
            e = jnp.exp(s - top)
            total = jnp.sum(e, axis=1, keepdims=True)
            p = (e * (1.0 / total)).astype(bf16)
            o_ref[sl, hs] = dot(p, vv, 1, 0).astype(bf16)
            lse_row.append(top + jnp.log(total))
        lses.append(jnp.concatenate(lse_row, axis=1))
    lse_ref[0, 0] = jnp.concatenate(lses, axis=0)


def bwd_kernel(q_ref, o_ref, do_ref, lse_ref, cos_ref, sin_ref, start_ref, k_ref, v_ref, dq_ref, dk_ref, dv_ref, *, heads, rb, hop):
    rows = q_ref.shape[0]
    scale = 1.0 / math.sqrt(128)

    @pl.when(pl.program_id(1) == 0)
    def _():
        dk_ref[...] = jnp.zeros_like(dk_ref)
        dv_ref[...] = jnp.zeros_like(dv_ref)

    for r in range(rows // rb):
        sl = pl.ds(r * rb, rb)
        k0 = max(0, r * rb + hop - WINDOW)
        k0 -= k0 % 128
        k1 = (r + 1) * rb + hop
        ks = pl.ds(k0, k1 - k0)
        bias = mask_bias(start_ref[sl, :], rb, r * rb, k1 - k0, k0, hop)
        cosine, sine = cos_ref[sl, :], sin_ref[sl, :]
        kk, vv = k_ref[0, ks, :], v_ref[0, ks, :]
        dk = dv = None
        for h in range(heads):
            hs = pl.ds(h * 128, 128)
            q, do = q_ref[sl, hs], do_ref[sl, hs]
            inner = jnp.sum(do.astype(f32) * o_ref[sl, hs].astype(f32), axis=1, keepdims=True)
            s = dot(q, kk, 1, 1) * scale + bias
            p = jnp.exp(s - lse_ref[0, 0, sl, h : h + 1])
            dp = dot(do, vv, 1, 1)
            ds = (p * ((dp - inner) * scale)).astype(bf16)
            dq = dot(ds, kk, 1, 0)
            dq_ref[sl, hs] = turn(dq, cosine, -sine).astype(bf16)
            dkh = dot(ds, q, 0, 0)
            dvh = dot(p.astype(bf16), do, 0, 0)
            dk = dkh if dk is None else dk + dkh
            dv = dvh if dv is None else dv + dvh
        dk_ref[0, ks, :] += dk
        dv_ref[0, ks, :] += dv


HEADS = 4
ROWS = 128


def attention_specs(L, span):
    wide = pl.BlockSpec((L, HEADS * 128), lambda s, h: (s, h))
    table = pl.BlockSpec((L, 128), lambda s, h: (s, 0))
    starts = pl.BlockSpec((L, 1), lambda s, h: (s, 0))
    keys = pl.BlockSpec((1, span, 128), lambda s, h: (s, 0, 0))
    lse = pl.BlockSpec((1, 1, L, HEADS), lambda s, h: (s, h, 0, 0))
    return wide, table, starts, keys, lse


def attention(q_lin, cosine, sine, starts, keys, values, hop, deps=()):
    T, width = q_lin.shape
    groups, span, _ = keys.shape
    L = T // groups
    wide, table, start, key, lse = attention_specs(L, span)
    steps = width // (HEADS * 128)
    return call(
        functools.partial(fwd_kernel, heads=HEADS, rb=ROWS, hop=hop),
        "attend",
        (q_lin, cosine, sine, starts, keys, values),
        deps,
        grid=(groups, steps),
        in_specs=[wide, table, table, start, key, key],
        out_specs=[wide, wide, lse],
        out_shape=[
            jax.ShapeDtypeStruct((T, width), bf16),
            jax.ShapeDtypeStruct((T, width), bf16),
            jax.ShapeDtypeStruct((groups, steps, L, HEADS), f32),
        ],
    )


def attention_back(queries, attended, d_attended, lses, cosine, sine, starts, keys, values, hop, deps=()):
    T, width = queries.shape
    groups, span, _ = keys.shape
    L = T // groups
    wide, table, start, key, lse = attention_specs(L, span)
    steps = width // (HEADS * 128)
    return call(
        functools.partial(bwd_kernel, heads=HEADS, rb=ROWS, hop=hop),
        "attend_back",
        (queries, attended, d_attended, lses, cosine, sine, starts, keys, values),
        deps,
        grid=(groups, steps),
        in_specs=[wide, wide, wide, lse, table, table, start, key, key],
        out_specs=[wide, key, key],
        out_shape=[
            jax.ShapeDtypeStruct((T, width), bf16),
            jax.ShapeDtypeStruct((groups, span, 128), f32),
            jax.ShapeDtypeStruct((groups, span, 128), f32),
        ],
    )


def whole(a):
    return pl.BlockSpec(a.shape, lambda *i: (0,) * a.ndim, pipeline_mode=ONCE)


def shape(dims, dtype=bf16):
    return jax.ShapeDtypeStruct(dims, dtype)


def norm_keys(tokens, gain, w_kv, cosine, sine):
    T, D = tokens.shape
    block = 128
    hd = w_kv.shape[1] // 2

    def kernel(x_ref, g_ref, w_ref, c_ref, s_ref, n_ref, inv_ref, kv_ref):
        x = x_ref[...].astype(f32)
        inv = lax.rsqrt(jnp.mean(x * x, axis=1, keepdims=True) + eps)
        normed = (x * inv * g_ref[...]).astype(bf16)
        n_ref[...] = normed
        inv_ref[...] = inv
        kv = dot(normed, w_ref[...], 1, 0)
        kv_ref[:, :hd] = turn(kv[:, :hd], c_ref[...], s_ref[...]).astype(bf16)
        kv_ref[:, hd:] = kv[:, hd:].astype(bf16)

    row = lambda w: pl.BlockSpec((block, w), lambda i: (i, 0))
    return call(
        kernel, "norm_keys", (tokens, gain.reshape(1, D), w_kv, cosine, sine), grid=(T // block,),
        in_specs=[row(D), pl.BlockSpec((1, D), lambda i: (0, 0)), whole(w_kv), row(hd), row(hd)],
        out_specs=[row(D), row(1), row(2 * hd)],
        out_shape=[shape((T, D)), shape((T, 1), f32), shape((T, 2 * hd))],
        vmem=56,
    )


def project_query(normed, w_query, deps=()):
    T, D = normed.shape
    N = w_query.shape[1]
    block = 512

    def kernel(a_ref, b_ref, o_ref):
        o_ref[...] = dot(a_ref[...], b_ref[...], 1, 0)

    return call(
        kernel, "query", (normed, w_query), deps, grid=(N // block,),
        in_specs=[whole(normed), pl.BlockSpec((D, block), lambda i: (0, i))],
        out_specs=pl.BlockSpec((T, block), lambda i: (0, i)),
        out_shape=shape((T, N), f32),
        vmem=56,
    )


def project_out(attended, w_output, x_rows, gain, deps=(), passes=()):
    T, D = x_rows.shape
    block = 512
    steps = D // block

    def kernel(a_ref, w_ref, x_ref, g_ref, mid_ref, n_ref, inv_ref, sq_ref):
        i = pl.program_id(0)
        part = x_ref[...].astype(f32) + dot(a_ref[...], w_ref[...], 1, 0)
        mid_ref[:, pl.ds(i * block, block)] = part
        sq = jnp.sum(part * part, axis=1, keepdims=True)

        @pl.when(i == 0)
        def _():
            sq_ref[...] = sq

        @pl.when(i > 0)
        def _():
            sq_ref[...] += sq

        @pl.when(i == steps - 1)
        def _():
            inv = lax.rsqrt(sq_ref[...] * (1.0 / D) + eps)
            inv_ref[...] = inv
            n_ref[...] = (mid_ref[...] * inv * g_ref[...]).astype(bf16)

    full = lambda w: pl.BlockSpec((T, w), lambda i: (0, 0))
    return call(
        kernel, "project_out", (attended, w_output, x_rows, gain.reshape(1, D)), deps, grid=(steps,),
        in_specs=[whole(attended), pl.BlockSpec((D, block), lambda i: (0, i)), pl.BlockSpec((T, block), lambda i: (0, i)), pl.BlockSpec((1, D), lambda i: (0, 0))],
        out_specs=[full(D), full(D), full(1)],
        out_shape=[shape((T, D), f32), shape((T, D)), shape((T, 1), f32)],
        scratch=[pltpu.VMEM((T, 1), f32)],
        passes=passes,
    )


def of_pieces(pieces, block, order=None, rows=None):
    order = order or range(len(pieces))
    rows = rows or [(0, p.shape[0]) for p in pieces]
    specs = [None] * len(pieces)
    starts, at = [None] * len(pieces), 0
    for k in order:
        first, n = rows[k][0] // block, rows[k][1] // block
        specs[k] = pl.BlockSpec(
            (block, pieces[k].shape[1]),
            lambda i, *s, at=at, first=first, n=n: (first + jnp.clip(i - at, 0, n - 1), 0),
        )
        starts[k] = at
        at += n
    order = list(order)

    def read(refs):
        i = pl.program_id(0)
        value = refs[order[0]][...]
        for k in order[1:]:
            value = jnp.where(i >= starts[k], refs[k][...], value)
        return value

    return specs, read, at


def quarter_columns(w):
    return pl.BlockSpec((w.shape[0], w.shape[1] // GROUP), lambda i, q: (0, q[0]), pipeline_mode=ONCE)


def quarter_rows(w):
    return pl.BlockSpec((w.shape[0] // GROUP, w.shape[1]), lambda i, q: (q[0], 0), pipeline_mode=ONCE)


def down_back(quarter, pieces, w_down, deps=()):
    block = 256
    fq = w_down.shape[0] // GROUP
    n = len(pieces)
    specs, read, steps = of_pieces(pieces, block)

    def kernel(q_ref, *refs):
        refs[n + 1][...] = dot(read(refs[:n]), refs[n][...], 1, 1, bf16)

    return call(
        kernel, "down_back", (*pieces, w_down), deps, (quarter,), grid=(steps,),
        in_specs=specs + [quarter_rows(w_down)],
        out_specs=pl.BlockSpec((block, fq), lambda i, q: (i, 0)),
        out_shape=shape((steps * block, fq)),
        vmem=56,
    )


def feed(quarter, pieces, d_hidden, first, w_gate, w_up, deps=(), passes=()):
    block = 256
    fq = w_gate.shape[1] // GROUP
    n = len(pieces)
    specs, read, steps = of_pieces(pieces, block)
    first = first // block

    def kernel(q_ref, *refs):
        dh_ref, wg_ref, wu_ref, h_ref, dg_ref, du_ref = refs[n:]
        value = read(refs[:n])
        gate = dot(value, wg_ref[...], 1, 0)
        up = dot(value, wu_ref[...], 1, 0)
        dh = dh_ref[...].astype(f32)
        sig = jax.nn.sigmoid(gate)
        silu = gate * sig
        h_ref[...] = (silu * up).astype(bf16)
        dg_ref[...] = (dh * up * (sig + silu * (1.0 - sig))).astype(bf16)
        du_ref[...] = (dh * silu).astype(bf16)

    out = pl.BlockSpec((block, fq), lambda i, q: (i, 0))
    return call(
        kernel, "feed", (*pieces, d_hidden, w_gate, w_up), deps, (quarter,), grid=(steps,),
        in_specs=specs
        + [pl.BlockSpec((block, fq), lambda i, q: (i + first, 0)), quarter_columns(w_gate), quarter_columns(w_up)],
        out_specs=[out] * 3,
        out_shape=[shape((steps * block, fq))] * 3,
        passes=passes,
    )


def partial_away(name, quarter, pairs, weights, cb, deps=()):
    block = 256
    T = pairs[0][0].shape[0] // 2
    D = weights[0].shape[1 - cb]
    specs, reads = [], []
    for pair in pairs:
        s, read, steps = of_pieces(pair, block, rows=[(T, T)] * 2)
        specs += s
        reads.append(read)
    m = len(weights)

    def kernel(q_ref, *refs):
        total = None
        for j in range(m):
            part = dot(reads[j](refs[2 * j : 2 * j + 2]), refs[2 * m + j][...], 1, cb)
            total = part if total is None else total + part
        refs[-1][0] = total.astype(bf16)

    per = T // block
    return call(
        kernel, name, (*[p for g in pairs for p in g], *weights), deps, (quarter,), grid=(steps,),
        in_specs=specs + [quarter_columns(w) if cb else quarter_rows(w) for w in weights],
        out_specs=pl.BlockSpec((1, block, D), lambda i, q: (i // per, i % per, 0)),
        out_shape=shape((2, T, D)),
        vmem=56,
    )


def partial_near(name, quarter, pairs, weights, cb, got, deps=()):
    block = 256
    T = pairs[0][0].shape[0] // 2
    D = weights[0].shape[1 - cb]
    per = T // block
    specs, reads = [], []
    for pair in pairs:
        s, read, steps = of_pieces(pair, block, order=(1, 0), rows=[(0, T)] * 2)
        specs += s
        reads.append(read)
    m = len(weights)

    def kernel(q_ref, *refs):
        got_ref, far_ref, own_ref = refs[3 * m :]
        total = got_ref[0].astype(f32)
        for j in range(m):
            total = total + dot(reads[j](refs[2 * j : 2 * j + 2]), refs[2 * m + j][...], 1, cb)
        i = pl.program_id(0)

        @pl.when(i < per)
        def _():
            far_ref[...] = total.astype(bf16)

        @pl.when(i >= per)
        def _():
            own_ref[...] = total.astype(bf16)

    return call(
        kernel, name, (*[p for g in pairs for p in g], *weights, got), deps, (quarter,), grid=(steps,),
        in_specs=specs
        + [quarter_columns(w) if cb else quarter_rows(w) for w in weights]
        + [pl.BlockSpec((1, block, D), lambda i, q: (1 - i // per, i % per, 0))],
        out_specs=[
            pl.BlockSpec((block, D), lambda i, q: (jnp.minimum(i, per - 1), 0)),
            pl.BlockSpec((block, D), lambda i, q: (jnp.maximum(i - per, 0), 0)),
        ],
        out_shape=[shape((T, D))] * 2,
        vmem=56,
    )


def rows_product(name, n_all, d_a, d_b, half, parts, got=None, deps=()):
    D, fq = n_all[0].shape[1], d_a.shape[1]
    T = n_all[0].shape[0]
    blocks, halves = parts
    block = D // (blocks * halves)
    extra = () if got is None else (got,)

    def kernel(s_ref, n0, n1, n2, n3, a_ref, b_ref, *rest):
        total = dot(n0[...], a_ref[:T], 0, 0) + dot(n1[...], a_ref[T:], 0, 0)
        total = total + dot(n2[...], b_ref[:T], 0, 0) + dot(n3[...], b_ref[T:], 0, 0)
        if extra:
            total = total + rest[0][0].astype(f32)
        rest[-1][0] = total.astype(bf16)

    cut = pl.BlockSpec((T, block), lambda i, s: (0, i * halves + s[0]))
    out = pl.BlockSpec((1, block, fq), lambda i, s: (i, 0, 0))
    return call(
        kernel, name, (*n_all, d_a, d_b, *extra), deps, (half,), grid=(blocks,),
        in_specs=[cut] * 4 + [whole(d_a), whole(d_b)] + [out] * len(extra),
        out_specs=out,
        out_shape=shape((blocks, block, fq)),
        vmem=56,
    )


def columns_product(name, h_a, h_b, c_all, half, halves, got=None, deps=()):
    D, fq = c_all[0].shape[1], h_a.shape[1]
    T = c_all[0].shape[0]
    block = 256
    steps = D // halves // block
    extra = () if got is None else (got,)

    def kernel(s_ref, c0, c1, c2, c3, a_ref, b_ref, *rest):
        total = dot(a_ref[:T], c0[...], 0, 0) + dot(a_ref[T:], c1[...], 0, 0)
        total = total + dot(b_ref[:T], c2[...], 0, 0) + dot(b_ref[T:], c3[...], 0, 0)
        if extra:
            total = total + rest[0][...].astype(f32)
        rest[-1][...] = total.astype(bf16)

    cut = pl.BlockSpec((T, block), lambda i, s: (0, s[0] * steps + i))
    out = pl.BlockSpec((fq, block), lambda i, s: (0, i))
    return call(
        kernel, name, (*c_all, h_a, h_b, *extra), deps, (half,), grid=(steps,),
        in_specs=[cut] * 4 + [whole(h_a), whole(h_b)] + [out] * len(extra),
        out_specs=out,
        out_shape=shape((fq, D // halves)),
        vmem=56,
    )


def token_products(name, rows, near, away, half, got=None, deps=(), passes=()):
    T, M = rows[0].shape
    N = near.shape[1] // 2
    block = 512
    extra = () if got is None else (got,)

    def kernel(s_ref, n0, n1, n2, n3, a_ref, b_ref, *rest):
        total = dot(n0[...], a_ref[:T], 0, 0) + dot(n1[...], a_ref[T:], 0, 0)
        total = total + dot(n2[...], b_ref[:T], 0, 0) + dot(n3[...], b_ref[T:], 0, 0)
        if extra:
            total = total + rest[0][...].astype(f32)
        rest[-1][...] = total.astype(bf16)

    cut = pl.BlockSpec((T, block), lambda i, s: (0, i))
    col = pl.BlockSpec((2 * T, N), lambda i, s: (0, s[0]), pipeline_mode=ONCE)
    out = pl.BlockSpec((block, N), lambda i, s: (i, 0))
    return call(
        kernel, name, (*rows, near, away, *extra), deps, (half,), grid=(M // block,),
        in_specs=[cut] * 4 + [col, col] + [out] * len(extra),
        out_specs=out,
        out_shape=shape((M, N)),
        passes=passes,
    )


def mid_back(own, got, mid, inverse, cot, gain, w_output, deps=()):
    T, D = mid.shape
    C = w_output.shape[0]
    block, rows = 512, 128

    def kernel(o_ref, g_ref, m_ref, i_ref, c_ref, gain_ref, w_ref, b_ref, n_ref, a_ref):
        @pl.when(pl.program_id(0) == 0)
        def _():
            for r in range(T // rows):
                sl = pl.ds(r * rows, rows)
                dn = o_ref[sl].astype(f32) + g_ref[sl].astype(f32)
                m, inv = m_ref[sl], i_ref[sl]
                mi = m * inv
                grad = jnp.sum(dn * mi, axis=0, keepdims=True)
                if r == 0:
                    n_ref[...] = grad
                else:
                    n_ref[...] += grad
                e = dn * gain_ref[...]
                mean = jnp.mean(e * mi, axis=1, keepdims=True)
                b_ref[sl] = (c_ref[sl].astype(f32) + inv * (e - mi * mean)).astype(bf16)

        a_ref[...] = dot(b_ref[...], w_ref[...], 1, 1, bf16)

    full = lambda w: pl.BlockSpec((T, w), lambda i: (0, 0))
    vec = pl.BlockSpec((1, D), lambda i: (0, 0))
    return call(
        kernel, "mid_back", (own, got, mid, inverse, cot, gain.reshape(1, D), w_output), deps, grid=(C // block,),
        in_specs=[whole(own), whole(got), whole(mid), full(1), whole(cot), vec, pl.BlockSpec((block, D), lambda i: (i, 0))],
        out_specs=[full(D), vec, pl.BlockSpec((T, block), lambda i: (0, i))],
        out_shape=[shape((T, D)), shape((1, D), f32), shape((T, C))],
        vmem=56,
    )


def tokens_back(d_query, d_kv, w_query, w_kv, d_branch, tokens, inverse, gain, deps=()):
    T, D = tokens.shape
    block, rows = 512, 128
    steps = D // block

    def kernel(q_ref, kv_ref, wq_ref, wkv_ref, b_ref, x_ref, i_ref, gain_ref, t_ref, n_ref, sum_ref):
        i = pl.program_id(0)
        at = pl.ds(i * block, block)
        inv = i_ref[...]
        dn = dot(q_ref[...], wq_ref[...], 1, 1) + dot(kv_ref[...], wkv_ref[...], 1, 1)
        xi = x_ref[...].astype(f32) * inv
        n_ref[...] = jnp.sum(dn * xi, axis=0, keepdims=True)
        e = dn * gain_ref[...]
        t_ref[:, at] = e
        part = jnp.sum(e * xi, axis=1, keepdims=True)

        @pl.when(i == 0)
        def _():
            sum_ref[...] = part

        @pl.when(i > 0)
        def _():
            sum_ref[...] += part

        @pl.when(i == steps - 1)
        def _():
            for r in range(T // rows):
                sl = pl.ds(r * rows, rows)
                iv = i_ref[sl]
                mean = sum_ref[sl] * (1.0 / D)
                t_ref[sl] = b_ref[sl].astype(f32) + iv * (t_ref[sl] - x_full[0][sl].astype(f32) * iv * mean)

    x_full = [None]

    def outer(q_ref, kv_ref, wq_ref, wkv_ref, b_ref, x_ref, xf_ref, i_ref, gain_ref, t_ref, n_ref, sum_ref):
        x_full[0] = xf_ref
        kernel(q_ref, kv_ref, wq_ref, wkv_ref, b_ref, x_ref, i_ref, gain_ref, t_ref, n_ref, sum_ref)

    full = lambda w: pl.BlockSpec((T, w), lambda i: (0, 0))
    vec = pl.BlockSpec((1, block), lambda i: (0, i))
    return call(
        outer, "tokens_back", (d_query, d_kv, w_query, w_kv, d_branch, tokens, tokens, inverse, gain.reshape(1, D)), deps, grid=(steps,),
        in_specs=[
            whole(d_query), whole(d_kv), pl.BlockSpec((block, w_query.shape[1]), lambda i: (i, 0)),
            pl.BlockSpec((block, w_kv.shape[1]), lambda i: (i, 0)), whole(d_branch),
            pl.BlockSpec((T, block), lambda i: (0, i)), whole(tokens), full(1), vec,
        ],
        out_specs=[full(D), vec],
        out_shape=[shape((T, D), f32), shape((1, D), f32)],
        scratch=[pltpu.VMEM((T, 1), f32)],
        vmem=56,
    )


def final_output(mid, own, got, deps=()):
    T, D = mid.shape
    block = 128

    def kernel(m_ref, a_ref, b_ref, o_ref):
        o_ref[...] = (m_ref[...] + a_ref[...].astype(f32) + b_ref[...].astype(f32)).astype(bf16)

    row = pl.BlockSpec((block, D), lambda i: (i, 0))
    return call(
        kernel, "output", (mid, own, got), deps, grid=(T // block,), in_specs=[row] * 3, out_specs=row,
        out_shape=shape((T, D)), vmem=56,
    )


def shards(
    tokens,
    segments,
    norm1_gain,
    w_query,
    w_key,
    w_value,
    w_output,
    norm2_gain,
    w_gate,
    w_up,
    w_down,
    cotangent,
):
    mv = Moves()
    nz, z, ny, nb = mv.nz, mv.z, mv.ny, mv.nb
    n_dev = nz * nb
    groups, L, D = tokens.shape
    hd = w_key.shape[1]
    FF = w_gate.shape[1]
    T = groups * L
    hops = (WINDOW + L - 1) // L
    hop = hops * L
    fq = FF // GROUP
    core, xb = mv.bit(1), mv.bit(2)
    quarter = mv.b % GROUP
    scalar = lambda v: v.astype(jnp.int32).reshape(1)
    qi, yi, xi = scalar(quarter), scalar(mv.y), scalar(xb)
    paired = ny == 2

    rows = tokens.reshape(T, D)
    cot = cotangent.reshape(T, D)
    others = [mv.shift(segments + 1, "z", range(nz), distance) for distance in range(1, nz)]
    cot1 = mv.flip(cot, 1)
    cot2 = mv.flip(cot, 2)
    every = jnp.concatenate([jnp.where(o == 0, big, o) for o in others] + [segments + 1], axis=1)
    starts = jnp.sum((every[:, None, :] <= segments[:, :, None]).astype(jnp.int32), axis=2)
    index = z * L + jnp.arange(L, dtype=jnp.int32)
    positions = (index[None, :] - starts).astype(f32).reshape(T, 1)
    starts_rel = (starts - z * L + hop).reshape(T, 1)
    half = hd // 2
    freq = jnp.exp(-math.log(rope_base) * jnp.arange(half, dtype=f32) / half)
    angle = positions * freq
    cos_half, sin_half = jnp.cos(angle), jnp.sin(angle)
    cosine = jnp.concatenate([cos_half, cos_half], axis=1)
    sine = jnp.concatenate([-sin_half, sin_half], axis=1)
    w_kv = jnp.concatenate([w_key, w_value], axis=1)

    normed, inv1, kv = norm_keys(rows, norm1_gain, w_kv, cosine, sine)
    kv = kv.reshape(groups, L, 2 * hd)
    earlier = [mv.shift(kv, "z", range(nz), distance) for distance in range(hops, 0, -1)]
    kv_all = jnp.concatenate(earlier + [kv], axis=1)
    keys, values = kv_all[:, :, :hd], kv_all[:, :, hd:]
    q_lin = project_query(normed, w_query, (kv,))
    attended, queries, lses = attention(q_lin, cosine, sine, starts_rel, keys, values, hop)
    mid, normed2, inv2, cot2 = project_out(attended, w_output, rows, norm2_gain, (cot1,), (cot2,))
    cot3 = mv.flip(cot2, 1)

    def of_group(v):
        far = mv.flip(v, GROUP)
        return v, mv.flip(v, 1), far, mv.flip(far, 1)

    normed_all, attended_all = (of_group(normed), of_group(attended)) if paired else ((), ())

    n1 = mv.flip(normed2, 1)
    n2 = mv.flip(normed2, 2)
    d_hidden = down_back(qi, (cot, cot1, cot2, cot3), w_down, (normed2,))
    h_a, dg_a, du_a, n2 = feed(qi, (normed2, n1), d_hidden, 0, w_gate, w_up, normed_all[1:], (n2,))
    n3 = mv.flip(n2, 1)
    h_b, dg_b, du_b = feed(qi, (n2, n3), d_hidden, 2 * T, w_gate, w_up, (du_a,))
    n_all, c_all = (normed2, n1, n2, n3), (cot, cot1, cot2, cot3)
    same_quarter = [[k * GROUP + q for k in range(nz * ny)] for q in range(GROUP)]

    def sum_all(grad):
        return lax.psum_scatter(grad, AXES, scatter_dimension=0, tiled=True, axis_index_groups=same_quarter)

    def send_rows(name, d_a, d_b, deps):
        if not paired:
            return rows_product(name, n_all, d_a, d_b, 0 * yi, (D // 256, 1), None, deps), None
        part = rows_product(name, n_all, d_a, d_b, 1 - yi, (nz, 2), None, deps)
        return part, mv.flip(part, GROUP)

    def keep_rows(name, sent, d_a, d_b, deps):
        if not paired:
            return sent[0], sum_all(sent[0].reshape(D, fq))[None]
        part = rows_product(name, n_all, d_a, d_b, yi, (nz, 2), sent[1], deps)
        return part, lax.psum_scatter(part, "seq", scatter_dimension=0, tiled=True)

    dn_pairs = [[dg_a, dg_b], [du_a, du_b]]
    gate_sent = send_rows("gate_send", dg_a, dg_b, (du_b,) + attended_all[1:])
    dn_away = partial_away("dn2_away", qi, dn_pairs, [w_gate, w_up], 1, (gate_sent[0],))
    dn_got = mv.flip(dn_away, 1)
    out_away = partial_away("out_away", qi, [[h_a, h_b]], [w_down], 0, (dn_away,))
    dn_far, dn_own = partial_near("dn2_near", qi, dn_pairs, [w_gate, w_up], 1, dn_got, (out_away,))
    dn_last = mv.flip(dn_far, 2)
    out_got = mv.flip(out_away, 1)
    up_sent = send_rows("up_send", du_a, du_b, (dn_far,))
    halves = 2 if paired else 1
    first_half = 1 - yi if paired else 0 * yi
    down_sent = columns_product("down_send", h_a, h_b, c_all, first_half, halves, None, (up_sent[0],))
    gate_kept, r_gate = keep_rows("gate_keep", gate_sent, dg_a, dg_b, (down_sent,))
    d_branch, norm2_term, d_attended = mid_back(
        dn_own, dn_last, mid, inv2, cot, norm2_gain, w_output, (gate_kept,)
    )
    out_far, out_own = partial_near("out_near", qi, [[h_a, h_b]], [w_down], 0, out_got, (d_attended,))
    out_last = mv.flip(out_far, 2)
    if paired:
        down_got = mv.flip(down_sent, GROUP)

    def to_quarters(d):
        cut = lambda v, i: lax.dynamic_slice_in_dim(v, i * (v.shape[1] // 2), v.shape[1] // 2, 1)
        chip = jnp.concatenate([cut(d, core), mv.flip(cut(d, 1 - core), 1)], axis=0)
        return cut(chip, mv.y), mv.flip(cut(chip, 1 - mv.y), GROUP)

    d_query, dk_all, dv_all = attention_back(
        queries, attended, d_attended, lses, cosine, sine, starts_rel, keys, values, hop, (out_far,)
    )
    dkv_all = jnp.concatenate([dk_all, dv_all], axis=2)
    backs = [
        mv.shift(dkv_all[:, (hops - k) * L : (hops - k + 1) * L].astype(bf16), "z", range(nz), -k)
        for k in range(1, hops + 1)
    ]
    if paired:
        db_near, db_away = to_quarters(d_branch)
        out_sent = token_products("w_out_send", attended_all, db_near, db_away, 1 - xi, None, (d_query,))
        out_recv = mv.flip(out_sent, 2)
        last = out_sent
    else:
        last = d_query
    up_kept, r_up = keep_rows("up_keep", up_sent, du_a, du_b, (last, r_gate))
    if paired:
        dq_near, dq_away = to_quarters(d_query)
        query_sent = token_products("w_query_send", normed_all, dq_near, dq_away, 1 - xi, None, (up_kept,))
        query_recv = mv.flip(query_sent, 2)
        g_out, *backs = token_products(
            "w_out_keep", attended_all, db_near, db_away, xi, out_recv, (query_sent,), backs
        )
        last = g_out
        r_out = lax.psum_scatter(g_out, "seq", scatter_dimension=0, tiled=True)
    own = dkv_all[:, hop:]
    for back in backs:
        own = own + back.astype(f32)
    own = own.reshape(T, 2 * hd)
    swapped = jnp.concatenate([own[:, half:hd], own[:, :half]], axis=1)
    d_key = (own[:, :hd] * cosine - swapped * sine).astype(bf16)
    d_kv = jnp.concatenate([d_key, own[:, hd:].astype(bf16)], axis=1)

    grad_tokens, norm1_term = tokens_back(
        d_query, d_kv, w_query, w_kv, d_branch, rows, inv1, norm1_gain, (last,)
    )
    output = final_output(mid, out_own, out_last, (norm1_term,))
    g_kv = dot(normed, d_kv, 0, 0, bf16)
    if paired:
        terms = jnp.concatenate([norm1_term, norm2_term, jnp.zeros((126, D), f32)], axis=0).T
        g_kv = jnp.concatenate([g_kv, terms.astype(bf16)], axis=1)
        width = g_kv.shape[1]
        g_kv = g_kv.reshape(nz, 2, 2, 2, D // n_dev, width)
        for axis, mask in ((3, 1), (2, 2), (1, GROUP)):
            bit = mv.bit(mask)
            away = mv.flip(lax.dynamic_index_in_dim(g_kv, 1 - bit, axis, keepdims=False), mask)
            kept = lax.dynamic_index_in_dim(g_kv, bit, axis, keepdims=False)
            g_kv = (kept.astype(f32) + away.astype(f32)).astype(bf16)
        r_kv = lax.psum_scatter(g_kv, "seq", scatter_dimension=0, tiled=True)[0].astype(f32)
        norms = r_kv[:, 2 * hd : 2 * hd + 2].T
    else:
        r_kv = lax.psum_scatter(g_kv, AXES, scatter_dimension=0, tiled=True).astype(f32)
        norms = jnp.concatenate([norm1_term, norm2_term], axis=0)
        norms = norms.reshape(2, n_dev, D // n_dev).transpose(1, 0, 2)
        norms = jnp.sum(lax.all_to_all(norms, AXES, 0, 0, tiled=True), axis=0)

    if paired:
        down_kept = columns_product("down_keep", h_a, h_b, c_all, yi, 2, down_got, (output, r_up))
        r_down = lax.psum_scatter(down_kept, "seq", scatter_dimension=0, tiled=True)
        g_query = token_products("w_query_keep", normed_all, dq_near, dq_away, xi, query_recv, (down_kept, r_out))

        def finish(r):
            r = lax.all_to_all(r.reshape(nb, D // n_dev, D // nb), "batch", 0, 0, tiled=True)
            order = [y_ * GROUP + x_ * 2 + c_ for c_ in range(2) for y_ in range(2) for x_ in range(2)]
            return jnp.concatenate([r[b_] for b_ in order], axis=1).astype(f32)

        r_query = lax.psum_scatter(g_query, "seq", scatter_dimension=0, tiled=True)
        grad_output, grad_query = finish(r_out), finish(r_query)
        r_down = r_down.reshape(2, fq // (2 * nz), D // 2)
        parts = []
        for k in range(2):
            pairs = [
                (z_ * nb + b_, (b_ % GROUP) * ny * nz + z_ * ny + (b_ // GROUP) ^ k)
                for z_ in range(nz)
                for b_ in range(nb)
            ]
            piece = lax.dynamic_index_in_dim(r_down, mv.y ^ k, 0, keepdims=False)
            parts.append(lax.ppermute(piece, AXES, pairs))
        first = jnp.where(core == 0, parts[0], parts[1])
        second = jnp.where(core == 0, parts[1], parts[0])
        grad_down = jnp.concatenate([first, second], axis=1).astype(f32)
    else:
        r_down = sum_all(down_sent)
        pairs = [
            (z_ * nb + b_, (b_ % GROUP) * ny * nz + z_ * ny + b_ // GROUP)
            for z_ in range(nz)
            for b_ in range(nb)
        ]
        grad_down = lax.ppermute(r_down, AXES, pairs).astype(f32)
        every_device = lambda g: lax.psum_scatter(g, AXES, scatter_dimension=0, tiled=True).astype(f32)
        grad_output = every_device(dot(attended, d_branch, 0, 0, bf16))
        grad_query = every_device(dot(normed, d_query, 0, 0, bf16))

    fours = [[k * GROUP + q for q in range(GROUP)] for k in range(ny)]

    def finish_quarter(r):
        k, height, width = r.shape
        r = r.reshape(k, GROUP, height // GROUP, width).transpose(1, 0, 2, 3)
        r = lax.all_to_all(r, "batch", 0, 0, tiled=True, axis_index_groups=fours)
        return r.transpose(1, 2, 0, 3).reshape(k, height // GROUP, FF).astype(f32)

    gu = finish_quarter(jnp.concatenate([r_gate, r_up], axis=0))
    return (
        output.reshape(groups, L, D),
        grad_tokens.reshape(groups, L, D),
        norms[0],
        grad_query,
        r_kv[:, :hd],
        r_kv[:, hd : 2 * hd],
        grad_output,
        norms[1],
        gu[0],
        gu[1],
        grad_down,
    )


def solution(mesh):
    data, vector, rows = P("batch", "seq", None), P(AXES), P(AXES, None)
    return jax.shard_map(
        shards,
        mesh=mesh,
        in_specs=(data, P("batch", "seq")) + (P(),) * 9 + (data,),
        out_specs=(data, data, vector, rows, rows, rows, rows, vector, rows, rows, rows),
        check_vma=False,
    )
```

time: 2480 us -> 697 us (0.28)
  waiting for transfers between devices: 1940 us -> 232 us
  matrix products: 374 us -> 2.34 us
  Pallas kernels: 0 us -> 345 us
  blocking collectives: 48.8 us -> 0 us
  starting transfers between devices: 21.2 us -> 58.2 us
    reduce_scatter x7 -> x6, waiting for transfers between devices: 1940 us -> 45.7 us  [the longest x1 38.5 us: shards(): r_down = lax.psum_scatter(down_kept, 'seq', scatter_dimension=0, tiled=True)]
    dot_general x27 -> x1, matrix products: 374 us -> 2.34 us  [dot(): lax.dot_general(a, b, (((ca,), (cb,)), ((), ())), preferred_element_type=...]
    pallas_call x0 -> x25, Pallas kernels: none -> 345 us  [call(): pl.pallas_call(body, grid_spec=pltpu.PrefetchScalarGridSpec(num_scalar_pr...]
    ppermute x8 -> x37, waiting for transfers between devices: 0.02 us -> 165 us  [the longest x28 108 us: flip(): return lax.ppermute(value, AXES, pairs)]
    unnamed x2 -> x0, blocking collectives: 48.8 us -> none
  transfers between devices with their start and end apart: 15 -> 46, of which waited for: 6 -> 20; matrix products, arithmetic and copies ran while one was open for 11% -> 5% of each run, Pallas kernels for 0% -> 45%
where the time goes in v1:
time: 697 us; the launch traced here: 693 us
  Pallas kernels  345 us (49%)
  waiting for transfers between devices  232 us (33%)
  starting transfers between devices  58.2 us (8%)
  local copies, waits for them, and re-layouts  24.2 us (3%)
  other arithmetic  15.9 us (2%)
  between operations  15.1 us (2%)
    pallas_call x25, Pallas kernels, call(): pl.pallas_call(body, grid_spec=pltpu.PrefetchScalarGridSpec(num_scalar_pr...  345 us
    ppermute x28, waiting for transfers between devices, flip(): return lax.ppermute(value, AXES, pairs)  108 us
    reduce_scatter x1, waiting for transfers between devices, shards(): r_down = lax.psum_scatter(down_kept, 'seq', scatter_dimension=0, tiled=True)  38.5 us
    ppermute x2, waiting for transfers between devices, shards(): parts.append(lax.ppermute(piece, AXES, pairs))  30.9 us
    ppermute x7, waiting for transfers between devices, shift(): return lax.ppermute(value, AXES, pairs)  26.7 us
    ppermute x28, starting transfers between devices, flip(): return lax.ppermute(value, AXES, pairs)  20.6 us
    all_to_all x1, waiting for transfers between devices, finish_quarter(): r = lax.all_to_all(r, 'batch', 0, 0, tiled=True, axis_index_groups=fours)  17 us
    ppermute x7, starting transfers between devices, shift(): return lax.ppermute(value, AXES, pairs)  14.4 us
  transfers between devices with their start and end apart: 46, of which 20 were waited for; matrix products, arithmetic and copies ran while one was open for 5% of the time, Pallas kernels for 45%

profile of v1, /device:TPU:5, one launch (start us, length us, event | category | flops | bytes accessed | tf_op | source)
XLA Modules:
  0.0 692.7 jit_solution(14136006593051344352)
XLA Ops:
  7.9 5.2 collective-permute-start.2
  24.7 4.9 norm_keys.1
  33.1 9.1 %query.1.refs_0_ = f32[512,2048]{1,0:T(8,128)} custom-call(bf16[512,2048]{1,0:T(8,128)(2,1)} %get-tuple-element.43.refs_0_.refs_1_, bf16[2048,2048]{1,0:T(8,128)(2,1)} %refs_2_.1, bf16[2,256,256]{2,1,0:T(8,128)(2,1)} %bitcast.142), custom_call_target="tpu_custom_call" | custom-call | flops 8999999488 | bytes 1 | tf_op jit(solution)/shard_map/query/pallas_call | solution.py:43
  44.2 30.5 %attend.1 = (bf16[512,2048]{1,0:T(8,128)(2,1)}, bf16[512,2048]{1,0:T(8,128)(2,1)}, f32[2,4,256,4]{3,2,1,0:T(8,128)}) custom-call(f32[512,2048]{1,0:T(8,128)} %query.1.refs_0_, f32[512,128]{1,0:T(8,128)} %get-tuple-element.104.refs_3_.refs_1_.refs_4_, f32[512,128]{1,0:T(8,128)} %get-tuple-element.105.refs_4_.refs_2_.refs_5_, s32[512,1]{1,0:T(8,128)} %bitcast.137, ...), custom_call_target="tpu_custom_call" | custom-call | flops 30000001024 | bytes 1 | tf_op jit(solution)/shard_map/attend/pallas_call | solution.py:43
  76.0 11.4 %project_out.1 = (f32[512,2048]{1,0:T(8,128)}, bf16[512,2048]{1,0:T(8,128)(2,1)}, f32[512,1]{1,0:T(8,128)}, bf16[512,2048]{1,0:T(8,128)(2,1)}) custom-call(bf16[512,2048]{1,0:T(8,128)(2,1)} %get-tuple-element.45.refs_0_.refs_1_, bf16[2048,2048]{1,0:T(8,128)(2,1)} %refs_6_.5, bf16[512,2048]{1,0:T(8,128)(2,1)} %bitcast.147, ...), custom_call_target="tpu_custom_call", output_to_operand_aliasing={{3}: (5, {})} | custom-call | flops 11000000512 | bytes 1 | tf_op jit(solution)/shard_map/project_out/pallas_call | solution.py:43
  89.9 5.3 collective-permute-done.8.refs_4_
  96.5 20.1 %down_back.1.refs_3_ = bf16[2048,1408]{1,0:T(8,128)(2,1)} custom-call(s32[1]{0:T(128)} %bitcast.5.refs_0_, bf16[512,2048]{1,0:T(8,128)(2,1)} %bitcast.152, bf16[512,2048]{1,0:T(8,128)(2,1)} %copy-done.15, bf16[512,2048]{1,0:T(8,128)(2,1)} %get-tuple-element.48.refs_3_, bf16[512,2048]{1,0:T(8,128)(2,1)} %collective-permute-done.8.refs_4_, ...), custom_call_target="tpu_custom_call" | custom-call | flops 20000000000 | bytes 1 | tf_op jit(solution)/shard_map/down_back/pallas_call | solution.py:43
  116.6 19.8 %collective-permute-done.12.refs_9_ = bf16[512,2048]{1,0:T(8,128)(2,1)} collective-permute-done((bf16[512,2048]{1,0:T(8,128)(2,1)}, bf16[512,2048]{1,0:T(8,128)(2,1)}, u32[]{:S(2)}, u32[]{:S(2)}) %collective-permute-start.12) | collective-permute-done | bytes 2097184 | tf_op jit(solution)/shard_map/ppermute | solution.py:75
  136.4 21.2 %feed.2 = (bf16[1024,1408]{1,0:T(8,128)(2,1)}, bf16[1024,1408]{1,0:T(8,128)(2,1)}, bf16[1024,1408]{1,0:T(8,128)(2,1)}, bf16[512,2048]{1,0:T(8,128)(2,1)}) custom-call(s32[1]{0:T(128)} %bitcast.5.refs_0_, bf16[512,2048]{1,0:T(8,128)(2,1)} %get-tuple-element.47.refs_6_.refs_1_, ...), custom_call_target="tpu_custom_call", output_to_operand_aliasing={{3}: (9, {})} | custom-call | flops 20999999488 | bytes 1 | tf_op jit(solution)/shard_map/feed/pallas_call | solution.py:43
  158.9 6.0 collective-permute-done.13.refs_2_.refs_4_
  164.8 21.6 %feed.3 = (bf16[1024,1408]{1,0:T(8,128)(2,1)}, bf16[1024,1408]{1,0:T(8,128)(2,1)}, bf16[1024,1408]{1,0:T(8,128)(2,1)}) custom-call(s32[1]{0:T(128)} %bitcast.5.refs_0_, bf16[512,2048]{1,0:T(8,128)(2,1)} %get-tuple-element.50.refs_1_.refs_3_, bf16[512,2048]{1,0:T(8,128)(2,1)} %collective-permute-done.13.refs_2_.refs_4_, bf16[2048,1408]{1,0:T(8,128)(2,1)} %down_back.1.refs_3_, ...), custom_call_target="tpu_custom_call" | custom-call | flops 20999999488 | bytes 1 | tf_op jit(solution)/shard_map/feed/pallas_call | solution.py:43
  187.8 11.5 %gate_send.1.refs_7_ = bf16[4,256,1408]{2,1,0:T(8,128)(2,1)} custom-call(s32[1]{0:T(128)S(6)} %sub.70.refs_0_, bf16[512,2048]{1,0:T(8,128)(2,1)} %get-tuple-element.47.refs_6_.refs_1_, bf16[512,2048]{1,0:T(8,128)(2,1)} %collective-permute-done.7.refs_2_, bf16[512,2048]{1,0:T(8,128)(2,1)} %get-tuple-element.50.refs_1_.refs_3_, ...), custom_call_target="tpu_custom_call" | custom-call | flops 11000000512 | bytes 1 | tf_op jit(solution)/shard_map/gate_send/pallas_call | solution.py:43
  199.3 20.3 %dn2_away.1.refs_4_ = bf16[2,512,2048]{2,1,0:T(8,128)(2,1)} custom-call(s32[1]{0:T(128)} %bitcast.5.refs_0_, bf16[1024,1408]{1,0:T(8,128)(2,1)} %get-tuple-element.53.refs_5_.refs_1_, bf16[1024,1408]{1,0:T(8,128)(2,1)} %get-tuple-element.54.refs_6_.refs_2_, bf16[1024,1408]{1,0:T(8,128)(2,1)} %get-tuple-element.51.refs_6_.refs_3_.refs_5_, ...), custom_call_target="tpu_custom_call" | custom-call | flops 20000000000 | bytes 1 | tf_op jit(solution)/shard_map/dn2_away/pallas_call | solution.py:43
  221.3 11.5 %out_away.1.refs_8_ = bf16[2,512,2048]{2,1,0:T(8,128)(2,1)} custom-call(s32[1]{0:T(128)} %bitcast.5.refs_0_, bf16[1024,1408]{1,0:T(8,128)(2,1)} %get-tuple-element.49.refs_1_.refs_5_, bf16[1024,1408]{1,0:T(8,128)(2,1)} %get-tuple-element.52.refs_2_.refs_6_, bf16[5632,2048]{1,0:T(8,128)(2,1)} %refs_3_.3, bf16[2,512,2048]{2,1,0:T(8,128)(2,1)} %dn2_away.1.refs_4_), custom_call_target="tpu_custom_call" | custom-call | flops 11000000512 | bytes 1 | tf_op jit(solution)/shard_map/out_away/pallas_call | solution.py:43
  233.2 21.8 %dn2_near.1 = (bf16[512,2048]{1,0:T(8,128)(2,1)}, bf16[512,2048]{1,0:T(8,128)(2,1)}) custom-call(s32[1]{0:T(128)} %bitcast.5.refs_0_, bf16[1024,1408]{1,0:T(8,128)(2,1)} %get-tuple-element.53.refs_5_.refs_1_, bf16[1024,1408]{1,0:T(8,128)(2,1)} %get-tuple-element.54.refs_6_.refs_2_, bf16[1024,1408]{1,0:T(8,128)(2,1)} %get-tuple-element.51.refs_6_.refs_3_.refs_5_, ...), custom_call_target="tpu_custom_call" | custom-call | flops 22000001024 | bytes 1 | tf_op jit(solution)/shard_map/dn2_near/pallas_call | solution.py:43
  255.7 11.5 %up_send.1.refs_7_ = bf16[4,256,1408]{2,1,0:T(8,128)(2,1)} custom-call(s32[1]{0:T(128)S(6)} %sub.70.refs_0_, bf16[512,2048]{1,0:T(8,128)(2,1)} %get-tuple-element.47.refs_6_.refs_1_, bf16[512,2048]{1,0:T(8,128)(2,1)} %collective-permute-done.7.refs_2_, bf16[512,2048]{1,0:T(8,128)(2,1)} %get-tuple-element.50.refs_1_.refs_3_, ...), custom_call_target="tpu_custom_call" | custom-call | flops 11000000512 | bytes 1 | tf_op jit(solution)/shard_map/up_send/pallas_call | solution.py:43
  267.4 11.0 %down_send.1.refs_8_ = bf16[1408,1024]{1,0:T(8,128)(2,1)} custom-call(s32[1]{0:T(128)S(6)} %sub.70.refs_0_, bf16[512,2048]{1,0:T(8,128)(2,1)} %bitcast.153, bf16[512,2048]{1,0:T(8,128)(2,1)} %copy-done.15, bf16[512,2048]{1,0:T(8,128)(2,1)} %get-tuple-element.48.refs_3_, bf16[512,2048]{1,0:T(8,128)(2,1)} %collective-permute-done.8.refs_4_, ...), custom_call_target="tpu_custom_call" | custom-call | flops 11000000512 | bytes 1 | tf_op jit(solution)/shard_map/down_send/pallas_call | solution.py:43
  278.5 5.7 collective-permute-done.20.refs_7_
  285.7 11.8 %gate_keep.1.refs_7_ = bf16[4,256,1408]{2,1,0:T(8,128)(2,1)} custom-call(s32[1]{0:T(128)} %bitcast.6.refs_0_, bf16[512,2048]{1,0:T(8,128)(2,1)} %get-tuple-element.47.refs_6_.refs_1_, bf16[512,2048]{1,0:T(8,128)(2,1)} %collective-permute-done.7.refs_2_, bf16[512,2048]{1,0:T(8,128)(2,1)} %get-tuple-element.50.refs_1_.refs_3_, ...), custom_call_target="tpu_custom_call" | custom-call | flops 12000000000 | bytes 1 | tf_op jit(solution)/shard_map/gate_keep/pallas_call | solution.py:43
  297.6 4.7 collective-permute-done.19.refs_1_
  302.3 14.6 %mid_back.1 = (bf16[512,2048]{1,0:T(8,128)(2,1)}, f32[1,2048]{1,0:T(1,128)}, bf16[512,2048]{1,0:T(8,128)(2,1)}) custom-call(bf16[512,2048]{1,0:T(8,128)(2,1)} %get-tuple-element.56.refs_0_, bf16[512,2048]{1,0:T(8,128)(2,1)} %collective-permute-done.19.refs_1_, f32[512,2048]{1,0:T(8,128)} %get-tuple-element.46.refs_2_.refs_0_, ...), custom_call_target="tpu_custom_call" | custom-call | flops 14000000000 | bytes 1 | tf_op jit(solution)/shard_map/mid_back/pallas_call | solution.py:43
  319.6 12.9 %out_near.1 = (bf16[512,2048]{1,0:T(8,128)(2,1)}, bf16[512,2048]{1,0:T(8,128)(2,1)}) custom-call(s32[1]{0:T(128)} %bitcast.5.refs_0_, bf16[1024,1408]{1,0:T(8,128)(2,1)} %get-tuple-element.49.refs_1_.refs_5_, bf16[1024,1408]{1,0:T(8,128)(2,1)} %get-tuple-element.52.refs_2_.refs_6_, bf16[5632,2048]{1,0:T(8,128)(2,1)} %refs_3_.3, ...), custom_call_target="tpu_custom_call" | custom-call | flops 12999999488 | bytes 1 | tf_op jit(solution)/shard_map/out_near/pallas_call | solution.py:43
  332.6 28.8 %attend_back.1 = (bf16[512,2048]{1,0:T(8,128)(2,1)}, f32[2,768,128]{2,1,0:T(8,128)}, f32[2,768,128]{2,1,0:T(8,128)}) custom-call(bf16[512,2048]{1,0:T(8,128)(2,1)} %get-tuple-element.62.refs_0_, bf16[512,2048]{1,0:T(8,128)(2,1)} %get-tuple-element.45.refs_0_.refs_1_, bf16[512,2048]{1,0:T(8,128)(2,1)} %get-tuple-element.59.refs_5_.refs_2_, ...), custom_call_target="tpu_custom_call" | custom-call | flops 28999999488 | bytes 1 | tf_op jit(solution)/shard_map/attend_back/pallas_call | solution.py:43
  367.4 21.9 %collective-permute-done.23.refs_6_ = bf16[1024,512]{1,0:T(8,128)(2,1)} collective-permute-done((bf16[1024,512]{1,0:T(8,128)(2,1)}, bf16[1024,512]{1,0:T(8,128)(2,1)}, u32[]{:S(2)}, u32[]{:S(2)}) %collective-permute-start.23) | collective-permute-done | bytes 1048608 | tf_op jit(solution)/shard_map/ppermute | solution.py:75
  389.3 6.8 w_out_send.1.refs_8_
  396.2 12.0 %up_keep.1.refs_7_ = bf16[4,256,1408]{2,1,0:T(8,128)(2,1)} custom-call(s32[1]{0:T(128)} %bitcast.6.refs_0_, bf16[512,2048]{1,0:T(8,128)(2,1)} %get-tuple-element.47.refs_6_.refs_1_, bf16[512,2048]{1,0:T(8,128)(2,1)} %collective-permute-done.7.refs_2_, bf16[512,2048]{1,0:T(8,128)(2,1)} %get-tuple-element.50.refs_1_.refs_3_, ...), custom_call_target="tpu_custom_call" | custom-call | flops 12000000000 | bytes 1 | tf_op jit(solution)/shard_map/up_keep/pallas_call | solution.py:43
  413.1 6.8 w_query_send.1.refs_8_
  422.4 24.2 %collective-permute-done.29.refs_10_ = bf16[2,256,256]{2,1,0:T(8,128)(2,1)S(1)} collective-permute-done((bf16[2,256,256]{2,1,0:T(8,128)(2,1)S(1)}, bf16[2,256,256]{2,1,0:T(8,128)(2,1)S(1)}, u32[]{:S(2)}, u32[]{:S(2)}) %collective-permute-start.29) | collective-permute-done | bytes 262176 | tf_op jit(solution)/shard_map/ppermute | solution.py:87
  446.6 29.3 %collective-permute-done.24.refs_7_ = bf16[2048,256]{1,0:T(8,128)(2,1)S(1)} collective-permute-done((bf16[2048,256]{1,0:T(8,128)(2,1)}, bf16[2048,256]{1,0:T(8,128)(2,1)S(1)}, u32[]{:S(2)}, u32[]{:S(2)}) %collective-permute-start.24) | collective-permute-done | bytes 1048608 | tf_op jit(solution)/shard_map/ppermute | solution.py:75
  476.9 7.2 %w_out_keep.1 = (bf16[2048,256]{1,0:T(8,128)(2,1)}, bf16[2,256,256]{2,1,0:T(8,128)(2,1)}, bf16[2,256,256]{2,1,0:T(8,128)(2,1)}) custom-call(s32[1]{0:T(128)} %bitcast.7.refs_0_, bf16[512,2048]{1,0:T(8,128)(2,1)} %get-tuple-element.45.refs_0_.refs_1_, bf16[512,2048]{1,0:T(8,128)(2,1)} %copy-done.17, ...), custom_call_target="tpu_custom_call", output_to_operand_aliasing={{1}: (9, {}), {2}: (10, {})} | custom-call | flops 7000000000 | bytes 1 | tf_op jit(solution)/shard_map/w_out_keep/pallas_call | solution.py:43
  486.4 13.6 %tokens_back.1 = (f32[512,2048]{1,0:T(8,128)}, f32[1,2048]{1,0:T(1,128)}) custom-call(bf16[512,2048]{1,0:T(8,128)(2,1)} %get-tuple-element.64.refs_7_.refs_0_, bf16[512,256]{1,0:T(8,128)(2,1)} %pad_maximum_fusion.5.refs_1_, bf16[2048,2048]{1,0:T(8,128)(2,1)} %refs_2_.1, bf16[2048,256]{1,0:T(8,128)(2,1)} %copy-done.7, ...), custom_call_target="tpu_custom_call" | custom-call | flops 14000000000 | bytes 1 | tf_op jit(solution)/shard_map/tokens_back/pallas_call | solution.py:43
  504.3 3.4 collective-permute-start.30
  511.4 8.9 %collective-permute-done.31 = bf16[4,2,64,384]{3,2,1,0:T(8,128)(2,1)S(1)} collective-permute-done((bf16[4,2,64,384]{3,2,1,0:T(8,128)(2,1)S(1)}, bf16[4,2,64,384]{3,2,1,0:T(8,128)(2,1)S(1)}, u32[]{:S(2)}, u32[]{:S(2)}) %collective-permute-start.31) | collective-permute-done | bytes 393248 | tf_op jit(solution)/shard_map/ppermute | solution.py:75
  521.7 5.3 output.1.refs_8_
  527.8 11.6 %down_keep.1.refs_8_ = bf16[1408,1024]{1,0:T(8,128)(2,1)} custom-call(s32[1]{0:T(128)} %bitcast.6.refs_0_, bf16[512,2048]{1,0:T(8,128)(2,1)} %bitcast.155, bf16[512,2048]{1,0:T(8,128)(2,1)} %copy-done.15, bf16[512,2048]{1,0:T(8,128)(2,1)} %get-tuple-element.48.refs_3_, bf16[512,2048]{1,0:T(8,128)(2,1)} %collective-permute-done.8.refs_4_, ...), custom_call_target="tpu_custom_call" | custom-call | flops 12000000000 | bytes 1 | tf_op jit(solution)/shard_map/down_keep/pallas_call | solution.py:43
  539.4 3.3 collective-permute-done.33.refs_7_
  543.7 7.2 %w_query_keep.1 = bf16[2048,256]{1,0:T(8,128)(2,1)} custom-call(s32[1]{0:T(128)} %bitcast.7.refs_0_, bf16[512,2048]{1,0:T(8,128)(2,1)} %get-tuple-element.43.refs_0_.refs_1_, bf16[512,2048]{1,0:T(8,128)(2,1)} %copy-done.16, bf16[512,2048]{1,0:T(8,128)(2,1)} %collective-permute-done.10.refs_7_.refs_3_, ...), custom_call_target="tpu_custom_call" | custom-call | flops 7000000000 | bytes 1 | tf_op jit(solution)/shard_map/w_query_keep/pallas_call | solution.py:43
  551.6 7.2 %reduce-scatter.9.cloned.1.call-done = bf16[1,64,384]{2,1,0:T(8,128)(2,1)} async-done(((bf16[4,64,384]{2,1,0:T(8,128)(2,1)}), bf16[1,64,384]{2,1,0:T(8,128)(2,1)}) %reduce-scatter.9.cloned.1.call-update) | async-done | bytes 49168 | tf_op jit(solution)/shard_map/reduce_scatter | solution.py:803
  559.6 6.7 all-to-all-start.1
  567.6 3.2 all-to-all-done.1
  572.2 5.6 all-to-all-start.2
  578.7 17.0 %all-to-all-done.2 = bf16[4,2,64,1408]{3,2,1,0:T(8,128)(2,1)} async-done(((bf16[4,2,64,1408]{3,2,1,0:T(8,128)(2,1)}), bf16[4,2,64,1408]{3,2,1,0:T(8,128)(2,1)}, u32[]{:S(2)}, u32[]{:S(2)}) %all-to-all-start.2) | async-done | bytes 1441824 | tf_op jit(solution)/shard_map/all_to_all | solution.py:853
  597.7 5.3 all-to-all-start
  607.5 38.5 %reduce-scatter.17.cloned.1.call-done = bf16[352,1024]{1,0:T(8,128)(2,1)} async-done(((bf16[1408,1024]{1,0:T(8,128)(2,1)}), bf16[352,1024]{1,0:T(8,128)(2,1)}) %reduce-scatter.17.cloned.1.call-update) | async-done | bytes 720912 | tf_op jit(solution)/shard_map/reduce_scatter | solution.py:813
  647.2 2.7 collective-permute-start.35
  649.8 2.7 collective-permute-start.36
  653.3 23.1 %collective-permute-done.35 = bf16[176,1024]{1,0:T(8,128)(2,1)S(1)} collective-permute-done((bf16[176,1024]{1,0:T(8,128)(2,1)S(1)}, bf16[176,1024]{1,0:T(8,128)(2,1)S(1)}, u32[]{:S(2)}, u32[]{:S(2)}) %collective-permute-start.35) | collective-permute-done | bytes 360480 | tf_op jit(solution)/shard_map/ppermute | solution.py:832
  676.5 7.8 %collective-permute-done.36 = bf16[176,1024]{1,0:T(8,128)(2,1)S(1)} collective-permute-done((bf16[176,1024]{1,0:T(8,128)(2,1)S(1)}, bf16[176,1024]{1,0:T(8,128)(2,1)S(1)}, u32[]{:S(2)}, u32[]{:S(2)}) %collective-permute-start.36) | collective-permute-done | bytes 360480 | tf_op jit(solution)/shard_map/ppermute | solution.py:832
  (193 shorter events, 75.2 us)
Async XLA Ops:
  7.2 389.0 %reduce-scatter.7.cloned.1.call-start = ((), (), s32[]{:S(2)}) async-start(), calls=%async_computation.9 | async-start | bytes 3604480 | tf_op jit(solution)/shard_map/reduce_scatter | solution.py:727
  7.9 13.6 %collective-permute-start.2 = (s32[2,256]{1,0:T(2,128)S(1)}, s32[2,256]{1,0:T(2,128)S(1)}, u32[]{:S(2)}, u32[]{:S(2)}) collective-permute-start(s32[2,256]{1,0:T(2,128)S(1)} %broadcast_add_fusion), channel_id=1, source_target_pairs={{0,24},{1,25},{2,26},{3,27},{4,28},{5,29},{6,30},{7,31}} | collective-permute-start | bytes 6152 | tf_op jit(solution)/shard_map/ppermute | solution.py:87
  13.2 8.4 %collective-permute-start.1 = (s32[2,256]{1,0:T(2,128)S(1)}, s32[2,256]{1,0:T(2,128)S(1)}, u32[]{:S(2)}, u32[]{:S(2)}) collective-permute-start(s32[2,256]{1,0:T(2,128)S(1)} %broadcast_add_fusion), channel_id=1, source_target_pairs={{0,16},{1,17},{2,18},{3,19},{4,20},{5,21},{6,22},{7,23},{8,24},{9,... | collective-permute-start | bytes 6152 | tf_op jit(solution)/shard_map/ppermute | solution.py:87
  14.5 7.1 %collective-permute-start = (s32[2,256]{1,0:T(2,128)S(1)}, s32[2,256]{1,0:T(2,128)S(1)}, u32[]{:S(2)}, u32[]{:S(2)}) collective-permute-start(s32[2,256]{1,0:T(2,128)S(1)} %broadcast_add_fusion), channel_id=1, source_target_pairs={{0,8},{1,9},{2,10},{3,11},{4,12},{5,13},{6,14},{7,15},{8,16},{9,17... | collective-permute-start | bytes 6152 | tf_op jit(solution)/shard_map/ppermute | solution.py:87
  16.7 58.1 %collective-permute-start.5 = (bf16[512,2048]{1,0:T(8,128)(2,1)}, bf16[512,2048]{1,0:T(8,128)(2,1)S(1)}, u32[]{:S(2)}, u32[]{:S(2)}) collective-permute-start(bf16[512,2048]{1,0:T(8,128)(2,1)} %bitcast.150), channel_id=1, source_target_pairs={{0,1},{1,0},{2,3},{3,2},{4,5},{5,4},{6,7},{7,6},{8,9},{9,8},{10,11... | collective-permute-start | bytes 6291464 | tf_op jit(solution)/shard_map/ppermute | solution.py:75
  18.0 56.8 %collective-permute-start.6 = (bf16[512,2048]{1,0:T(8,128)(2,1)}, bf16[512,2048]{1,0:T(8,128)(2,1)}, u32[]{:S(2)}, u32[]{:S(2)}) collective-permute-start(bf16[512,2048]{1,0:T(8,128)(2,1)} %bitcast.151), channel_id=1, source_target_pairs={{0,2},{1,3},{2,0},{3,1},{4,6},{5,7},{6,4},{7,5},{8,10},{9,11},{10,... | collective-permute-start | bytes 6291464 | tf_op jit(solution)/shard_map/ppermute | solution.py:75
  29.6 13.4 %collective-permute-start.4 = (bf16[2,256,256]{2,1,0:T(8,128)(2,1)}, bf16[2,256,256]{2,1,0:T(8,128)(2,1)S(1)}, u32[]{:S(2)}, u32[]{:S(2)}) collective-permute-start(bf16[2,256,256]{2,1,0:T(8,128)(2,1)} %bitcast.140), channel_id=1, source_target_pairs={{0,8},{1,9},{2,10},{3,11},{4,12},{5,13},{6,14},{7,15},{8,16},{9,17... | collective-permute-start | bytes 786440 | tf_op jit(solution)/shard_map/ppermute | solution.py:87
  31.3 11.8 %collective-permute-start.3 = (bf16[2,256,256]{2,1,0:T(8,128)(2,1)}, bf16[2,256,256]{2,1,0:T(8,128)(2,1)S(1)}, u32[]{:S(2)}, u32[]{:S(2)}) collective-permute-start(bf16[2,256,256]{2,1,0:T(8,128)(2,1)} %bitcast.141), channel_id=1, source_target_pairs={{0,16},{1,17},{2,18},{3,19},{4,20},{5,21},{6,22},{7,23},{8,24},{9,... | collective-permute-start | bytes 786440 | tf_op jit(solution)/shard_map/ppermute | solution.py:87
  32.8 56.8 %collective-permute-start.10 = (bf16[512,2048]{1,0:T(8,128)(2,1)}, bf16[512,2048]{1,0:T(8,128)(2,1)}, u32[]{:S(2)}, u32[]{:S(2)}) collective-permute-start(bf16[512,2048]{1,0:T(8,128)(2,1)} %get-tuple-element.43.refs_0_.refs_1_), channel_id=1, source_target_pairs={{0,4},{1,5},{2,6},{3,7},{4,0},{5,1},{6,2},{7,3},{8,12},{9,13},{10,... | collective-permute-start | bytes 6291464 | tf_op jit(solution)/shard_map/ppermute | solution.py:75
  87.4 7.7 %collective-permute-start.8 = (bf16[512,2048]{1,0:T(8,128)(2,1)}, bf16[512,2048]{1,0:T(8,128)(2,1)}, u32[]{:S(2)}, u32[]{:S(2)}) collective-permute-start(bf16[512,2048]{1,0:T(8,128)(2,1)} %get-tuple-element.48.refs_3_), channel_id=1, source_target_pairs={{0,1},{1,0},{2,3},{3,2},{4,5},{5,4},{6,7},{7,6},{8,9},{9,8},{10,11... | collective-permute-start | bytes 6291464 | tf_op jit(solution)/shard_map/ppermute | solution.py:75
  88.3 28.3 %collective-permute-start.9 = (bf16[512,2048]{1,0:T(8,128)(2,1)}, bf16[512,2048]{1,0:T(8,128)(2,1)S(1)}, u32[]{:S(2)}, u32[]{:S(2)}) collective-permute-start(bf16[512,2048]{1,0:T(8,128)(2,1)} %get-tuple-element.43.refs_0_.refs_1_), channel_id=1, source_target_pairs={{0,1},{1,0},{2,3},{3,2},{4,5},{5,4},{6,7},{7,6},{8,9},{9,8},{10,11... | collective-permute-start | bytes 6291464 | tf_op jit(solution)/shard_map/ppermute | solution.py:75
  88.3 28.3 %collective-permute-start.7 = (bf16[512,2048]{1,0:T(8,128)(2,1)}, bf16[512,2048]{1,0:T(8,128)(2,1)}, u32[]{:S(2)}, u32[]{:S(2)}) collective-permute-start(bf16[512,2048]{1,0:T(8,128)(2,1)} %get-tuple-element.47.refs_6_.refs_1_), channel_id=1, source_target_pairs={{0,1},{1,0},{2,3},{3,2},{4,5},{5,4},{6,7},{7,6},{8,9},{9,8},{10,11... | collective-permute-start | bytes 6291464 | tf_op jit(solution)/shard_map/ppermute | solution.py:75
  88.8 47.6 %collective-permute-start.12 = (bf16[512,2048]{1,0:T(8,128)(2,1)}, bf16[512,2048]{1,0:T(8,128)(2,1)}, u32[]{:S(2)}, u32[]{:S(2)}) collective-permute-start(bf16[512,2048]{1,0:T(8,128)(2,1)} %get-tuple-element.47.refs_6_.refs_1_), channel_id=1, source_target_pairs={{0,2},{1,3},{2,0},{3,1},{4,6},{5,7},{6,4},{7,5},{8,10},{9,11},{10,... | collective-permute-start | bytes 6291464 | tf_op jit(solution)/shard_map/ppermute | solution.py:75
  89.6 46.7 %collective-permute-start.11 = (bf16[512,2048]{1,0:T(8,128)(2,1)}, bf16[512,2048]{1,0:T(8,128)(2,1)}, u32[]{:S(2)}, u32[]{:S(2)}) collective-permute-start(bf16[512,2048]{1,0:T(8,128)(2,1)} %collective-permute-done.10.refs_7_.refs_3_), channel_id=1, source_target_pairs={{0,1},{1,0},{2,3},{3,2},{4,5},{5,4},{6,7},{7,6},{8,9},{9,8},{10,11... | collective-permute-start | bytes 6291464 | tf_op jit(solution)/shard_map/ppermute | solution.py:75
  95.2 63.2 %collective-permute-start.15 = (bf16[512,2048]{1,0:T(8,128)(2,1)}, bf16[512,2048]{1,0:T(8,128)(2,1)}, u32[]{:S(2)}, u32[]{:S(2)}) collective-permute-start(bf16[512,2048]{1,0:T(8,128)(2,1)} %get-tuple-element.45.refs_0_.refs_1_), channel_id=1, source_target_pairs={{0,4},{1,5},{2,6},{3,7},{4,0},{5,1},{6,2},{7,3},{8,12},{9,13},{10,... | collective-permute-start | bytes 6291464 | tf_op jit(solution)/shard_map/ppermute | solution.py:75
  157.6 7.3 %collective-permute-start.13 = (bf16[512,2048]{1,0:T(8,128)(2,1)}, bf16[512,2048]{1,0:T(8,128)(2,1)}, u32[]{:S(2)}, u32[]{:S(2)}) collective-permute-start(bf16[512,2048]{1,0:T(8,128)(2,1)} %get-tuple-element.50.refs_1_.refs_3_), channel_id=1, source_target_pairs={{0,1},{1,0},{2,3},{3,2},{4,5},{5,4},{6,7},{7,6},{8,9},{9,8},{10,11... | collective-permute-start | bytes 6291464 | tf_op jit(solution)/shard_map/ppermute | solution.py:75
  158.4 28.1 %collective-permute-start.14 = (bf16[512,2048]{1,0:T(8,128)(2,1)}, bf16[512,2048]{1,0:T(8,128)(2,1)S(1)}, u32[]{:S(2)}, u32[]{:S(2)}) collective-permute-start(bf16[512,2048]{1,0:T(8,128)(2,1)} %get-tuple-element.45.refs_0_.refs_1_), channel_id=1, source_target_pairs={{0,1},{1,0},{2,3},{3,2},{4,5},{5,4},{6,7},{7,6},{8,9},{9,8},{10,11... | collective-permute-start | bytes 6291464 | tf_op jit(solution)/shard_map/ppermute | solution.py:75
  158.4 28.0 %collective-permute-start.16 = (bf16[512,2048]{1,0:T(8,128)(2,1)}, bf16[512,2048]{1,0:T(8,128)(2,1)}, u32[]{:S(2)}, u32[]{:S(2)}) collective-permute-start(bf16[512,2048]{1,0:T(8,128)(2,1)} %collective-permute-done.15.refs_9_.refs_3_), channel_id=1, source_target_pairs={{0,1},{1,0},{2,3},{3,2},{4,5},{5,4},{6,7},{7,6},{8,9},{9,8},{10,11... | collective-permute-start | bytes 6291464 | tf_op jit(solution)/shard_map/ppermute | solution.py:75
  219.6 13.6 %collective-permute-start.18 = (bf16[2,512,2048]{2,1,0:T(8,128)(2,1)}, bf16[2,512,2048]{2,1,0:T(8,128)(2,1)}, u32[]{:S(2)}, u32[]{:S(2)}) collective-permute-start(bf16[2,512,2048]{2,1,0:T(8,128)(2,1)} %dn2_away.1.refs_4_), channel_id=1, source_target_pairs={{0,1},{1,0},{2,3},{3,2},{4,5},{5,4},{6,7},{7,6},{8,9},{9,8},{10,11... | collective-permute-start | bytes 12582920 | tf_op jit(solution)/shard_map/ppermute | solution.py:75
  220.0 64.1 %collective-permute-start.20 = (bf16[4,256,1408]{2,1,0:T(8,128)(2,1)S(1)}, bf16[4,256,1408]{2,1,0:T(8,128)(2,1)S(1)}, u32[]{:S(2)}, u32[]{:S(2)}) collective-permute-start(bf16[4,256,1408]{2,1,0:T(8,128)(2,1)S(1)} %copy-done.13), channel_id=1, source_target_pairs={{0,4},{1,5},{2,6},{3,7},{4,0},{5,1},{6,2},{7,3},{8,12},{9,13},{10,... | collective-permute-start | bytes 8650760 | tf_op jit(solution)/shard_map/ppermute | solution.py:75
  232.8 86.8 %collective-permute-start.17 = (bf16[2,512,2048]{2,1,0:T(8,128)(2,1)}, bf16[2,512,2048]{2,1,0:T(8,128)(2,1)}, u32[]{:S(2)}, u32[]{:S(2)}) collective-permute-start(bf16[2,512,2048]{2,1,0:T(8,128)(2,1)} %out_away.1.refs_8_), channel_id=1, source_target_pairs={{0,1},{1,0},{2,3},{3,2},{4,5},{5,4},{6,7},{7,6},{8,9},{9,8},{10,11... | collective-permute-start | bytes 12582920 | tf_op jit(solution)/shard_map/ppermute | solution.py:75
  254.9 47.4 %collective-permute-start.19 = (bf16[512,2048]{1,0:T(8,128)(2,1)}, bf16[512,2048]{1,0:T(8,128)(2,1)}, u32[]{:S(2)}, u32[]{:S(2)}) collective-permute-start(bf16[512,2048]{1,0:T(8,128)(2,1)} %get-tuple-element.57.refs_7_), channel_id=1, source_target_pairs={{0,2},{1,3},{2,0},{3,1},{4,6},{5,7},{6,4},{7,5},{8,10},{9,11},{10,... | collective-permute-start | bytes 6291464 | tf_op jit(solution)/shard_map/ppermute | solution.py:75
  267.2 128.9 %collective-permute-start.27 = (bf16[4,256,1408]{2,1,0:T(8,128)(2,1)}, bf16[4,256,1408]{2,1,0:T(8,128)(2,1)}, u32[]{:S(2)}, u32[]{:S(2)}) collective-permute-start(bf16[4,256,1408]{2,1,0:T(8,128)(2,1)} %up_send.1.refs_7_), channel_id=1, source_target_pairs={{0,4},{1,5},{2,6},{3,7},{4,0},{5,1},{6,2},{7,3},{8,12},{9,13},{10,... | collective-permute-start | bytes 8650760 | tf_op jit(solution)/shard_map/ppermute | solution.py:75
  297.6 230.3 %reduce-scatter.11.cloned.1.call-start = ((), (), s32[]{:S(2)}) async-start(), calls=%async_computation.11 | async-start | bytes 3604480 | tf_op jit(solution)/shard_map/reduce_scatter | solution.py:727
  318.6 44.6 %collective-permute-start.22 = (bf16[512,1024]{1,0:T(8,128)(2,1)S(1)}, bf16[512,1024]{1,0:T(8,128)(2,1)S(1)}, u32[]{:S(2)}, u32[]{:S(2)}) collective-permute-start(bf16[512,1024]{1,0:T(8,128)(2,1)S(1)} %get-tuple-element.85), channel_id=1, source_target_pairs={{0,1},{1,0},{2,3},{3,2},{4,5},{5,4},{6,7},{7,6},{8,9},{9,8},{10,11... | collective-permute-start | bytes 3145736 | tf_op jit(solution)/shard_map/ppermute | solution.py:75
  363.1 2.7 collective-permute-start.25
  364.7 24.6 %collective-permute-start.23 = (bf16[1024,512]{1,0:T(8,128)(2,1)}, bf16[1024,512]{1,0:T(8,128)(2,1)}, u32[]{:S(2)}, u32[]{:S(2)}) collective-permute-start(bf16[1024,512]{1,0:T(8,128)(2,1)} %get-tuple-element.83), channel_id=1, source_target_pairs={{0,4},{1,5},{2,6},{3,7},{4,0},{5,1},{6,2},{7,3},{8,12},{9,13},{10,... | collective-permute-start | bytes 3145736 | tf_op jit(solution)/shard_map/ppermute | solution.py:75
  367.0 44.7 %collective-permute-start.26 = (bf16[1024,512]{1,0:T(8,128)(2,1)S(1)}, bf16[1024,512]{1,0:T(8,128)(2,1)}, u32[]{:S(2)}, u32[]{:S(2)}) collective-permute-start(bf16[1024,512]{1,0:T(8,128)(2,1)S(1)} %get-tuple-element.79), channel_id=1, source_target_pairs={{0,4},{1,5},{2,6},{3,7},{4,0},{5,1},{6,2},{7,3},{8,12},{9,13},{10,... | collective-permute-start | bytes 3145736 | tf_op jit(solution)/shard_map/ppermute | solution.py:75
  408.2 134.5 %reduce-scatter.13.cloned.1.call-start = ((), (), s32[]{:S(2)}) async-start(), calls=%async_computation.12 | async-start | bytes 1310720 | tf_op jit(solution)/shard_map/reduce_scatter | solution.py:779
  408.4 119.4 %collective-permute-start.34 = (bf16[1408,1024]{1,0:T(8,128)(2,1)}, bf16[1408,1024]{1,0:T(8,128)(2,1)}, u32[]{:S(2)}, u32[]{:S(2)}) collective-permute-start(bf16[1408,1024]{1,0:T(8,128)(2,1)} %down_send.1.refs_8_), channel_id=1, source_target_pairs={{0,4},{1,5},{2,6},{3,7},{4,0},{5,1},{6,2},{7,3},{8,12},{9,13},{10,... | collective-permute-start | bytes 8650760 | tf_op jit(solution)/shard_map/ppermute | solution.py:75
  408.6 113.2 %collective-permute-start.21 = (bf16[512,2048]{1,0:T(8,128)(2,1)}, bf16[512,2048]{1,0:T(8,128)(2,1)}, u32[]{:S(2)}, u32[]{:S(2)}) collective-permute-start(bf16[512,2048]{1,0:T(8,128)(2,1)} %get-tuple-element.61.refs_9_), channel_id=1, source_target_pairs={{0,2},{1,3},{2,0},{3,1},{4,6},{5,7},{6,4},{7,5},{8,10},{9,11},{10,... | collective-permute-start | bytes 6291464 | tf_op jit(solution)/shard_map/ppermute | solution.py:75
  409.4 66.5 %collective-permute-start.24 = (bf16[2048,256]{1,0:T(8,128)(2,1)}, bf16[2048,256]{1,0:T(8,128)(2,1)S(1)}, u32[]{:S(2)}, u32[]{:S(2)}) collective-permute-start(bf16[2048,256]{1,0:T(8,128)(2,1)} %w_out_send.1.refs_8_), channel_id=1, source_target_pairs={{0,2},{1,3},{2,0},{3,1},{4,6},{5,7},{6,4},{7,5},{8,10},{9,11},{10,... | collective-permute-start | bytes 3145736 | tf_op jit(solution)/shard_map/ppermute | solution.py:75
  410.3 12.1 %collective-permute-start.28 = (bf16[2,256,256]{2,1,0:T(8,128)(2,1)S(1)}, bf16[2,256,256]{2,1,0:T(8,128)(2,1)S(1)}, u32[]{:S(2)}, u32[]{:S(2)}) collective-permute-start(bf16[2,256,256]{2,1,0:T(8,128)(2,1)S(1)} %get-tuple-element.88), channel_id=1, source_target_pairs={{8,0},{9,1},{10,2},{11,3},{12,4},{13,5},{14,6},{15,7},{16,8},{17,9... | collective-permute-start | bytes 786440 | tf_op jit(solution)/shard_map/ppermute | solution.py:87
  411.8 34.9 %collective-permute-start.29 = (bf16[2,256,256]{2,1,0:T(8,128)(2,1)S(1)}, bf16[2,256,256]{2,1,0:T(8,128)(2,1)S(1)}, u32[]{:S(2)}, u32[]{:S(2)}) collective-permute-start(bf16[2,256,256]{2,1,0:T(8,128)(2,1)S(1)} %get-tuple-element.87), channel_id=1, source_target_pairs={{16,0},{17,1},{18,2},{19,3},{20,4},{21,5},{22,6},{23,7},{24,8},{25... | collective-permute-start | bytes 786440 | tf_op jit(solution)/shard_map/ppermute | solution.py:87
  422.4 53.5 %copy-start.8 = (bf16[2,256,256]{2,1,0:T(8,128)(2,1)}, bf16[2,256,256]{2,1,0:T(8,128)(2,1)S(1)}, u32[]{:S(2)}) copy-start(bf16[2,256,256]{2,1,0:T(8,128)(2,1)S(1)} %collective-permute-done.28.refs_9_) | copy-start | bytes 786436
  446.6 29.3 %copy-start.10 = (bf16[2,256,256]{2,1,0:T(8,128)(2,1)}, bf16[2,256,256]{2,1,0:T(8,128)(2,1)S(1)}, u32[]{:S(2)}) copy-start(bf16[2,256,256]{2,1,0:T(8,128)(2,1)S(1)} %collective-permute-done.29.refs_10_) | copy-start | bytes 786436
  504.3 5.3 collective-permute-start.30
  507.7 51.0 %reduce-scatter.9.cloned.1.call-start = ((), (), s32[]{:S(2)}) async-start(), calls=%async_computation.10 | async-start | bytes 245760 | tf_op jit(solution)/shard_map/reduce_scatter | solution.py:803
  509.9 10.4 %collective-permute-start.31 = (bf16[4,2,64,384]{3,2,1,0:T(8,128)(2,1)S(1)}, bf16[4,2,64,384]{3,2,1,0:T(8,128)(2,1)S(1)}, u32[]{:S(2)}, u32[]{:S(2)}) collective-permute-start(bf16[4,2,64,384]{3,2,1,0:T(8,128)(2,1)S(1)} %dynamic-slice_bitcast_fusion.1), channel_id=1, source_target_pairs={{0,2},{1,3},{2,0},{3,1},{4,6},{5,7},{6,4},{7,5},{8,10},{9,11},{10,... | collective-permute-start | bytes 1179656 | tf_op jit(solution)/shard_map/ppermute | solution.py:75
  510.8 32.0 %collective-permute-start.33 = (bf16[2048,256]{1,0:T(8,128)(2,1)}, bf16[2048,256]{1,0:T(8,128)(2,1)S(1)}, u32[]{:S(2)}, u32[]{:S(2)}) collective-permute-start(bf16[2048,256]{1,0:T(8,128)(2,1)} %w_query_send.1.refs_8_), channel_id=1, source_target_pairs={{0,2},{1,3},{2,0},{3,1},{4,6},{5,7},{6,4},{7,5},{8,10},{9,11},{10,... | collective-permute-start | bytes 3145736 | tf_op jit(solution)/shard_map/ppermute | solution.py:75
  520.4 6.6 collective-permute-start.32
  527.8 69.9 %reduce-scatter.15.cloned.1.call-start = ((), (), s32[]{:S(2)}) async-start(), calls=%async_computation.13 | async-start | bytes 1310720 | tf_op jit(solution)/shard_map/reduce_scatter | solution.py:821
  551.0 95.0 %reduce-scatter.17.cloned.1.call-start = ((), (), s32[]{:S(2)}) async-start(), calls=%async_computation.14 | async-start | bytes 3604480 | tf_op jit(solution)/shard_map/reduce_scatter | solution.py:813
  559.6 11.2 %all-to-all-start.1 = ((bf16[8,64,256]{2,1,0:T(8,128)(2,1)}), bf16[8,64,256]{2,1,0:T(8,128)(2,1)S(1)}, u32[]{:S(2)}, u32[]{:S(2)}) async-start(bf16[8,64,256]{2,1,0:T(8,128)(2,1)} %bitcast.31), calls=%async_computation.6 | async-start | bytes 524288 | tf_op jit(solution)/shard_map/all_to_all | solution.py:817
  572.2 23.5 %all-to-all-start.2 = ((bf16[4,2,64,1408]{3,2,1,0:T(8,128)(2,1)}), bf16[4,2,64,1408]{3,2,1,0:T(8,128)(2,1)}, u32[]{:S(2)}, u32[]{:S(2)}) async-start(bf16[4,2,64,1408]{3,2,1,0:T(8,128)(2,1)} %bitcast.125), calls=%async_computation.7 | async-start | bytes 2883584 | tf_op jit(solution)/shard_map/all_to_all | solution.py:853
  597.7 9.8 %all-to-all-start = ((bf16[8,64,256]{2,1,0:T(8,128)(2,1)}), bf16[8,64,256]{2,1,0:T(8,128)(2,1)S(1)}, u32[]{:S(2)}, u32[]{:S(2)}) async-start(bf16[8,64,256]{2,1,0:T(8,128)(2,1)} %bitcast.139), calls=%async_computation.5 | async-start | bytes 524288 | tf_op jit(solution)/shard_map/all_to_all | solution.py:817
  647.2 29.3 %collective-permute-start.35 = (bf16[176,1024]{1,0:T(8,128)(2,1)S(1)}, bf16[176,1024]{1,0:T(8,128)(2,1)S(1)}, u32[]{:S(2)}, u32[]{:S(2)}) collective-permute-start(bf16[176,1024]{1,0:T(8,128)(2,1)S(1)} %get-tuple-element.93), channel_id=1, source_target_pairs={{0,0},{1,8},{2,16},{3,24},{4,1},{5,9},{6,17},{7,25},{8,2},{9,10},{... | collective-permute-start | bytes 1081352 | tf_op jit(solution)/shard_map/ppermute | solution.py:832
  649.8 34.4 %collective-permute-start.36 = (bf16[176,1024]{1,0:T(8,128)(2,1)S(1)}, bf16[176,1024]{1,0:T(8,128)(2,1)S(1)}, u32[]{:S(2)}, u32[]{:S(2)}) collective-permute-start(bf16[176,1024]{1,0:T(8,128)(2,1)S(1)} %get-tuple-element.94), channel_id=1, source_target_pairs={{0,1},{1,9},{2,17},{3,25},{4,0},{5,8},{6,16},{7,24},{8,3},{9,11},{... | collective-permute-start | bytes 1081352 | tf_op jit(solution)/shard_map/ppermute | solution.py:832
  (18 other events, 122.9 us)
Sparse Core Ops, SparseCore 0:
  297.7 61.6 reduce-scatter.6
  408.4 72.3 reduce-scatter.10
  507.8 32.0 reduce-scatter.12
  542.7 15.9 reduce-scatter.8
  561.5 27.3 reduce-scatter.14
  591.1 54.8 reduce-scatter.16

commit v2 on v1

--- a/solution.py
+++ b/solution.py
@@ -22,11 +22,12 @@
 MIB = 2**20
 ONCE = pl.Buffered(1)
 ANY = pl.BlockSpec(memory_space=pl.ANY)
-SCALE = 1.0
+SCALE = 20.0
+HOLD_KV = True
 COST = dict(
-    norm_keys=5, query=9, attend=30, project_out=11, down_back=20, feed=21, gate_send=11, up_send=11, down_send=11,
+    norm_keys=5, query=9, attend=14, project_out=11, down_back=20, feed=21, gate=19, gate_send=11, up_send=11, down_send=11,
     gate_keep=12, up_keep=12, down_keep=12, dn2_away=20, dn2_near=22, out_away=11, out_near=13, mid_back=14,
-    attend_back=29, w_out_send=7, w_out_keep=7, w_query_send=7, w_query_keep=7, tokens_back=14, output=5,
+    attend_back=23, w_out_send=7, w_out_keep=7, w_query_send=7, w_query_keep=7, tokens_back=14, output=5, hold=1,
 )
 
 
@@ -101,37 +102,46 @@
     return jnp.where(allow, 0.0, masked)
 
 
-def fwd_kernel(q_ref, cos_ref, sin_ref, start_ref, k_ref, v_ref, o_ref, qr_ref, lse_ref, *, heads, rb, hop):
-    rows = q_ref.shape[0]
-    scale = 1.0 / math.sqrt(128)
-    lses = []
-    for r in range(rows // rb):
-        sl = pl.ds(r * rb, rb)
-        k0 = max(0, r * rb + hop - WINDOW)
-        k0 -= k0 % 128
-        k1 = (r + 1) * rb + hop
-        bias = mask_bias(start_ref[sl, :], rb, r * rb, k1 - k0, k0, hop)
-        cosine, sine = cos_ref[sl, :], sin_ref[sl, :]
-        kk = k_ref[0, pl.ds(k0, k1 - k0), :]
-        vv = v_ref[0, pl.ds(k0, k1 - k0), :]
-        lse_row = []
-        for h in range(heads):
-            hs = pl.ds(h * 128, 128)
-            qr = turn(q_ref[sl, hs], cosine, sine).astype(bf16)
-            qr_ref[sl, hs] = qr
-            s = dot(qr, kk, 1, 1) * scale + bias
+def row_blocks(rows, block, hop):
+    for r in range(0, rows, block):
+        first = max(0, r + hop - WINDOW)
+        first -= first % 128
+        yield pl.ds(r, block), r, first, r + block + hop - first
+
+
+def masked_scores(q, k, bias):
+    rows, keys = bias.shape
+    s = dot(q, k, 1, 1)
+    return (s.reshape(s.shape[0] // rows, rows, keys) + bias[None]).reshape(s.shape)
+
+
+def fwd_kernel(q_ref, cos_ref, sin_ref, start_ref, k_ref, v_ref, o_ref, qr_ref, lse_ref, *, hop):
+    scale = math.log2(math.e) / math.sqrt(128)
+    for sl, r, first, count in row_blocks(q_ref.shape[0], ROWS, hop):
+        bias = mask_bias(start_ref[sl, :], ROWS, r, count, first, hop)
+        cosine, sine = cos_ref[sl, :] * scale, sin_ref[sl, :] * scale
+        kk, vv = k_ref[0, pl.ds(first, count), :], v_ref[0, pl.ds(first, count), :]
+        for g in range(0, HEADS, TOGETHER):
+            heads = range(g, g + TOGETHER)
+            parts = []
+            for h in heads:
+                hs = pl.ds(h * 128, 128)
+                part = turn(q_ref[sl, hs], cosine, sine).astype(bf16)
+                qr_ref[sl, hs] = part
+                parts.append(part)
+            s = masked_scores(jnp.concatenate(parts, axis=0), kk, bias)
             top = jnp.max(s, axis=1, keepdims=True)
-            e = jnp.exp(s - top)
+            e = jnp.exp2(s - top)
             total = jnp.sum(e, axis=1, keepdims=True)
-            p = (e * (1.0 / total)).astype(bf16)
-            o_ref[sl, hs] = dot(p, vv, 1, 0).astype(bf16)
-            lse_row.append(top + jnp.log(total))
-        lses.append(jnp.concatenate(lse_row, axis=1))
-    lse_ref[0, 0] = jnp.concatenate(lses, axis=0)
-
-
-def bwd_kernel(q_ref, o_ref, do_ref, lse_ref, cos_ref, sin_ref, start_ref, k_ref, v_ref, dq_ref, dk_ref, dv_ref, *, heads, rb, hop):
-    rows = q_ref.shape[0]
+            o = dot(e.astype(bf16), vv, 1, 0) * (1.0 / total)
+            lse = top + jnp.log2(total)
+            for i, h in enumerate(heads):
+                at = slice(i * ROWS, (i + 1) * ROWS)
+                o_ref[sl, pl.ds(h * 128, 128)] = o[at].astype(bf16)
+                lse_ref[0, 0, sl, h : h + 1] = lse[at]
+
+
+def bwd_kernel(q_ref, o_ref, do_ref, lse_ref, cos_ref, sin_ref, start_ref, k_ref, v_ref, dq_ref, dk_ref, dv_ref, *, hop):
     scale = 1.0 / math.sqrt(128)
 
     @pl.when(pl.program_id(1) == 0)
@@ -139,35 +149,33 @@
         dk_ref[...] = jnp.zeros_like(dk_ref)
         dv_ref[...] = jnp.zeros_like(dv_ref)
 
-    for r in range(rows // rb):
-        sl = pl.ds(r * rb, rb)
-        k0 = max(0, r * rb + hop - WINDOW)
-        k0 -= k0 % 128
-        k1 = (r + 1) * rb + hop
-        ks = pl.ds(k0, k1 - k0)
-        bias = mask_bias(start_ref[sl, :], rb, r * rb, k1 - k0, k0, hop)
-        cosine, sine = cos_ref[sl, :], sin_ref[sl, :]
+    for sl, r, first, count in row_blocks(q_ref.shape[0], ROWS, hop):
+        ks = pl.ds(first, count)
+        bias = mask_bias(start_ref[sl, :], ROWS, r, count, first, hop)
+        cosine, sine = cos_ref[sl, :] * scale, sin_ref[sl, :] * scale
         kk, vv = k_ref[0, ks, :], v_ref[0, ks, :]
         dk = dv = None
-        for h in range(heads):
-            hs = pl.ds(h * 128, 128)
-            q, do = q_ref[sl, hs], do_ref[sl, hs]
-            inner = jnp.sum(do.astype(f32) * o_ref[sl, hs].astype(f32), axis=1, keepdims=True)
-            s = dot(q, kk, 1, 1) * scale + bias
-            p = jnp.exp(s - lse_ref[0, 0, sl, h : h + 1])
-            dp = dot(do, vv, 1, 1)
-            ds = (p * ((dp - inner) * scale)).astype(bf16)
+        for g in range(0, HEADS, TOGETHER):
+            heads = range(g, g + TOGETHER)
+            of = lambda ref: [ref[sl, pl.ds(h * 128, 128)] for h in heads]
+            q, do = jnp.concatenate(of(q_ref), axis=0), jnp.concatenate(of(do_ref), axis=0)
+            o = jnp.concatenate(of(o_ref), axis=0)
+            lse = jnp.concatenate([lse_ref[0, 0, sl, h : h + 1] for h in heads], axis=0)
+            inner = jnp.sum(do.astype(f32) * o.astype(f32), axis=1, keepdims=True)
+            p = jnp.exp2(masked_scores(q, kk, bias) - lse)
+            ds = (p * (dot(do, vv, 1, 1) - inner)).astype(bf16)
             dq = dot(ds, kk, 1, 0)
-            dq_ref[sl, hs] = turn(dq, cosine, -sine).astype(bf16)
-            dkh = dot(ds, q, 0, 0)
-            dvh = dot(p.astype(bf16), do, 0, 0)
-            dk = dkh if dk is None else dk + dkh
-            dv = dvh if dv is None else dv + dvh
-        dk_ref[0, ks, :] += dk
+            for i, h in enumerate(heads):
+                dq_ref[sl, pl.ds(h * 128, 128)] = turn(dq[i * ROWS : (i + 1) * ROWS], cosine, -sine).astype(bf16)
+            dk_part, dv_part = dot(ds, q, 0, 0), dot(p.astype(bf16), do, 0, 0)
+            dk = dk_part if dk is None else dk + dk_part
+            dv = dv_part if dv is None else dv + dv_part
+        dk_ref[0, ks, :] += dk * (1.0 / math.log2(math.e))
         dv_ref[0, ks, :] += dv
 
 
-HEADS = 4
+HEADS = 8
+TOGETHER = 4
 ROWS = 128
 
 
@@ -187,7 +195,7 @@
     wide, table, start, key, lse = attention_specs(L, span)
     steps = width // (HEADS * 128)
     return call(
-        functools.partial(fwd_kernel, heads=HEADS, rb=ROWS, hop=hop),
+        functools.partial(fwd_kernel, hop=hop),
         "attend",
         (q_lin, cosine, sine, starts, keys, values),
         deps,
@@ -209,7 +217,7 @@
     wide, table, start, key, lse = attention_specs(L, span)
     steps = width // (HEADS * 128)
     return call(
-        functools.partial(bwd_kernel, heads=HEADS, rb=ROWS, hop=hop),
+        functools.partial(bwd_kernel, hop=hop),
         "attend_back",
         (queries, attended, d_attended, lses, cosine, sine, starts, keys, values),
         deps,
@@ -230,6 +238,11 @@
 
 def shape(dims, dtype=bf16):
     return jax.ShapeDtypeStruct(dims, dtype)
+
+
+def hold(value, deps):
+    [out] = call(lambda: None, "hold", (), deps, out_shape=[], out_specs=[], passes=(value,))
+    return out
 
 
 def norm_keys(tokens, gain, w_kv, cosine, sine):
@@ -510,25 +523,27 @@
     )
 
 
-def token_products(name, rows, near, away, half, got=None, deps=(), passes=()):
+def token_products(name, rows, d_all, half, got=None, deps=(), passes=()):
     T, M = rows[0].shape
-    N = near.shape[1] // 2
+    N = d_all[0].shape[1] // 2
     block = 512
+    n = len(rows)
     extra = () if got is None else (got,)
 
-    def kernel(s_ref, n0, n1, n2, n3, a_ref, b_ref, *rest):
-        total = dot(n0[...], a_ref[:T], 0, 0) + dot(n1[...], a_ref[T:], 0, 0)
-        total = total + dot(n2[...], b_ref[:T], 0, 0) + dot(n3[...], b_ref[T:], 0, 0)
+    def kernel(s_ref, *refs):
+        total = dot(refs[0][...], refs[n][...], 0, 0)
+        for i in range(1, n):
+            total = total + dot(refs[i][...], refs[n + i][...], 0, 0)
         if extra:
-            total = total + rest[0][...].astype(f32)
-        rest[-1][...] = total.astype(bf16)
+            total = total + refs[2 * n][...].astype(f32)
+        refs[-1][...] = total.astype(bf16)
 
     cut = pl.BlockSpec((T, block), lambda i, s: (0, i))
-    col = pl.BlockSpec((2 * T, N), lambda i, s: (0, s[0]), pipeline_mode=ONCE)
+    col = pl.BlockSpec((T, N), lambda i, s: (0, s[0]), pipeline_mode=ONCE)
     out = pl.BlockSpec((block, N), lambda i, s: (i, 0))
     return call(
-        kernel, name, (*rows, near, away, *extra), deps, (half,), grid=(M // block,),
-        in_specs=[cut] * 4 + [col, col] + [out] * len(extra),
+        kernel, name, (*rows, *d_all, *extra), deps, (half,), grid=(M // block,),
+        in_specs=[cut] * n + [col] * n + [out] * len(extra),
         out_specs=out,
         out_shape=shape((M, N)),
         passes=passes,
@@ -688,12 +703,15 @@
 
     normed, inv1, kv = norm_keys(rows, norm1_gain, w_kv, cosine, sine)
     kv = kv.reshape(groups, L, 2 * hd)
-    earlier = [mv.shift(kv, "z", range(nz), distance) for distance in range(hops, 0, -1)]
-    kv_all = jnp.concatenate(earlier + [kv], axis=1)
+    blocks = [kv]
+    for _ in range(hops):
+        blocks.insert(0, mv.shift(blocks[0], "z", range(nz), 1))
+    kv_all = jnp.concatenate(blocks, axis=1)
     keys, values = kv_all[:, :, :hd], kv_all[:, :, hd:]
     q_lin = project_query(normed, w_query, (kv,))
     attended, queries, lses = attention(q_lin, cosine, sine, starts_rel, keys, values, hop)
-    mid, normed2, inv2, cot2 = project_out(attended, w_output, rows, norm2_gain, (cot1,), (cot2,))
+    mid, normed2, inv2 = project_out(attended, w_output, rows, norm2_gain, (cot1,))
+    cot2 = hold(cot2, (normed2,))
     cot3 = mv.flip(cot2, 1)
 
     def of_group(v):
@@ -705,7 +723,8 @@
     n1 = mv.flip(normed2, 1)
     n2 = mv.flip(normed2, 2)
     d_hidden = down_back(qi, (cot, cot1, cot2, cot3), w_down, (normed2,))
-    h_a, dg_a, du_a, n2 = feed(qi, (normed2, n1), d_hidden, 0, w_gate, w_up, normed_all[1:], (n2,))
+    h_a, dg_a, du_a = feed(qi, (normed2, n1), d_hidden, 0, w_gate, w_up, normed_all[1:])
+    n2 = hold(n2, (du_a,))
     n3 = mv.flip(n2, 1)
     h_b, dg_b, du_b = feed(qi, (n2, n3), d_hidden, 2 * T, w_gate, w_up, (du_a,))
     n_all, c_all = (normed2, n1, n2, n3), (cot, cot1, cot2, cot3)
@@ -727,98 +746,110 @@
         return part, lax.psum_scatter(part, "seq", scatter_dimension=0, tiled=True)
 
     dn_pairs = [[dg_a, dg_b], [du_a, du_b]]
-    gate_sent = send_rows("gate_send", dg_a, dg_b, (du_b,) + attended_all[1:])
-    dn_away = partial_away("dn2_away", qi, dn_pairs, [w_gate, w_up], 1, (gate_sent[0],))
-    dn_got = mv.flip(dn_away, 1)
-    out_away = partial_away("out_away", qi, [[h_a, h_b]], [w_down], 0, (dn_away,))
-    dn_far, dn_own = partial_near("dn2_near", qi, dn_pairs, [w_gate, w_up], 1, dn_got, (out_away,))
-    dn_last = mv.flip(dn_far, 2)
-    out_got = mv.flip(out_away, 1)
-    up_sent = send_rows("up_send", du_a, du_b, (dn_far,))
     halves = 2 if paired else 1
     first_half = 1 - yi if paired else 0 * yi
-    down_sent = columns_product("down_send", h_a, h_b, c_all, first_half, halves, None, (up_sent[0],))
-    gate_kept, r_gate = keep_rows("gate_keep", gate_sent, dg_a, dg_b, (down_sent,))
-    d_branch, norm2_term, d_attended = mid_back(
-        dn_own, dn_last, mid, inv2, cot, norm2_gain, w_output, (gate_kept,)
-    )
-    out_far, out_own = partial_near("out_near", qi, [[h_a, h_b]], [w_down], 0, out_got, (d_attended,))
-    out_last = mv.flip(out_far, 2)
+    up_sent = send_rows("up_send", du_a, du_b, (du_b,) + attended_all[1:])
+    g_gate = rows_product("gate", n_all, dg_a, dg_b, 0 * yi, (D // 256, 1), None, (up_sent[0],))
+    dg_a = hold(dg_a, (g_gate,))
+    dn_pairs = [[dg_a, dg_b], [du_a, du_b]]
+    dn_away = partial_away("dn2_away", qi, dn_pairs, [w_gate, w_up], 1, ())
+    dn_got = mv.flip(dn_away, 1)
+    down_sent = columns_product("down_send", h_a, h_b, c_all, first_half, halves, None, (dn_away,))
+    dn_far, dn_own = partial_near("dn2_near", qi, dn_pairs, [w_gate, w_up], 1, dn_got, (down_sent,))
+    dn_last = mv.flip(dn_far, 2)
+    out_away = partial_away("out_away", qi, [[h_a, h_b]], [w_down], 0, (dn_far,))
+    out_got = mv.flip(out_away, 1)
+    g_gate = g_gate.reshape(D, fq)
     if paired:
         down_got = mv.flip(down_sent, GROUP)
-
-    def to_quarters(d):
-        cut = lambda v, i: lax.dynamic_slice_in_dim(v, i * (v.shape[1] // 2), v.shape[1] // 2, 1)
-        chip = jnp.concatenate([cut(d, core), mv.flip(cut(d, 1 - core), 1)], axis=0)
-        return cut(chip, mv.y), mv.flip(cut(chip, 1 - mv.y), GROUP)
-
+        z_gate = lax.psum_scatter(g_gate, "seq", scatter_dimension=0, tiled=True)
+    else:
+        z_gate = sum_all(g_gate)
+    up_kept, r_up = keep_rows("up_keep", up_sent, du_a, du_b, (out_away,))
+    out_far, out_own = partial_near("out_near", qi, [[h_a, h_b]], [w_down], 0, out_got, (up_kept,))
+    out_last = mv.flip(out_far, 2)
+    d_branch, norm2_term, d_attended = mid_back(
+        dn_own, dn_last, mid, inv2, cot, norm2_gain, w_output, (out_far,)
+    )
+
+    def quarters(d):
+        w = D // GROUP
+        at = core * 2 + mv.y
+        return [lax.dynamic_slice_in_dim(d, (at ^ k) * w, w, 1) for k in (0, 2, 1, 3)]
+
+    def exchange(cuts):
+        return cuts[0], mv.flip(cuts[1], 1), mv.flip(cuts[2], GROUP), mv.flip(cuts[3], GROUP + 1)
+
+    db_cuts = quarters(d_branch) if paired else ()
+    db_all = exchange(db_cuts) if paired else ()
     d_query, dk_all, dv_all = attention_back(
-        queries, attended, d_attended, lses, cosine, sine, starts_rel, keys, values, hop, (out_far,)
+        queries, attended, d_attended, lses, cosine, sine, starts_rel, keys, values, hop, db_cuts
     )
     dkv_all = jnp.concatenate([dk_all, dv_all], axis=2)
-    backs = [
-        mv.shift(dkv_all[:, (hops - k) * L : (hops - k + 1) * L].astype(bf16), "z", range(nz), -k)
-        for k in range(1, hops + 1)
-    ]
+    parts = [dkv_all[:, k * L : (k + 1) * L].astype(bf16) for k in range(hops)]
+    back = mv.shift(parts[0], "z", range(nz), -1)
     if paired:
-        db_near, db_away = to_quarters(d_branch)
-        out_sent = token_products("w_out_send", attended_all, db_near, db_away, 1 - xi, None, (d_query,))
+        dq_all = exchange(quarters(d_query))
+        down_kept = columns_product(
+            "down_keep", h_a, h_b, c_all, yi, 2, down_got, (d_query, z_gate) + tuple(db_all[1:2])
+        )
+        r_down = lax.psum_scatter(down_kept, "seq", scatter_dimension=0, tiled=True)
+        last = down_kept
+    else:
+        r_gate, last = z_gate[None], d_query
+    output = final_output(mid, out_own, out_last, (last,))
+    last = output
+    if paired:
+        z_gate = hold(z_gate, (output,)).reshape(2, D // (2 * nz), fq)
+        gate_away = mv.flip(lax.dynamic_index_in_dim(z_gate, 1 - mv.y, 0, keepdims=False), GROUP)
+    back = hold(back, (last,))
+    for part in parts[1:]:
+        back = mv.shift((back.astype(f32) + part.astype(f32)).astype(bf16), "z", range(nz), -1)
+    if paired:
+        out_sent = token_products("w_out_send", attended_all, db_all, 1 - xi, None, (last, r_up) + dq_all[1:])
         out_recv = mv.flip(out_sent, 2)
-        last = out_sent
-    else:
-        last = d_query
-    up_kept, r_up = keep_rows("up_keep", up_sent, du_a, du_b, (last, r_gate))
-    if paired:
-        dq_near, dq_away = to_quarters(d_query)
-        query_sent = token_products("w_query_send", normed_all, dq_near, dq_away, 1 - xi, None, (up_kept,))
+        query_sent = token_products("w_query_send", normed_all, dq_all, 1 - xi, None, (out_sent,))
         query_recv = mv.flip(query_sent, 2)
-        g_out, *backs = token_products(
-            "w_out_keep", attended_all, db_near, db_away, xi, out_recv, (query_sent,), backs
-        )
-        last = g_out
-        r_out = lax.psum_scatter(g_out, "seq", scatter_dimension=0, tiled=True)
-    own = dkv_all[:, hop:]
-    for back in backs:
-        own = own + back.astype(f32)
+        back = hold(back, (query_sent,))
+        last = query_sent
+    own = dkv_all[:, hop:] + back.astype(f32)
     own = own.reshape(T, 2 * hd)
     swapped = jnp.concatenate([own[:, half:hd], own[:, :half]], axis=1)
     d_key = (own[:, :hd] * cosine - swapped * sine).astype(bf16)
     d_kv = jnp.concatenate([d_key, own[:, hd:].astype(bf16)], axis=1)
-
     grad_tokens, norm1_term = tokens_back(
         d_query, d_kv, w_query, w_kv, d_branch, rows, inv1, norm1_gain, (last,)
     )
-    output = final_output(mid, out_own, out_last, (norm1_term,))
     g_kv = dot(normed, d_kv, 0, 0, bf16)
     if paired:
         terms = jnp.concatenate([norm1_term, norm2_term, jnp.zeros((126, D), f32)], axis=0).T
+        size = D // n_dev
         g_kv = jnp.concatenate([g_kv, terms.astype(bf16)], axis=1)
-        width = g_kv.shape[1]
-        g_kv = g_kv.reshape(nz, 2, 2, 2, D // n_dev, width)
-        for axis, mask in ((3, 1), (2, 2), (1, GROUP)):
-            bit = mv.bit(mask)
-            away = mv.flip(lax.dynamic_index_in_dim(g_kv, 1 - bit, axis, keepdims=False), mask)
-            kept = lax.dynamic_index_in_dim(g_kv, bit, axis, keepdims=False)
-            g_kv = (kept.astype(f32) + away.astype(f32)).astype(bf16)
-        r_kv = lax.psum_scatter(g_kv, "seq", scatter_dimension=0, tiled=True)[0].astype(f32)
-        norms = r_kv[:, 2 * hd : 2 * hd + 2].T
-    else:
-        r_kv = lax.psum_scatter(g_kv, AXES, scatter_dimension=0, tiled=True).astype(f32)
-        norms = jnp.concatenate([norm1_term, norm2_term], axis=0)
-        norms = norms.reshape(2, n_dev, D // n_dev).transpose(1, 0, 2)
-        norms = jnp.sum(lax.all_to_all(norms, AXES, 0, 0, tiled=True), axis=0)
-
-    if paired:
-        down_kept = columns_product("down_keep", h_a, h_b, c_all, yi, 2, down_got, (output, r_up))
-        r_down = lax.psum_scatter(down_kept, "seq", scatter_dimension=0, tiled=True)
-        g_query = token_products("w_query_keep", normed_all, dq_near, dq_away, xi, query_recv, (down_kept, r_out))
+        g_kv = g_kv.reshape(nz, nb, size, 2 * hd + 128).transpose(1, 0, 2, 3)
+        g_kv = lax.all_to_all(g_kv, "batch", 0, 0, tiled=True)
+        g_out = token_products("w_out_keep", attended_all, db_all, xi, out_recv, (grad_tokens, r_down))
+        r_out = lax.psum_scatter(g_out, "seq", scatter_dimension=0, tiled=True)
+        g_query = token_products("w_query_keep", normed_all, dq_all, xi, query_recv, (g_out,))
+        g_kv = hold(g_kv, (g_query,)) if HOLD_KV else g_kv
+        g_kv = jnp.sum(g_kv.astype(f32), axis=0).astype(bf16)
+        gate_away = hold(gate_away, (g_out,))
+        gate_kept = lax.dynamic_index_in_dim(z_gate, mv.y, 0, keepdims=False)
+        r_gate = (gate_kept.astype(f32) + gate_away.astype(f32)).astype(bf16)[None]
+        joined = [
+            g_query.reshape(nz, D // nz, D // nb),
+            g_kv[:, :, : 2 * hd],
+            jnp.pad(g_kv[:, :, 2 * hd :], ((0, 0), (0, 0), (0, D // nb - 128))),
+        ]
+        r_query = lax.psum_scatter(jnp.concatenate(joined, axis=1), "seq", scatter_dimension=0, tiled=True)[0]
+        r_kv = r_query[D // nz : D // nz + size].astype(f32)
+        norms = r_query[D // nz + size :, :2].astype(f32).T
+        r_query = r_query[: D // nz]
 
         def finish(r):
             r = lax.all_to_all(r.reshape(nb, D // n_dev, D // nb), "batch", 0, 0, tiled=True)
             order = [y_ * GROUP + x_ * 2 + c_ for c_ in range(2) for y_ in range(2) for x_ in range(2)]
             return jnp.concatenate([r[b_] for b_ in order], axis=1).astype(f32)
 
-        r_query = lax.psum_scatter(g_query, "seq", scatter_dimension=0, tiled=True)
         grad_output, grad_query = finish(r_out), finish(r_query)
         r_down = r_down.reshape(2, fq // (2 * nz), D // 2)
         parts = []
@@ -834,6 +865,10 @@
         second = jnp.where(core == 0, parts[1], parts[0])
         grad_down = jnp.concatenate([first, second], axis=1).astype(f32)
     else:
+        r_kv = lax.psum_scatter(g_kv, AXES, scatter_dimension=0, tiled=True).astype(f32)
+        norms = jnp.concatenate([norm1_term, norm2_term], axis=0)
+        norms = norms.reshape(2, n_dev, D // n_dev).transpose(1, 0, 2)
+        norms = jnp.sum(lax.all_to_all(norms, AXES, 0, 0, tiled=True), axis=0)
         r_down = sum_all(down_sent)
         pairs = [
             (z_ * nb + b_, (b_ % GROUP) * ny * nz + z_ * ny + b_ // GROUP)
@@ -860,7 +895,7 @@
         norms[0],
         grad_query,
         r_kv[:, :hd],
-        r_kv[:, hd : 2 * hd],
+        r_kv[:, hd:],
         grad_output,
         norms[1],
         gu[0],

time: 697 us -> 526 us (0.75)
  waiting for transfers between devices: 232 us -> 54.8 us
  Pallas kernels: 345 us -> 319 us
  starting transfers between devices: 58.2 us -> 69.7 us
  local copies, waits for them, and re-layouts: 24.2 us -> 33.8 us
  other arithmetic: 15.9 us -> 23.1 us
    ppermute x28 -> x27, waiting for transfers between devices: 108 us -> 16.3 us  [flip(): return lax.ppermute(value, AXES, pairs)]
    reduce_scatter x1, waiting for transfers between devices: 38.5 us -> 0.01 us  [shards(): r_down = lax.psum_scatter(down_kept, 'seq', scatter_dimension=0, tiled=True)]
    pallas_call x25 -> x32, Pallas kernels: 345 us -> 319 us  [call(): pl.pallas_call(body, grid_spec=pltpu.PrefetchScalarGridSpec(num_scalar_pr...]
    ppermute x7, waiting for transfers between devices: 26.7 us -> 2.89 us  [shift(): return lax.ppermute(value, AXES, pairs)]
    ppermute x2, waiting for transfers between devices: 30.9 us -> 8.54 us  [shards(): parts.append(lax.ppermute(piece, AXES, pairs))]
    all_to_all x1, waiting for transfers between devices: 17 us -> 3.41 us  [finish_quarter(): r = lax.all_to_all(r, 'batch', 0, 0, tiled=True, axis_index_groups=fours)]
    all_to_all x0 -> x1, waiting for transfers between devices: none -> 13.1 us  [shards(): g_kv = lax.all_to_all(g_kv, 'batch', 0, 0, tiled=True)]
    unnamed x61 -> x77, local copies, waits for them, and re-layouts: 11.4 us -> 15.5 us
  transfers between devices with their start and end apart: 46 -> 45, of which waited for: 20 -> 11; matrix products, arithmetic and copies ran while one was open for 5% -> 8% of each run, Pallas kernels for 45% -> 58%
where the time goes in v2:
time: 526 us; the launch traced here: 518 us
  Pallas kernels  319 us (61%)
  starting transfers between devices  69.7 us (13%)
  waiting for transfers between devices  54.8 us (10%)
  local copies, waits for them, and re-layouts  33.8 us (6%)
  other arithmetic  23.1 us (4%)
  between operations  14.7 us (3%)
    pallas_call x32, Pallas kernels, call(): pl.pallas_call(body, grid_spec=pltpu.PrefetchScalarGridSpec(num_scalar_pr...  319 us
    ppermute x27, starting transfers between devices, flip(): return lax.ppermute(value, AXES, pairs)  24.2 us
    ppermute x7, starting transfers between devices, shift(): return lax.ppermute(value, AXES, pairs)  18.1 us
    ppermute x27, waiting for transfers between devices, flip(): return lax.ppermute(value, AXES, pairs)  16.3 us
    unnamed x77, local copies, waits for them, and re-layouts  15.5 us
    all_to_all x1, waiting for transfers between devices, shards(): g_kv = lax.all_to_all(g_kv, 'batch', 0, 0, tiled=True)  13.1 us
  transfers between devices with their start and end apart: 45, of which 11 were waited for; matrix products, arithmetic and copies ran while one was open for 8% of the time, Pallas kernels for 58%

profile of v2, /device:TPU:5, one launch (start us, length us, event | category | flops | bytes accessed | tf_op | source)
XLA Modules:
  0.0 517.5 jit_solution(6976097532899170316)
XLA Ops:
  7.9 5.2 %collective-permute-start.2 = (s32[2,256]{1,0:T(2,128)S(1)}, s32[2,256]{1,0:T(2,128)S(1)}, u32[]{:S(2)}, u32[]{:S(2)}) collective-permute-start(s32[2,256]{1,0:T(2,128)S(1)} %broadcast_add_fusion), channel_id=1, source_target_pairs={{0,24},{1,25},{2,26},{3,27},{4,28},{5,29},{6,30},{7,31}} | collective-permute-start | bytes 6152 | tf_op jit(solution)/shard_map/ppermute | solution.py:88
  14.5 2.2 collective-permute-start
  22.8 4.9 norm_keys.1
  27.7 2.6 collective-permute-start.3
  31.5 2.6 collective-permute-start.5
  34.4 4.0 collective-permute-start.4
  38.4 9.2 %query.1.refs_0_ = f32[512,2048]{1,0:T(8,128)} custom-call(bf16[512,2048]{1,0:T(8,128)(2,1)} %get-tuple-element.38.refs_0_.refs_1_, bf16[2048,2048]{1,0:T(8,128)(2,1)} %refs_2_.1, bf16[2,256,256]{2,1,0:T(8,128)(2,1)} %bitcast.149), custom_call_target="tpu_custom_call" | custom-call | flops 179999997952 | bytes 1 | tf_op jit(solution)/shard_map/query/pallas_call | solution.py:44
  50.6 13.7 %attend.1 = (bf16[512,2048]{1,0:T(8,128)(2,1)}, bf16[512,2048]{1,0:T(8,128)(2,1)}, f32[2,2,256,8]{3,2,1,0:T(8,128)}) custom-call(f32[512,2048]{1,0:T(8,128)} %query.1.refs_0_, f32[512,128]{1,0:T(8,128)} %get-tuple-element.92.refs_3_.refs_1_.refs_4_, f32[512,128]{1,0:T(8,128)} %get-tuple-element.93.refs_4_.refs_2_.refs_5_, s32[512,1]{1,0:T(8,128)} %bitcast.145, ...), custom_call_target="tpu_custom_call" | custom-call | flops 280000004096 | bytes 1 | tf_op jit(solution)/shard_map/attend/pallas_call | solution.py:44
  64.3 11.5 %project_out.1 = (f32[512,2048]{1,0:T(8,128)}, bf16[512,2048]{1,0:T(8,128)(2,1)}, f32[512,1]{1,0:T(8,128)}) custom-call(bf16[512,2048]{1,0:T(8,128)(2,1)} %get-tuple-element.40.refs_0_.refs_1_, bf16[2048,2048]{1,0:T(8,128)(2,1)} %refs_6_.5, bf16[512,2048]{1,0:T(8,128)(2,1)} %bitcast.154, f32[1,2048]{1,0:T(1,128)} %bitcast.157, ...), custom_call_target="tpu_custom_call" | custom-call | flops 219999993856 | bytes 1 | tf_op jit(solution)/shard_map/project_out/pallas_call | solution.py:44
  75.8 3.3 collective-permute-start.8
  82.5 2.7 collective-permute-done.8.refs_4_
  86.6 20.1 %down_back.1.refs_3_ = bf16[2048,1408]{1,0:T(8,128)(2,1)} custom-call(s32[1]{0:T(128)} %bitcast.5.refs_0_, bf16[512,2048]{1,0:T(8,128)(2,1)} %bitcast.4.refs_1_.refs_4_, bf16[512,2048]{1,0:T(8,128)(2,1)} %collective-permute-done.5.refs_4_.refs_2_, bf16[512,2048]{1,0:T(8,128)(2,1)} %hold.8.refs_3_, bf16[512,2048]{1,0:T(8,128)(2,1)} %copy-done.24, ...), custom_call_target="tpu_custom_call" | custom-call | flops 399999991808 | bytes 1 | tf_op jit(solution)/shard_map/down_back/pallas_call | solution.py:44
  106.7 21.2 %feed.2 = (bf16[1024,1408]{1,0:T(8,128)(2,1)}, bf16[1024,1408]{1,0:T(8,128)(2,1)}, bf16[1024,1408]{1,0:T(8,128)(2,1)}) custom-call(s32[1]{0:T(128)} %bitcast.5.refs_0_, bf16[512,2048]{1,0:T(8,128)(2,1)} %get-tuple-element.42.refs_0_.refs_6_.refs_1_, bf16[512,2048]{1,0:T(8,128)(2,1)} %collective-permute-done.6.refs_2_, bf16[2048,1408]{1,0:T(8,128)(2,1)} %down_back.1.refs_3_, ...), custom_call_target="tpu_custom_call" | custom-call | flops 420000006144 | bytes 1 | tf_op jit(solution)/shard_map/feed/pallas_call | solution.py:44
  129.4 2.9 collective-permute-done.13.refs_2_.refs_4_
  133.7 21.4 %feed.3 = (bf16[1024,1408]{1,0:T(8,128)(2,1)}, bf16[1024,1408]{1,0:T(8,128)(2,1)}, bf16[1024,1408]{1,0:T(8,128)(2,1)}) custom-call(s32[1]{0:T(128)} %bitcast.5.refs_0_, bf16[512,2048]{1,0:T(8,128)(2,1)} %hold.9.refs_1_.refs_3_, bf16[512,2048]{1,0:T(8,128)(2,1)} %copy-done.25, bf16[2048,1408]{1,0:T(8,128)(2,1)} %down_back.1.refs_3_, ...), custom_call_target="tpu_custom_call" | custom-call | flops 420000006144 | bytes 1 | tf_op jit(solution)/shard_map/feed/pallas_call | solution.py:44
  155.1 11.5 %up_send.1.refs_7_ = bf16[4,256,1408]{2,1,0:T(8,128)(2,1)} custom-call(s32[1]{0:T(128)S(6)} %sub.54.refs_0_, bf16[512,2048]{1,0:T(8,128)(2,1)} %get-tuple-element.42.refs_0_.refs_6_.refs_1_, bf16[512,2048]{1,0:T(8,128)(2,1)} %collective-permute-done.6.refs_2_, bf16[512,2048]{1,0:T(8,128)(2,1)} %hold.9.refs_1_.refs_3_, bf16[512,2048]{1,0:T(8,128)(2,1)} %copy-done.25, ...), custom_call_target="tpu_custom_call" | custom-call | flops 219999993856 | bytes 1 | tf_op jit(solution)/shard_map/up_send/pallas_call | solution.py:44
  167.4 19.0 %gate.1.refs_0_ = bf16[8,256,1408]{2,1,0:T(8,128)(2,1)} custom-call(s32[1]{0:T(128)} %constant.98.clone.1.refs_0_, bf16[512,2048]{1,0:T(8,128)(2,1)} %get-tuple-element.42.refs_0_.refs_6_.refs_1_, bf16[512,2048]{1,0:T(8,128)(2,1)} %collective-permute-done.6.refs_2_, bf16[512,2048]{1,0:T(8,128)(2,1)} %hold.9.refs_1_.refs_3_, bf16[512,2048]{1,0:T(8,128)(2,1)} %copy-done.25, ...), custom_call_target="tpu_custom_call" | custom-call | flops 380000010240 | bytes 1 | tf_op jit(solution)/shard_map/gate/pallas_call | solution.py:44
  186.5 21.3 %dn2_away.1.refs_7_ = bf16[2,512,2048]{2,1,0:T(8,128)(2,1)} custom-call(s32[1]{0:T(128)} %bitcast.5.refs_0_, bf16[1024,1408]{1,0:T(8,128)(2,1)} %hold.10.refs_1_, bf16[1024,1408]{1,0:T(8,128)(2,1)} %get-tuple-element.47.refs_6_.refs_2_, bf16[1024,1408]{1,0:T(8,128)(2,1)} %get-tuple-element.44.refs_0_.refs_6_.refs_5_.refs_3_, ...), custom_call_target="tpu_custom_call" | custom-call | flops 399999991808 | bytes 1 | tf_op jit(solution)/shard_map/dn2_away/pallas_call | solution.py:44
  208.7 11.2 %down_send.1.refs_8_ = bf16[1408,1024]{1,0:T(8,128)(2,1)} custom-call(s32[1]{0:T(128)S(6)} %sub.54.refs_0_, bf16[512,2048]{1,0:T(8,128)(2,1)} %bitcast.4.refs_1_.refs_4_, bf16[512,2048]{1,0:T(8,128)(2,1)} %collective-permute-done.5.refs_4_.refs_2_, bf16[512,2048]{1,0:T(8,128)(2,1)} %hold.8.refs_3_, bf16[512,2048]{1,0:T(8,128)(2,1)} %copy-done.24, ...), custom_call_target="tpu_custom_call" | custom-call | flops 219999993856 | bytes 1 | tf_op jit(solution)/shard_map/down_send/pallas_call | solution.py:44
  220.6 21.9 %dn2_near.1 = (bf16[512,2048]{1,0:T(8,128)(2,1)}, bf16[512,2048]{1,0:T(8,128)(2,1)}) custom-call(s32[1]{0:T(128)} %bitcast.5.refs_0_, bf16[1024,1408]{1,0:T(8,128)(2,1)} %hold.10.refs_1_, bf16[1024,1408]{1,0:T(8,128)(2,1)} %get-tuple-element.47.refs_6_.refs_2_, bf16[1024,1408]{1,0:T(8,128)(2,1)} %get-tuple-element.44.refs_0_.refs_6_.refs_5_.refs_3_, ...), custom_call_target="tpu_custom_call" | custom-call | flops 439999987712 | bytes 1 | tf_op jit(solution)/shard_map/dn2_near/pallas_call | solution.py:44
  243.7 11.5 %out_away.1.refs_8_ = bf16[2,512,2048]{2,1,0:T(8,128)(2,1)} custom-call(s32[1]{0:T(128)} %bitcast.5.refs_0_, bf16[1024,1408]{1,0:T(8,128)(2,1)} %get-tuple-element.43.refs_5_.refs_1_, bf16[1024,1408]{1,0:T(8,128)(2,1)} %get-tuple-element.45.refs_6_.refs_2_, bf16[5632,2048]{1,0:T(8,128)(2,1)} %refs_3_.3, bf16[512,2048]{1,0:T(8,128)(2,1)} %get-tuple-element.49.refs_4_), custom_call_target="tpu_custom_call" | custom-call | flops 219999993856 | bytes 1 | tf_op jit(solution)/shard_map/out_away/pallas_call | solution.py:44
  255.8 11.8 %up_keep.1.refs_5_ = bf16[4,256,1408]{2,1,0:T(8,128)(2,1)} custom-call(s32[1]{0:T(128)} %bitcast.6.refs_0_, bf16[512,2048]{1,0:T(8,128)(2,1)} %get-tuple-element.42.refs_0_.refs_6_.refs_1_, bf16[512,2048]{1,0:T(8,128)(2,1)} %collective-permute-done.6.refs_2_, bf16[512,2048]{1,0:T(8,128)(2,1)} %hold.9.refs_1_.refs_3_, bf16[512,2048]{1,0:T(8,128)(2,1)} %copy-done.25, ...), custom_call_target="tpu_custom_call" | custom-call | flops 240000008192 | bytes 1 | tf_op jit(solution)/shard_map/up_keep/pallas_call | solution.py:44
  267.7 13.1 %out_near.1 = (bf16[512,2048]{1,0:T(8,128)(2,1)}, bf16[512,2048]{1,0:T(8,128)(2,1)}) custom-call(s32[1]{0:T(128)} %bitcast.5.refs_0_, bf16[1024,1408]{1,0:T(8,128)(2,1)} %get-tuple-element.43.refs_5_.refs_1_, bf16[1024,1408]{1,0:T(8,128)(2,1)} %get-tuple-element.45.refs_6_.refs_2_, bf16[5632,2048]{1,0:T(8,128)(2,1)} %refs_3_.3, ...), custom_call_target="tpu_custom_call" | custom-call | flops 260000006144 | bytes 1 | tf_op jit(solution)/shard_map/out_near/pallas_call | solution.py:44
  281.0 8.6 %collective-permute-done.22.refs_1_ = bf16[512,2048]{1,0:T(8,128)(2,1)} collective-permute-done((bf16[512,2048]{1,0:T(8,128)(2,1)}, bf16[512,2048]{1,0:T(8,128)(2,1)}, u32[]{:S(2)}, u32[]{:S(2)}) %collective-permute-start.22) | collective-permute-done | bytes 2097184 | tf_op jit(solution)/shard_map/ppermute | solution.py:76
  289.6 14.5 %mid_back.1 = (bf16[512,2048]{1,0:T(8,128)(2,1)}, f32[1,2048]{1,0:T(1,128)}, bf16[512,2048]{1,0:T(8,128)(2,1)}) custom-call(bf16[512,2048]{1,0:T(8,128)(2,1)} %get-tuple-element.53.refs_0_, bf16[512,2048]{1,0:T(8,128)(2,1)} %collective-permute-done.22.refs_1_, f32[512,2048]{1,0:T(8,128)} %get-tuple-element.41.refs_2_.refs_0_, ...), custom_call_target="tpu_custom_call" | custom-call | flops 280000004096 | bytes 1 | tf_op jit(solution)/shard_map/mid_back/pallas_call | solution.py:44
  304.1 2.9 constant_dynamic-slice_fusion.4
  307.0 3.0 collective-permute-start.28
  310.4 22.9 %attend_back.1 = (bf16[512,2048]{1,0:T(8,128)(2,1)}, f32[2,768,128]{2,1,0:T(8,128)}, f32[2,768,128]{2,1,0:T(8,128)}) custom-call(bf16[512,2048]{1,0:T(8,128)(2,1)} %get-tuple-element.52.refs_0_, bf16[512,2048]{1,0:T(8,128)(2,1)} %get-tuple-element.40.refs_0_.refs_1_, bf16[512,2048]{1,0:T(8,128)(2,1)} %get-tuple-element.55.refs_2_, ...), custom_call_target="tpu_custom_call" | custom-call | flops 460000002048 | bytes 1 | tf_op jit(solution)/shard_map/attend_back/pallas_call | solution.py:44
  342.5 11.4 %down_keep.1.refs_3_ = bf16[1408,1024]{1,0:T(8,128)(2,1)} custom-call(s32[1]{0:T(128)} %bitcast.6.refs_0_, bf16[512,2048]{1,0:T(8,128)(2,1)} %bitcast.4.refs_1_.refs_4_, bf16[512,2048]{1,0:T(8,128)(2,1)} %collective-permute-done.5.refs_4_.refs_2_, bf16[512,2048]{1,0:T(8,128)(2,1)} %hold.8.refs_3_, bf16[512,2048]{1,0:T(8,128)(2,1)} %copy-done.24, ...), custom_call_target="tpu_custom_call" | custom-call | flops 240000008192 | bytes 1 | tf_op jit(solution)/shard_map/down_keep/pallas_call | solution.py:44
  355.4 5.2 %output.1.refs_9_.refs_0_ = bf16[512,2048]{1,0:T(8,128)(2,1)} custom-call(f32[512,2048]{1,0:T(8,128)} %get-tuple-element.41.refs_2_.refs_0_, bf16[512,2048]{1,0:T(8,128)(2,1)} %get-tuple-element.50.refs_1_, bf16[512,2048]{1,0:T(8,128)(2,1)} %collective-permute-done.20.refs_2_, bf16[1408,1024]{1,0:T(8,128)(2,1)} %down_keep.1.refs_3_), custom_call_target="tpu_custom_call" | custom-call | flops 99999997952 | bytes 1 | tf_op jit(solution)/shard_map/output/pallas_call | solution.py:44
  369.6 6.9 %w_out_send.1.refs_9_ = bf16[2048,256]{1,0:T(8,128)(2,1)} custom-call(s32[1]{0:T(128)S(6)} %sub.56.refs_0_, bf16[512,2048]{1,0:T(8,128)(2,1)} %get-tuple-element.40.refs_0_.refs_1_, bf16[512,2048]{1,0:T(8,128)(2,1)} %collective-permute-done.14.refs_8_.refs_2_, bf16[512,2048]{1,0:T(8,128)(2,1)} %collective-permute-done.15.refs_9_.refs_3_, ...), custom_call_target="tpu_custom_call" | custom-call | flops 140000002048 | bytes 1 | tf_op jit(solution)/shard_map/w_out_send/pallas_call | solution.py:44
  377.3 6.8 %w_query_send.1.refs_0_.refs_9_ = bf16[2048,256]{1,0:T(8,128)(2,1)} custom-call(s32[1]{0:T(128)S(6)} %sub.56.refs_0_, bf16[512,2048]{1,0:T(8,128)(2,1)} %get-tuple-element.38.refs_0_.refs_1_, bf16[512,2048]{1,0:T(8,128)(2,1)} %collective-permute-done.9.refs_6_.refs_2_, bf16[512,2048]{1,0:T(8,128)(2,1)} %collective-permute-done.10.refs_7_.refs_3_, ...), custom_call_target="tpu_custom_call" | custom-call | flops 140000002048 | bytes 1 | tf_op jit(solution)/shard_map/w_query_send/pallas_call | solution.py:44
  384.8 2.9 collective-permute-done.30.refs_1_
  390.3 13.7 %tokens_back.1 = (f32[512,2048]{1,0:T(8,128)}, f32[1,2048]{1,0:T(1,128)}) custom-call(bf16[512,2048]{1,0:T(8,128)(2,1)} %get-tuple-element.58.refs_8_.refs_0_, bf16[512,256]{1,0:T(8,128)(2,1)} %pad_maximum_fusion.4.refs_1_, bf16[2048,2048]{1,0:T(8,128)(2,1)} %refs_2_.1, bf16[2048,256]{1,0:T(8,128)(2,1)} %copy-done.17, ...), custom_call_target="tpu_custom_call" | custom-call | flops 280000004096 | bytes 1 | tf_op jit(solution)/shard_map/tokens_back/pallas_call | solution.py:44
  404.8 2.3 convolution_convert_fusion
  409.6 6.1 %all-to-all-start = ((bf16[8,4,64,384]{3,2,1,0:T(8,128)(2,1)}), bf16[8,4,64,384]{3,2,1,0:T(8,128)(2,1)}, u32[]{:S(2)}, u32[]{:S(2)}) async-start(bf16[8,4,64,384]{3,2,1,0:T(8,128)(2,1)} %bitcast.128), calls=%async_computation.3 | async-start | bytes 3145728 | tf_op jit(solution)/shard_map/all_to_all | solution.py:829
  415.8 2.0 dynamic-slice_bitcast_fusion.2
  417.8 4.7 collective-permute-start.34
  422.7 7.2 %w_out_keep.1.refs_10_.refs_0_ = bf16[2048,256]{1,0:T(8,128)(2,1)} custom-call(s32[1]{0:T(128)} %bitcast.9.refs_0_, bf16[512,2048]{1,0:T(8,128)(2,1)} %get-tuple-element.40.refs_0_.refs_1_, bf16[512,2048]{1,0:T(8,128)(2,1)} %collective-permute-done.14.refs_8_.refs_2_, bf16[512,2048]{1,0:T(8,128)(2,1)} %collective-permute-done.15.refs_9_.refs_3_, ...), custom_call_target="tpu_custom_call" | custom-call | flops 140000002048 | bytes 1 | tf_op jit(solution)/shard_map/w_out_keep/pallas_call | solution.py:44
  429.9 7.2 %w_query_keep.1.refs_0_ = bf16[2048,256]{1,0:T(8,128)(2,1)} custom-call(s32[1]{0:T(128)} %bitcast.9.refs_0_, bf16[512,2048]{1,0:T(8,128)(2,1)} %get-tuple-element.38.refs_0_.refs_1_, bf16[512,2048]{1,0:T(8,128)(2,1)} %collective-permute-done.9.refs_6_.refs_2_, bf16[512,2048]{1,0:T(8,128)(2,1)} %collective-permute-done.10.refs_7_.refs_3_, ...), custom_call_target="tpu_custom_call" | custom-call | flops 140000002048 | bytes 1 | tf_op jit(solution)/shard_map/w_query_keep/pallas_call | solution.py:44
  441.2 13.1 %all-to-all-done.refs_1_ = bf16[8,4,64,384]{3,2,1,0:T(8,128)(2,1)} async-done(((bf16[8,4,64,384]{3,2,1,0:T(8,128)(2,1)}), bf16[8,4,64,384]{3,2,1,0:T(8,128)(2,1)}, u32[]{:S(2)}, u32[]{:S(2)}) %all-to-all-start) | async-done | bytes 1572896 | tf_op jit(solution)/shard_map/all_to_all | solution.py:829
  454.2 5.8 %all-to-all-start.3 = ((bf16[4,2,64,1408]{3,2,1,0:T(8,128)(2,1)}), bf16[4,2,64,1408]{3,2,1,0:T(8,128)(2,1)}, u32[]{:S(2)}, u32[]{:S(2)}) async-start(bf16[4,2,64,1408]{3,2,1,0:T(8,128)(2,1)} %maximum_bitcast_fusion), calls=%async_computation.8 | async-start | bytes 2883584 | tf_op jit(solution)/shard_map/all_to_all | solution.py:888
  463.0 8.5 %collective-permute-done.35 = bf16[176,1024]{1,0:T(8,128)(2,1)} collective-permute-done((bf16[176,1024]{1,0:T(8,128)(2,1)}, bf16[176,1024]{1,0:T(8,128)(2,1)}, u32[]{:S(2)}, u32[]{:S(2)}) %collective-permute-start.35) | collective-permute-done | bytes 360480 | tf_op jit(solution)/shard_map/ppermute | solution.py:863
  474.0 3.4 all-to-all-done.3
  479.0 5.8 %all-to-all-start.2 = ((bf16[8,64,256]{2,1,0:T(8,128)(2,1)}), bf16[8,64,256]{2,1,0:T(8,128)(2,1)S(1)}, u32[]{:S(2)}, u32[]{:S(2)}) async-start(bf16[8,64,256]{2,1,0:T(8,128)(2,1)} %bitcast.147), calls=%async_computation.7 | async-start | bytes 524288 | tf_op jit(solution)/shard_map/all_to_all | solution.py:849
  490.2 8.0 %reduce-scatter.12.cloned.1.call-done = bf16[1,640,256]{2,1,0:T(8,128)(2,1)} async-done(((bf16[4,640,256]{2,1,0:T(8,128)(2,1)}), bf16[1,640,256]{2,1,0:T(8,128)(2,1)}) %reduce-scatter.12.cloned.1.call-update) | async-done | bytes 327696 | tf_op jit(solution)/shard_map/reduce_scatter | solution.py:843
  500.6 4.7 all-to-all-start.1
  507.4 2.4 all-to-all-done.1
  (213 shorter events, 73.8 us)
Async XLA Ops:
  7.2 335.3 %reduce-scatter.6.cloned.1.call-start = ((), (), s32[]{:S(2)}) async-start(), calls=%async_computation.9 | async-start | bytes 7208960 | tf_op jit(solution)/shard_map/reduce_scatter | solution.py:765
  7.9 11.1 %collective-permute-start.2 = (s32[2,256]{1,0:T(2,128)S(1)}, s32[2,256]{1,0:T(2,128)S(1)}, u32[]{:S(2)}, u32[]{:S(2)}) collective-permute-start(s32[2,256]{1,0:T(2,128)S(1)} %broadcast_add_fusion), channel_id=1, source_target_pairs={{0,24},{1,25},{2,26},{3,27},{4,28},{5,29},{6,30},{7,31}} | collective-permute-start | bytes 6152 | tf_op jit(solution)/shard_map/ppermute | solution.py:88
  13.2 5.9 %collective-permute-start.1 = (s32[2,256]{1,0:T(2,128)S(1)}, s32[2,256]{1,0:T(2,128)S(1)}, u32[]{:S(2)}, u32[]{:S(2)}) collective-permute-start(s32[2,256]{1,0:T(2,128)S(1)} %broadcast_add_fusion), channel_id=1, source_target_pairs={{0,16},{1,17},{2,18},{3,19},{4,20},{5,21},{6,22},{7,23},{8,24},{9,... | collective-permute-start | bytes 6152 | tf_op jit(solution)/shard_map/ppermute | solution.py:88
  14.5 4.6 collective-permute-start
  27.7 6.7 %collective-permute-start.3 = (bf16[2,256,256]{2,1,0:T(8,128)(2,1)}, bf16[2,256,256]{2,1,0:T(8,128)(2,1)}, u32[]{:S(2)}, u32[]{:S(2)}) collective-permute-start(bf16[2,256,256]{2,1,0:T(8,128)(2,1)} %bitcast.148), channel_id=1, source_target_pairs={{0,8},{1,9},{2,10},{3,11},{4,12},{5,13},{6,14},{7,15},{8,16},{9,17... | collective-permute-start | bytes 786440 | tf_op jit(solution)/shard_map/ppermute | solution.py:88
  30.3 45.5 %collective-permute-start.7 = (bf16[512,2048]{1,0:T(8,128)(2,1)}, bf16[512,2048]{1,0:T(8,128)(2,1)}, u32[]{:S(2)}, u32[]{:S(2)}) collective-permute-start(bf16[512,2048]{1,0:T(8,128)(2,1)} %bitcast.4.refs_1_.refs_4_), channel_id=1, source_target_pairs={{0,2},{1,3},{2,0},{3,1},{4,6},{5,7},{6,4},{7,5},{8,10},{9,11},{10,... | collective-permute-start | bytes 6291464 | tf_op jit(solution)/shard_map/ppermute | solution.py:76
  31.5 32.8 %collective-permute-start.5 = (bf16[512,2048]{1,0:T(8,128)(2,1)}, bf16[512,2048]{1,0:T(8,128)(2,1)}, u32[]{:S(2)}, u32[]{:S(2)}) collective-permute-start(bf16[512,2048]{1,0:T(8,128)(2,1)} %bitcast.4.refs_1_.refs_4_), channel_id=1, source_target_pairs={{0,1},{1,0},{2,3},{3,2},{4,5},{5,4},{6,7},{7,6},{8,9},{9,8},{10,11... | collective-permute-start | bytes 6291464 | tf_op jit(solution)/shard_map/ppermute | solution.py:76
  34.2 47.6 %collective-permute-start.10 = (bf16[512,2048]{1,0:T(8,128)(2,1)}, bf16[512,2048]{1,0:T(8,128)(2,1)}, u32[]{:S(2)}, u32[]{:S(2)}) collective-permute-start(bf16[512,2048]{1,0:T(8,128)(2,1)} %get-tuple-element.38.refs_0_.refs_1_), channel_id=1, source_target_pairs={{0,4},{1,5},{2,6},{3,7},{4,0},{5,1},{6,2},{7,3},{8,12},{9,13},{10,... | collective-permute-start | bytes 6291464 | tf_op jit(solution)/shard_map/ppermute | solution.py:76
  34.4 14.0 %collective-permute-start.4 = (bf16[2,256,256]{2,1,0:T(8,128)(2,1)}, bf16[2,256,256]{2,1,0:T(8,128)(2,1)}, u32[]{:S(2)}, u32[]{:S(2)}) collective-permute-start(bf16[2,256,256]{2,1,0:T(8,128)(2,1)} %collective-permute-done.3), channel_id=1, source_target_pairs={{0,8},{1,9},{2,10},{3,11},{4,12},{5,13},{6,14},{7,15},{8,16},{9,17... | collective-permute-start | bytes 786440 | tf_op jit(solution)/shard_map/ppermute | solution.py:88
  75.8 9.4 %collective-permute-start.8 = (bf16[512,2048]{1,0:T(8,128)(2,1)}, bf16[512,2048]{1,0:T(8,128)(2,1)S(1)}, u32[]{:S(2)}, u32[]{:S(2)}) collective-permute-start(bf16[512,2048]{1,0:T(8,128)(2,1)} %hold.8.refs_3_), channel_id=1, source_target_pairs={{0,1},{1,0},{2,3},{3,2},{4,5},{5,4},{6,7},{7,6},{8,9},{9,8},{10,11... | collective-permute-start | bytes 6291464 | tf_op jit(solution)/shard_map/ppermute | solution.py:76
  79.2 27.5 %collective-permute-start.9 = (bf16[512,2048]{1,0:T(8,128)(2,1)}, bf16[512,2048]{1,0:T(8,128)(2,1)}, u32[]{:S(2)}, u32[]{:S(2)}) collective-permute-start(bf16[512,2048]{1,0:T(8,128)(2,1)} %get-tuple-element.38.refs_0_.refs_1_), channel_id=1, source_target_pairs={{0,1},{1,0},{2,3},{3,2},{4,5},{5,4},{6,7},{7,6},{8,9},{9,8},{10,11... | collective-permute-start | bytes 6291464 | tf_op jit(solution)/shard_map/ppermute | solution.py:76
  79.2 49.8 %collective-permute-start.15 = (bf16[512,2048]{1,0:T(8,128)(2,1)}, bf16[512,2048]{1,0:T(8,128)(2,1)}, u32[]{:S(2)}, u32[]{:S(2)}) collective-permute-start(bf16[512,2048]{1,0:T(8,128)(2,1)} %get-tuple-element.40.refs_0_.refs_1_), channel_id=1, source_target_pairs={{0,4},{1,5},{2,6},{3,7},{4,0},{5,1},{6,2},{7,3},{8,12},{9,13},{10,... | collective-permute-start | bytes 6291464 | tf_op jit(solution)/shard_map/ppermute | solution.py:76
  79.5 48.4 %collective-permute-start.12 = (bf16[512,2048]{1,0:T(8,128)(2,1)}, bf16[512,2048]{1,0:T(8,128)(2,1)}, u32[]{:S(2)}, u32[]{:S(2)}) collective-permute-start(bf16[512,2048]{1,0:T(8,128)(2,1)} %get-tuple-element.42.refs_0_.refs_6_.refs_1_), channel_id=1, source_target_pairs={{0,2},{1,3},{2,0},{3,1},{4,6},{5,7},{6,4},{7,5},{8,10},{9,11},{10,... | collective-permute-start | bytes 6291464 | tf_op jit(solution)/shard_map/ppermute | solution.py:76
  81.8 24.9 %collective-permute-start.6 = (bf16[512,2048]{1,0:T(8,128)(2,1)}, bf16[512,2048]{1,0:T(8,128)(2,1)}, u32[]{:S(2)}, u32[]{:S(2)}) collective-permute-start(bf16[512,2048]{1,0:T(8,128)(2,1)} %get-tuple-element.42.refs_0_.refs_6_.refs_1_), channel_id=1, source_target_pairs={{0,1},{1,0},{2,3},{3,2},{4,5},{5,4},{6,7},{7,6},{8,9},{9,8},{10,11... | collective-permute-start | bytes 6291464 | tf_op jit(solution)/shard_map/ppermute | solution.py:76
  85.2 21.4 %collective-permute-start.11 = (bf16[512,2048]{1,0:T(8,128)(2,1)}, bf16[512,2048]{1,0:T(8,128)(2,1)}, u32[]{:S(2)}, u32[]{:S(2)}) collective-permute-start(bf16[512,2048]{1,0:T(8,128)(2,1)} %collective-permute-done.10.refs_7_.refs_3_), channel_id=1, source_target_pairs={{0,1},{1,0},{2,3},{3,2},{4,5},{5,4},{6,7},{7,6},{8,9},{9,8},{10,11... | collective-permute-start | bytes 6291464 | tf_op jit(solution)/shard_map/ppermute | solution.py:76
  127.9 4.4 collective-permute-start.13
  128.9 26.2 %collective-permute-start.14 = (bf16[512,2048]{1,0:T(8,128)(2,1)}, bf16[512,2048]{1,0:T(8,128)(2,1)}, u32[]{:S(2)}, u32[]{:S(2)}) collective-permute-start(bf16[512,2048]{1,0:T(8,128)(2,1)} %get-tuple-element.40.refs_0_.refs_1_), channel_id=1, source_target_pairs={{0,1},{1,0},{2,3},{3,2},{4,5},{5,4},{6,7},{7,6},{8,9},{9,8},{10,11... | collective-permute-start | bytes 6291464 | tf_op jit(solution)/shard_map/ppermute | solution.py:76
  129.0 26.1 %collective-permute-start.16 = (bf16[512,2048]{1,0:T(8,128)(2,1)}, bf16[512,2048]{1,0:T(8,128)(2,1)}, u32[]{:S(2)}, u32[]{:S(2)}) collective-permute-start(bf16[512,2048]{1,0:T(8,128)(2,1)} %collective-permute-done.15.refs_9_.refs_3_), channel_id=1, source_target_pairs={{0,1},{1,0},{2,3},{3,2},{4,5},{5,4},{6,7},{7,6},{8,9},{9,8},{10,11... | collective-permute-start | bytes 6291464 | tf_op jit(solution)/shard_map/ppermute | solution.py:76
  166.6 89.2 %collective-permute-start.19 = (bf16[4,256,1408]{2,1,0:T(8,128)(2,1)}, bf16[4,256,1408]{2,1,0:T(8,128)(2,1)}, u32[]{:S(2)}, u32[]{:S(2)}) collective-permute-start(bf16[4,256,1408]{2,1,0:T(8,128)(2,1)} %up_send.1.refs_7_), channel_id=1, source_target_pairs={{0,4},{1,5},{2,6},{3,7},{4,0},{5,1},{6,2},{7,3},{8,12},{9,13},{10,... | collective-permute-start | bytes 8650760 | tf_op jit(solution)/shard_map/ppermute | solution.py:76
  186.4 182.2 %reduce-scatter.8.cloned.1.call-start = ((), (), s32[]{:S(2)}) async-start(), calls=%async_computation.10 | async-start | bytes 3604480 | tf_op jit(solution)/shard_map/reduce_scatter | solution.py:746
  207.8 12.9 %collective-permute-start.17 = (bf16[2,512,2048]{2,1,0:T(8,128)(2,1)}, bf16[2,512,2048]{2,1,0:T(8,128)(2,1)}, u32[]{:S(2)}, u32[]{:S(2)}) collective-permute-start(bf16[2,512,2048]{2,1,0:T(8,128)(2,1)} %dn2_away.1.refs_7_), channel_id=1, source_target_pairs={{0,1},{1,0},{2,3},{3,2},{4,5},{5,4},{6,7},{7,6},{8,9},{9,8},{10,11... | collective-permute-start | bytes 12582920 | tf_op jit(solution)/shard_map/ppermute | solution.py:76
  219.9 119.6 %collective-permute-start.21 = (bf16[1408,1024]{1,0:T(8,128)(2,1)}, bf16[1408,1024]{1,0:T(8,128)(2,1)}, u32[]{:S(2)}, u32[]{:S(2)}) collective-permute-start(bf16[1408,1024]{1,0:T(8,128)(2,1)} %down_send.1.refs_8_), channel_id=1, source_target_pairs={{0,4},{1,5},{2,6},{3,7},{4,0},{5,1},{6,2},{7,3},{8,12},{9,13},{10,... | collective-permute-start | bytes 8650760 | tf_op jit(solution)/shard_map/ppermute | solution.py:76
  242.5 47.1 %collective-permute-start.22 = (bf16[512,2048]{1,0:T(8,128)(2,1)}, bf16[512,2048]{1,0:T(8,128)(2,1)}, u32[]{:S(2)}, u32[]{:S(2)}) collective-permute-start(bf16[512,2048]{1,0:T(8,128)(2,1)} %get-tuple-element.49.refs_4_), channel_id=1, source_target_pairs={{0,2},{1,3},{2,0},{3,1},{4,6},{5,7},{6,4},{7,5},{8,10},{9,11},{10,... | collective-permute-start | bytes 6291464 | tf_op jit(solution)/shard_map/ppermute | solution.py:76
  255.2 12.5 %collective-permute-start.18 = (bf16[2,512,2048]{2,1,0:T(8,128)(2,1)}, bf16[2,512,2048]{2,1,0:T(8,128)(2,1)}, u32[]{:S(2)}, u32[]{:S(2)}) collective-permute-start(bf16[2,512,2048]{2,1,0:T(8,128)(2,1)} %out_away.1.refs_8_), channel_id=1, source_target_pairs={{0,1},{1,0},{2,3},{3,2},{4,5},{5,4},{6,7},{7,6},{8,9},{9,8},{10,11... | collective-permute-start | bytes 12582920 | tf_op jit(solution)/shard_map/ppermute | solution.py:76
  267.7 148.1 %reduce-scatter.10.cloned.1.call-start = ((), (), s32[]{:S(2)}) async-start(), calls=%async_computation.11 | async-start | bytes 3604480 | tf_op jit(solution)/shard_map/reduce_scatter | solution.py:796
  280.8 73.1 %collective-permute-start.20 = (bf16[512,2048]{1,0:T(8,128)(2,1)}, bf16[512,2048]{1,0:T(8,128)(2,1)}, u32[]{:S(2)}, u32[]{:S(2)}) collective-permute-start(bf16[512,2048]{1,0:T(8,128)(2,1)} %get-tuple-element.51.refs_7_), channel_id=1, source_target_pairs={{0,2},{1,3},{2,0},{3,1},{4,6},{5,7},{6,4},{7,5},{8,10},{9,11},{10,... | collective-permute-start | bytes 6291464 | tf_op jit(solution)/shard_map/ppermute | solution.py:76
  307.0 57.9 %collective-permute-start.28 = (bf16[512,512]{1,0:T(8,128)(2,1)}, bf16[512,512]{1,0:T(8,128)(2,1)}, u32[]{:S(2)}, u32[]{:S(2)}) collective-permute-start(bf16[512,512]{1,0:T(8,128)(2,1)} %get-tuple-element.73.refs_12_), channel_id=1, source_target_pairs={{0,5},{1,4},{2,7},{3,6},{4,1},{5,0},{6,3},{7,2},{8,13},{9,12},{10,... | collective-permute-start | bytes 1572872 | tf_op jit(solution)/shard_map/ppermute | solution.py:76
  310.0 56.1 %collective-permute-start.27 = (bf16[512,512]{1,0:T(8,128)(2,1)}, bf16[512,512]{1,0:T(8,128)(2,1)}, u32[]{:S(2)}, u32[]{:S(2)}) collective-permute-start(bf16[512,512]{1,0:T(8,128)(2,1)} %get-tuple-element.74.refs_11_), channel_id=1, source_target_pairs={{0,4},{1,5},{2,6},{3,7},{4,0},{5,1},{6,2},{7,3},{8,12},{9,13},{10,... | collective-permute-start | bytes 1572872 | tf_op jit(solution)/shard_map/ppermute | solution.py:76
  310.4 30.6 %collective-permute-start.23 = (bf16[512,512]{1,0:T(8,128)(2,1)}, bf16[512,512]{1,0:T(8,128)(2,1)}, u32[]{:S(2)}, u32[]{:S(2)}) collective-permute-start(bf16[512,512]{1,0:T(8,128)(2,1)} %get-tuple-element.75.refs_10_), channel_id=1, source_target_pairs={{0,1},{1,0},{2,3},{3,2},{4,5},{5,4},{6,7},{7,6},{8,9},{9,8},{10,11... | collective-permute-start | bytes 1572872 | tf_op jit(solution)/shard_map/ppermute | solution.py:76
  310.4 22.9 %copy-start.20 = (f32[1,2048]{1,0:T(1,128)S(1)}, f32[1,2048]{1,0:T(1,128)}, u32[]{:S(2)}) copy-start(f32[1,2048]{1,0:T(1,128)} %get-tuple-element.64) | copy-start | bytes 24580
  339.5 21.1 %collective-permute-start.29 = (bf16[2,256,256]{2,1,0:T(8,128)(2,1)}, bf16[2,256,256]{2,1,0:T(8,128)(2,1)}, u32[]{:S(2)}, u32[]{:S(2)}) collective-permute-start(bf16[2,256,256]{2,1,0:T(8,128)(2,1)} %slice.154), channel_id=1, source_target_pairs={{8,0},{9,1},{10,2},{11,3},{12,4},{13,5},{14,6},{15,7},{16,8},{17,9... | collective-permute-start | bytes 786440 | tf_op jit(solution)/shard_map/ppermute | solution.py:88
  341.0 26.6 %collective-permute-start.26 = (bf16[512,512]{1,0:T(8,128)(2,1)}, bf16[512,512]{1,0:T(8,128)(2,1)}, u32[]{:S(2)}, u32[]{:S(2)}) collective-permute-start(bf16[512,512]{1,0:T(8,128)(2,1)} %get-tuple-element.69), channel_id=1, source_target_pairs={{0,5},{1,4},{2,7},{3,6},{4,1},{5,0},{6,3},{7,2},{8,13},{9,12},{10,... | collective-permute-start | bytes 1572872 | tf_op jit(solution)/shard_map/ppermute | solution.py:76
  354.9 13.7 %collective-permute-start.25 = (bf16[512,512]{1,0:T(8,128)(2,1)S(1)}, bf16[512,512]{1,0:T(8,128)(2,1)S(1)}, u32[]{:S(2)}, u32[]{:S(2)}) collective-permute-start(bf16[512,512]{1,0:T(8,128)(2,1)S(1)} %copy-done.16), channel_id=1, source_target_pairs={{0,4},{1,5},{2,6},{3,7},{4,0},{5,1},{6,2},{7,3},{8,12},{9,13},{10,... | collective-permute-start | bytes 1572872 | tf_op jit(solution)/shard_map/ppermute | solution.py:76
  361.7 6.9 %collective-permute-start.24 = (bf16[512,512]{1,0:T(8,128)(2,1)S(1)}, bf16[512,512]{1,0:T(8,128)(2,1)S(1)}, u32[]{:S(2)}, u32[]{:S(2)}) collective-permute-start(bf16[512,512]{1,0:T(8,128)(2,1)S(1)} %copy-done.15), channel_id=1, source_target_pairs={{0,1},{1,0},{2,3},{3,2},{4,5},{5,4},{6,7},{7,6},{8,9},{9,8},{10,11... | collective-permute-start | bytes 1572872 | tf_op jit(solution)/shard_map/ppermute | solution.py:76
  364.8 22.8 %collective-permute-start.30 = (bf16[2,256,256]{2,1,0:T(8,128)(2,1)}, bf16[2,256,256]{2,1,0:T(8,128)(2,1)}, u32[]{:S(2)}, u32[]{:S(2)}) collective-permute-start(bf16[2,256,256]{2,1,0:T(8,128)(2,1)} %add_convert_fusion), channel_id=1, source_target_pairs={{8,0},{9,1},{10,2},{11,3},{12,4},{13,5},{14,6},{15,7},{16,8},{17,9... | collective-permute-start | bytes 786440 | tf_op jit(solution)/shard_map/ppermute | solution.py:88
  366.1 71.0 %collective-permute-start.33 = (bf16[256,1408]{1,0:T(8,128)(2,1)}, bf16[256,1408]{1,0:T(8,128)(2,1)}, u32[]{:S(2)}, u32[]{:S(2)}) collective-permute-start(bf16[256,1408]{1,0:T(8,128)(2,1)} %dynamic-slice_bitcast_fusion), channel_id=1, source_target_pairs={{0,4},{1,5},{2,6},{3,7},{4,0},{5,1},{6,2},{7,3},{8,12},{9,13},{10,... | collective-permute-start | bytes 2162696 | tf_op jit(solution)/shard_map/ppermute | solution.py:76
  376.4 46.3 %collective-permute-start.32 = (bf16[2048,256]{1,0:T(8,128)(2,1)}, bf16[2048,256]{1,0:T(8,128)(2,1)}, u32[]{:S(2)}, u32[]{:S(2)}) collective-permute-start(bf16[2048,256]{1,0:T(8,128)(2,1)} %w_out_send.1.refs_9_), channel_id=1, source_target_pairs={{0,2},{1,3},{2,0},{3,1},{4,6},{5,7},{6,4},{7,5},{8,10},{9,11},{10,... | collective-permute-start | bytes 3145736 | tf_op jit(solution)/shard_map/ppermute | solution.py:76
  384.1 45.8 %collective-permute-start.31 = (bf16[2048,256]{1,0:T(8,128)(2,1)}, bf16[2048,256]{1,0:T(8,128)(2,1)}, u32[]{:S(2)}, u32[]{:S(2)}) collective-permute-start(bf16[2048,256]{1,0:T(8,128)(2,1)} %w_query_send.1.refs_0_.refs_9_), channel_id=1, source_target_pairs={{0,2},{1,3},{2,0},{3,1},{4,6},{5,7},{6,4},{7,5},{8,10},{9,11},{10,... | collective-permute-start | bytes 3145736 | tf_op jit(solution)/shard_map/ppermute | solution.py:76
  390.3 14.4 %copy-start.12 = (bf16[512,128]{1,0:T(8,128)(2,1)S(1)}, bf16[512,128]{1,0:T(8,128)(2,1)}, u32[]{:S(2)}) copy-start(bf16[512,128]{1,0:T(8,128)(2,1)} %copy-done.11) | copy-start | bytes 393220
  390.3 14.4 %copy-start.14 = (bf16[512,128]{1,0:T(8,128)(2,1)S(1)}, bf16[512,128]{1,0:T(8,128)(2,1)}, u32[]{:S(2)}) copy-start(bf16[512,128]{1,0:T(8,128)(2,1)} %copy-done.13) | copy-start | bytes 393220
  409.6 44.6 %all-to-all-start = ((bf16[8,4,64,384]{3,2,1,0:T(8,128)(2,1)}), bf16[8,4,64,384]{3,2,1,0:T(8,128)(2,1)}, u32[]{:S(2)}, u32[]{:S(2)}) async-start(bf16[8,4,64,384]{3,2,1,0:T(8,128)(2,1)} %bitcast.128), calls=%async_computation.3 | async-start | bytes 3145728 | tf_op jit(solution)/shard_map/all_to_all | solution.py:829
  415.8 63.2 %reduce-scatter.14.cloned.1.call-start = ((), (), s32[]{:S(2)}) async-start(), calls=%async_computation.13 | async-start | bytes 1310720 | tf_op jit(solution)/shard_map/reduce_scatter | solution.py:831
  417.8 45.2 %collective-permute-start.34 = (bf16[176,1024]{1,0:T(8,128)(2,1)}, bf16[176,1024]{1,0:T(8,128)(2,1)}, u32[]{:S(2)}, u32[]{:S(2)}) collective-permute-start(bf16[176,1024]{1,0:T(8,128)(2,1)} %get-tuple-element.81), channel_id=1, source_target_pairs={{0,0},{1,8},{2,16},{3,24},{4,1},{5,9},{6,17},{7,25},{8,2},{9,10},{... | collective-permute-start | bytes 1081352 | tf_op jit(solution)/shard_map/ppermute | solution.py:863
  422.5 49.0 %collective-permute-start.35 = (bf16[176,1024]{1,0:T(8,128)(2,1)}, bf16[176,1024]{1,0:T(8,128)(2,1)}, u32[]{:S(2)}, u32[]{:S(2)}) collective-permute-start(bf16[176,1024]{1,0:T(8,128)(2,1)} %get-tuple-element.82), channel_id=1, source_target_pairs={{0,1},{1,9},{2,17},{3,25},{4,0},{5,8},{6,16},{7,24},{8,3},{9,11},{... | collective-permute-start | bytes 1081352 | tf_op jit(solution)/shard_map/ppermute | solution.py:863
  454.2 23.1 %all-to-all-start.3 = ((bf16[4,2,64,1408]{3,2,1,0:T(8,128)(2,1)}), bf16[4,2,64,1408]{3,2,1,0:T(8,128)(2,1)}, u32[]{:S(2)}, u32[]{:S(2)}) async-start(bf16[4,2,64,1408]{3,2,1,0:T(8,128)(2,1)} %maximum_bitcast_fusion), calls=%async_computation.8 | async-start | bytes 2883584 | tf_op jit(solution)/shard_map/all_to_all | solution.py:888
  460.1 38.2 %reduce-scatter.12.cloned.1.call-start = ((), (), s32[]{:S(2)}) async-start(), calls=%async_computation.12 | async-start | bytes 1638400 | tf_op jit(solution)/shard_map/reduce_scatter | solution.py:843
  479.0 10.3 %all-to-all-start.2 = ((bf16[8,64,256]{2,1,0:T(8,128)(2,1)}), bf16[8,64,256]{2,1,0:T(8,128)(2,1)S(1)}, u32[]{:S(2)}, u32[]{:S(2)}) async-start(bf16[8,64,256]{2,1,0:T(8,128)(2,1)} %bitcast.147), calls=%async_computation.7 | async-start | bytes 524288 | tf_op jit(solution)/shard_map/all_to_all | solution.py:849
  500.6 9.2 %all-to-all-start.1 = ((bf16[8,64,256]{2,1,0:T(8,128)(2,1)}), bf16[8,64,256]{2,1,0:T(8,128)(2,1)S(1)}, u32[]{:S(2)}, u32[]{:S(2)}) async-start(bf16[8,64,256]{2,1,0:T(8,128)(2,1)} %bitcast.18), calls=%async_computation.5 | async-start | bytes 524288 | tf_op jit(solution)/shard_map/all_to_all | solution.py:849
  (25 other events, 64.8 us)
Sparse Core Ops, SparseCore 0:
  186.5 100.4 reduce-scatter.5
  289.3 58.4 reduce-scatter.7
  354.0 61.0 reduce-scatter.9
  430.0 34.1 reduce-scatter.13
  466.5 31.7 reduce-scatter.11

commit v3 on v2

--- a/solution.py
+++ b/solution.py
@@ -27,7 +27,7 @@
 COST = dict(
     norm_keys=5, query=9, attend=14, project_out=11, down_back=20, feed=21, gate=19, gate_send=11, up_send=11, down_send=11,
     gate_keep=12, up_keep=12, down_keep=12, dn2_away=20, dn2_near=22, out_away=11, out_near=13, mid_back=14,
-    attend_back=23, w_out_send=7, w_out_keep=7, w_query_send=7, w_query_keep=7, tokens_back=14, output=5, hold=1,
+    attend_back=23, w_out_send=7, w_out_keep=7, w_query_send=7, w_query_keep=7, tokens_back=14, output=5, hold=1, join=1,
 )
 
 
@@ -53,7 +53,7 @@
         out_shape=shapes + [jax.ShapeDtypeStruct(p.shape, p.dtype) for p in passes],
         input_output_aliases={n_s + n_a + n_d + i: n_o + i for i in range(n_p)},
         compiler_params=pltpu.CompilerParams(vmem_limit_bytes=vmem * MIB),
-        cost_estimate=pl.CostEstimate(flops=int(SCALE * COST[name] * 10**9), bytes_accessed=1, transcendentals=0),
+        cost_estimate=pl.CostEstimate(flops=int(SCALE * COST.get(name, 1) * 10**9), bytes_accessed=1, transcendentals=0),
         name=name,
     )(*scalars, *args, *deps, *passes)
     return out if several or passes else out[0]
@@ -141,13 +141,12 @@
                 lse_ref[0, 0, sl, h : h + 1] = lse[at]
 
 
-def bwd_kernel(q_ref, o_ref, do_ref, lse_ref, cos_ref, sin_ref, start_ref, k_ref, v_ref, dq_ref, dk_ref, dv_ref, *, hop):
+def bwd_kernel(q_ref, o_ref, do_ref, lse_ref, cos_ref, sin_ref, start_ref, k_ref, v_ref, dq_ref, dkv_ref, *, hop):
     scale = 1.0 / math.sqrt(128)
 
     @pl.when(pl.program_id(1) == 0)
     def _():
-        dk_ref[...] = jnp.zeros_like(dk_ref)
-        dv_ref[...] = jnp.zeros_like(dv_ref)
+        dkv_ref[...] = jnp.zeros_like(dkv_ref)
 
     for sl, r, first, count in row_blocks(q_ref.shape[0], ROWS, hop):
         ks = pl.ds(first, count)
@@ -170,8 +169,8 @@
             dk_part, dv_part = dot(ds, q, 0, 0), dot(p.astype(bf16), do, 0, 0)
             dk = dk_part if dk is None else dk + dk_part
             dv = dv_part if dv is None else dv + dv_part
-        dk_ref[0, ks, :] += dk * (1.0 / math.log2(math.e))
-        dv_ref[0, ks, :] += dv
+        dkv_ref[0, ks, :128] += dk * (1.0 / math.log2(math.e))
+        dkv_ref[0, ks, 128:] += dv
 
 
 HEADS = 8
@@ -183,24 +182,24 @@
     wide = pl.BlockSpec((L, HEADS * 128), lambda s, h: (s, h))
     table = pl.BlockSpec((L, 128), lambda s, h: (s, 0))
     starts = pl.BlockSpec((L, 1), lambda s, h: (s, 0))
-    keys = pl.BlockSpec((1, span, 128), lambda s, h: (s, 0, 0))
+    keys = pl.BlockSpec((1, span, 128), lambda s, h: (s, 0, 0)), pl.BlockSpec((1, span, 128), lambda s, h: (s, 0, 1))
     lse = pl.BlockSpec((1, 1, L, HEADS), lambda s, h: (s, h, 0, 0))
     return wide, table, starts, keys, lse
 
 
-def attention(q_lin, cosine, sine, starts, keys, values, hop, deps=()):
+def attention(q_lin, cosine, sine, starts, kv, hop, deps=()):
     T, width = q_lin.shape
-    groups, span, _ = keys.shape
+    groups, span, _ = kv.shape
     L = T // groups
     wide, table, start, key, lse = attention_specs(L, span)
     steps = width // (HEADS * 128)
     return call(
         functools.partial(fwd_kernel, hop=hop),
         "attend",
-        (q_lin, cosine, sine, starts, keys, values),
+        (q_lin, cosine, sine, starts, kv, kv),
         deps,
         grid=(groups, steps),
-        in_specs=[wide, table, table, start, key, key],
+        in_specs=[wide, table, table, start, *key],
         out_specs=[wide, wide, lse],
         out_shape=[
             jax.ShapeDtypeStruct((T, width), bf16),
@@ -210,24 +209,23 @@
     )
 
 
-def attention_back(queries, attended, d_attended, lses, cosine, sine, starts, keys, values, hop, deps=()):
+def attention_back(queries, attended, d_attended, lses, cosine, sine, starts, kv, hop, deps=()):
     T, width = queries.shape
-    groups, span, _ = keys.shape
+    groups, span, _ = kv.shape
     L = T // groups
     wide, table, start, key, lse = attention_specs(L, span)
     steps = width // (HEADS * 128)
     return call(
         functools.partial(bwd_kernel, hop=hop),
         "attend_back",
-        (queries, attended, d_attended, lses, cosine, sine, starts, keys, values),
+        (queries, attended, d_attended, lses, cosine, sine, starts, kv, kv),
         deps,
         grid=(groups, steps),
-        in_specs=[wide, wide, wide, lse, table, table, start, key, key],
-        out_specs=[wide, key, key],
+        in_specs=[wide, wide, wide, lse, table, table, start, *key],
+        out_specs=[wide, pl.BlockSpec((1, span, 256), lambda s, h: (s, 0, 0))],
         out_shape=[
             jax.ShapeDtypeStruct((T, width), bf16),
-            jax.ShapeDtypeStruct((groups, span, 128), f32),
-            jax.ShapeDtypeStruct((groups, span, 128), f32),
+            jax.ShapeDtypeStruct((groups, span, 256), f32),
         ],
     )
 
@@ -245,25 +243,24 @@
     return out
 
 
-def norm_keys(tokens, gain, w_kv, cosine, sine):
+def norm_keys(tokens, gain, w_key, w_value, cosine, sine):
     T, D = tokens.shape
     block = 128
-    hd = w_kv.shape[1] // 2
-
-    def kernel(x_ref, g_ref, w_ref, c_ref, s_ref, n_ref, inv_ref, kv_ref):
+    hd = w_key.shape[1]
+
+    def kernel(x_ref, g_ref, wk_ref, wv_ref, c_ref, s_ref, n_ref, inv_ref, kv_ref):
         x = x_ref[...].astype(f32)
         inv = lax.rsqrt(jnp.mean(x * x, axis=1, keepdims=True) + eps)
         normed = (x * inv * g_ref[...]).astype(bf16)
         n_ref[...] = normed
         inv_ref[...] = inv
-        kv = dot(normed, w_ref[...], 1, 0)
-        kv_ref[:, :hd] = turn(kv[:, :hd], c_ref[...], s_ref[...]).astype(bf16)
-        kv_ref[:, hd:] = kv[:, hd:].astype(bf16)
+        kv_ref[:, :hd] = turn(dot(normed, wk_ref[...], 1, 0), c_ref[...], s_ref[...]).astype(bf16)
+        kv_ref[:, hd:] = dot(normed, wv_ref[...], 1, 0, bf16)
 
     row = lambda w: pl.BlockSpec((block, w), lambda i: (i, 0))
     return call(
-        kernel, "norm_keys", (tokens, gain.reshape(1, D), w_kv, cosine, sine), grid=(T // block,),
-        in_specs=[row(D), pl.BlockSpec((1, D), lambda i: (0, 0)), whole(w_kv), row(hd), row(hd)],
+        kernel, "norm_keys", (tokens, gain.reshape(1, D), w_key, w_value, cosine, sine), grid=(T // block,),
+        in_specs=[row(D), pl.BlockSpec((1, D), lambda i: (0, 0)), whole(w_key), whole(w_value), row(hd), row(hd)],
         out_specs=[row(D), row(1), row(2 * hd)],
         out_shape=[shape((T, D)), shape((T, 1), f32), shape((T, 2 * hd))],
         vmem=56,
@@ -585,16 +582,18 @@
     )
 
 
-def tokens_back(d_query, d_kv, w_query, w_kv, d_branch, tokens, inverse, gain, deps=()):
+def tokens_back(d_query, d_kv, w_query, w_key, w_value, d_branch, tokens, inverse, gain, deps=()):
     T, D = tokens.shape
     block, rows = 512, 128
+    hd = w_key.shape[1]
     steps = D // block
 
-    def kernel(q_ref, kv_ref, wq_ref, wkv_ref, b_ref, x_ref, i_ref, gain_ref, t_ref, n_ref, sum_ref):
+    def kernel(q_ref, kv_ref, wq_ref, wk_ref, wv_ref, b_ref, x_ref, i_ref, gain_ref, t_ref, n_ref, sum_ref):
         i = pl.program_id(0)
         at = pl.ds(i * block, block)
         inv = i_ref[...]
-        dn = dot(q_ref[...], wq_ref[...], 1, 1) + dot(kv_ref[...], wkv_ref[...], 1, 1)
+        dn = dot(q_ref[...], wq_ref[...], 1, 1)
+        dn = dn + dot(kv_ref[:, :hd], wk_ref[...], 1, 1) + dot(kv_ref[:, hd:], wv_ref[...], 1, 1)
         xi = x_ref[...].astype(f32) * inv
         n_ref[...] = jnp.sum(dn * xi, axis=0, keepdims=True)
         e = dn * gain_ref[...]
@@ -619,17 +618,17 @@
 
     x_full = [None]
 
-    def outer(q_ref, kv_ref, wq_ref, wkv_ref, b_ref, x_ref, xf_ref, i_ref, gain_ref, t_ref, n_ref, sum_ref):
+    def outer(q_ref, kv_ref, wq_ref, wk_ref, wv_ref, b_ref, x_ref, xf_ref, i_ref, gain_ref, t_ref, n_ref, sum_ref):
         x_full[0] = xf_ref
-        kernel(q_ref, kv_ref, wq_ref, wkv_ref, b_ref, x_ref, i_ref, gain_ref, t_ref, n_ref, sum_ref)
+        kernel(q_ref, kv_ref, wq_ref, wk_ref, wv_ref, b_ref, x_ref, i_ref, gain_ref, t_ref, n_ref, sum_ref)
 
     full = lambda w: pl.BlockSpec((T, w), lambda i: (0, 0))
     vec = pl.BlockSpec((1, block), lambda i: (0, i))
     return call(
-        outer, "tokens_back", (d_query, d_kv, w_query, w_kv, d_branch, tokens, tokens, inverse, gain.reshape(1, D)), deps, grid=(steps,),
+        outer, "tokens_back", (d_query, d_kv, w_query, w_key, w_value, d_branch, tokens, tokens, inverse, gain.reshape(1, D)), deps, grid=(steps,),
         in_specs=[
             whole(d_query), whole(d_kv), pl.BlockSpec((block, w_query.shape[1]), lambda i: (i, 0)),
-            pl.BlockSpec((block, w_kv.shape[1]), lambda i: (i, 0)), whole(d_branch),
+            pl.BlockSpec((block, hd), lambda i: (i, 0)), pl.BlockSpec((block, hd), lambda i: (i, 0)), whole(d_branch),
             pl.BlockSpec((T, block), lambda i: (0, i)), whole(tokens), full(1), vec,
         ],
         out_specs=[full(D), vec],
@@ -650,6 +649,32 @@
     return call(
         kernel, "output", (mid, own, got), deps, grid=(T // block,), in_specs=[row] * 3, out_specs=row,
         out_shape=shape((T, D)), vmem=56,
+    )
+
+
+def join_columns(name, parts, order):
+    n, r, w = parts.shape
+
+    def kernel(p_ref, o_ref):
+        for k, b in enumerate(order):
+            o_ref[:, k * w : (k + 1) * w] = p_ref[b].astype(f32)
+
+    full = lambda d: pl.BlockSpec(d, lambda i: (0,) * len(d))
+    return call(kernel, name, (parts,), in_specs=[full(parts.shape)], out_specs=full((r, n * w)), out_shape=shape((r, n * w), f32))
+
+
+def join_two(name, parts, order):
+    n, _, r, w = parts.shape
+
+    def kernel(p_ref, a_ref, b_ref):
+        for k, at in enumerate(order):
+            a_ref[:, at * w : (at + 1) * w] = p_ref[k, 0].astype(f32)
+            b_ref[:, at * w : (at + 1) * w] = p_ref[k, 1].astype(f32)
+
+    full = lambda d: pl.BlockSpec(d, lambda i: (0,) * len(d))
+    return call(
+        kernel, name, (parts,), in_specs=[full(parts.shape)], out_specs=[full((r, n * w))] * 2,
+        out_shape=[shape((r, n * w), f32)] * 2,
     )
 
 
@@ -678,10 +703,11 @@
     hop = hops * L
     fq = FF // GROUP
     core, xb = mv.bit(1), mv.bit(2)
-    quarter = mv.b % GROUP
+    quarter = core * 2 + xb
     scalar = lambda v: v.astype(jnp.int32).reshape(1)
     qi, yi, xi = scalar(quarter), scalar(mv.y), scalar(xb)
     paired = ny == 2
+    quarter_of = lambda b: b % 2 * 2 + b // 2 % 2
 
     rows = tokens.reshape(T, D)
     cot = cotangent.reshape(T, D)
@@ -699,17 +725,15 @@
     cos_half, sin_half = jnp.cos(angle), jnp.sin(angle)
     cosine = jnp.concatenate([cos_half, cos_half], axis=1)
     sine = jnp.concatenate([-sin_half, sin_half], axis=1)
-    w_kv = jnp.concatenate([w_key, w_value], axis=1)
-
-    normed, inv1, kv = norm_keys(rows, norm1_gain, w_kv, cosine, sine)
+
+    normed, inv1, kv = norm_keys(rows, norm1_gain, w_key, w_value, cosine, sine)
     kv = kv.reshape(groups, L, 2 * hd)
     blocks = [kv]
     for _ in range(hops):
         blocks.insert(0, mv.shift(blocks[0], "z", range(nz), 1))
     kv_all = jnp.concatenate(blocks, axis=1)
-    keys, values = kv_all[:, :, :hd], kv_all[:, :, hd:]
     q_lin = project_query(normed, w_query, (kv,))
-    attended, queries, lses = attention(q_lin, cosine, sine, starts_rel, keys, values, hop)
+    attended, queries, lses = attention(q_lin, cosine, sine, starts_rel, kv_all, hop)
     mid, normed2, inv2 = project_out(attended, w_output, rows, norm2_gain, (cot1,))
     cot2 = hold(cot2, (normed2,))
     cot3 = mv.flip(cot2, 1)
@@ -782,10 +806,9 @@
 
     db_cuts = quarters(d_branch) if paired else ()
     db_all = exchange(db_cuts) if paired else ()
-    d_query, dk_all, dv_all = attention_back(
-        queries, attended, d_attended, lses, cosine, sine, starts_rel, keys, values, hop, db_cuts
-    )
-    dkv_all = jnp.concatenate([dk_all, dv_all], axis=2)
+    d_query, dkv_all = attention_back(
+        queries, attended, d_attended, lses, cosine, sine, starts_rel, kv_all, hop, db_cuts
+    )
     parts = [dkv_all[:, k * L : (k + 1) * L].astype(bf16) for k in range(hops)]
     back = mv.shift(parts[0], "z", range(nz), -1)
     if paired:
@@ -818,7 +841,7 @@
     d_key = (own[:, :hd] * cosine - swapped * sine).astype(bf16)
     d_kv = jnp.concatenate([d_key, own[:, hd:].astype(bf16)], axis=1)
     grad_tokens, norm1_term = tokens_back(
-        d_query, d_kv, w_query, w_kv, d_branch, rows, inv1, norm1_gain, (last,)
+        d_query, d_kv, w_query, w_key, w_value, d_branch, rows, inv1, norm1_gain, (last,)
     )
     g_kv = dot(normed, d_kv, 0, 0, bf16)
     if paired:
@@ -845,17 +868,17 @@
         norms = r_query[D // nz + size :, :2].astype(f32).T
         r_query = r_query[: D // nz]
 
-        def finish(r):
+        def finish(name, r):
             r = lax.all_to_all(r.reshape(nb, D // n_dev, D // nb), "batch", 0, 0, tiled=True)
             order = [y_ * GROUP + x_ * 2 + c_ for c_ in range(2) for y_ in range(2) for x_ in range(2)]
-            return jnp.concatenate([r[b_] for b_ in order], axis=1).astype(f32)
-
-        grad_output, grad_query = finish(r_out), finish(r_query)
+            return join_columns(name, r, order)
+
+        grad_output, grad_query = finish("join_out", r_out), finish("join_query", r_query)
         r_down = r_down.reshape(2, fq // (2 * nz), D // 2)
         parts = []
         for k in range(2):
             pairs = [
-                (z_ * nb + b_, (b_ % GROUP) * ny * nz + z_ * ny + (b_ // GROUP) ^ k)
+                (z_ * nb + b_, quarter_of(b_) * ny * nz + (z_ * ny + b_ // GROUP) ^ k)
                 for z_ in range(nz)
                 for b_ in range(nb)
             ]
@@ -871,7 +894,7 @@
         norms = jnp.sum(lax.all_to_all(norms, AXES, 0, 0, tiled=True), axis=0)
         r_down = sum_all(down_sent)
         pairs = [
-            (z_ * nb + b_, (b_ % GROUP) * ny * nz + z_ * ny + b_ // GROUP)
+            (z_ * nb + b_, quarter_of(b_) * ny * nz + z_ * ny + b_ // GROUP)
             for z_ in range(nz)
             for b_ in range(nb)
         ]
@@ -885,10 +908,14 @@
     def finish_quarter(r):
         k, height, width = r.shape
         r = r.reshape(k, GROUP, height // GROUP, width).transpose(1, 0, 2, 3)
-        r = lax.all_to_all(r, "batch", 0, 0, tiled=True, axis_index_groups=fours)
-        return r.transpose(1, 2, 0, 3).reshape(k, height // GROUP, FF).astype(f32)
+        return lax.all_to_all(r, "batch", 0, 0, tiled=True, axis_index_groups=fours)
 
     gu = finish_quarter(jnp.concatenate([r_gate, r_up], axis=0))
+    if paired:
+        grad_gate, grad_up = join_two("join", gu, [quarter_of(i) for i in range(GROUP)])
+    else:
+        gu = jnp.stack([gu[quarter_of(i)] for i in range(GROUP)]).transpose(1, 2, 0, 3).reshape(2, D // n_dev, FF).astype(f32)
+        grad_gate, grad_up = gu[0], gu[1]
     return (
         output.reshape(groups, L, D),
         grad_tokens.reshape(groups, L, D),
@@ -898,8 +925,8 @@
         r_kv[:, hd:],
         grad_output,
         norms[1],
-        gu[0],
-        gu[1],
+        grad_gate,
+        grad_up,
         grad_down,
     )
 

time: 526 us -> 525 us (level)
  local copies, waits for them, and re-layouts: 33.8 us -> 24.9 us
  Pallas kernels: 319 us -> 327 us
    all_to_all x1, waiting for transfers between devices: 3.41 us -> 14.9 us  [finish_quarter(): return lax.all_to_all(r, 'batch', 0, 0, tiled=True, axis_index_groups=fours)]
    ppermute x2, waiting for transfers between devices: 8.54 us -> 0.01 us  [shards(): parts.append(lax.ppermute(piece, AXES, pairs))]
    pallas_call x32 -> x35, Pallas kernels: 319 us -> 327 us  [call(): pl.pallas_call(body, grid_spec=pltpu.PrefetchScalarGridSpec(num_scalar_pr...]
    all_to_all x1, waiting for transfers between devices: 13.1 us -> 5.66 us  [shards(): g_kv = lax.all_to_all(g_kv, 'batch', 0, 0, tiled=True)]
    unnamed x77 -> x57, local copies, waits for them, and re-layouts: 15.5 us -> 11 us
  transfers between devices with their start and end apart: 45 -> 45, of which waited for: 11 -> 12; matrix products, arithmetic and copies ran while one was open for 8% -> 6% of each run, Pallas kernels for 58% -> 60%
where the time goes in v3:
time: 525 us; the launch traced here: 517 us
  Pallas kernels  327 us (62%)
  starting transfers between devices  72.8 us (14%)
  waiting for transfers between devices  52.3 us (10%)
  local copies, waits for them, and re-layouts  24.9 us (5%)
  other arithmetic  22.7 us (4%)
  between operations  14.5 us (3%)
    pallas_call x35, Pallas kernels, call(): pl.pallas_call(body, grid_spec=pltpu.PrefetchScalarGridSpec(num_scalar_pr...  327 us
    ppermute x27, starting transfers between devices, flip(): return lax.ppermute(value, AXES, pairs)  25.3 us
    ppermute x7, starting transfers between devices, shift(): return lax.ppermute(value, AXES, pairs)  19.5 us
    ppermute x27, waiting for transfers between devices, flip(): return lax.ppermute(value, AXES, pairs)  15.6 us
    all_to_all x1, waiting for transfers between devices, finish_quarter(): return lax.all_to_all(r, 'batch', 0, 0, tiled=True, axis_index_groups=fours)  14.9 us
    unnamed x57, local copies, waits for them, and re-layouts  11 us
  transfers between devices with their start and end apart: 45, of which 12 were waited for; matrix products, arithmetic and copies ran while one was open for 6% of the time, Pallas kernels for 60%

profile of v3, /device:TPU:5, one launch (start us, length us, event | category | flops | bytes accessed | tf_op | source)
XLA Modules:
  0.0 516.7 jit_solution(4650624913208318532)
XLA Ops:
  7.9 5.2 %collective-permute-start.2 = (s32[2,256]{1,0:T(2,128)S(1)}, s32[2,256]{1,0:T(2,128)S(1)}, u32[]{:S(2)}, u32[]{:S(2)}) collective-permute-start(s32[2,256]{1,0:T(2,128)S(1)} %broadcast_add_fusion), channel_id=1, source_target_pairs={{0,24},{1,25},{2,26},{3,27},{4,28},{5,29},{6,30},{7,31}} | collective-permute-start | bytes 6152 | tf_op jit(solution)/shard_map/ppermute | solution.py:88
  14.4 2.2 collective-permute-start
  21.7 5.1 norm_keys.1
  26.8 4.3 collective-permute-start.3
  32.3 2.7 collective-permute-start.5
  35.2 3.9 collective-permute-start.4
  39.2 9.2 %query.1.refs_0_ = f32[512,2048]{1,0:T(8,128)} custom-call(bf16[512,2048]{1,0:T(8,128)(2,1)} %get-tuple-element.39.refs_0_.refs_1_, bf16[2048,2048]{1,0:T(8,128)(2,1)} %refs_2_.3, bf16[2,256,256]{2,1,0:T(8,128)(2,1)} %bitcast.69), custom_call_target="tpu_custom_call" | custom-call | flops 179999997952 | bytes 1 | tf_op jit(solution)/shard_map/query/pallas_call | solution.py:44
  51.1 13.7 %attend.1 = (bf16[512,2048]{1,0:T(8,128)(2,1)}, bf16[512,2048]{1,0:T(8,128)(2,1)}, f32[2,2,256,8]{3,2,1,0:T(8,128)}) custom-call(f32[512,2048]{1,0:T(8,128)} %query.1.refs_0_, f32[512,128]{1,0:T(8,128)} %get-tuple-element.90.refs_4_.refs_1_, f32[512,128]{1,0:T(8,128)} %get-tuple-element.91.refs_5_.refs_2_, s32[512,1]{1,0:T(8,128)} %bitcast.65, ...), custom_call_target="tpu_custom_call" | custom-call | flops 280000004096 | bytes 1 | tf_op jit(solution)/shard_map/attend/pallas_call | solution.py:44
  64.9 11.5 %project_out.1 = (f32[512,2048]{1,0:T(8,128)}, bf16[512,2048]{1,0:T(8,128)(2,1)}, f32[512,1]{1,0:T(8,128)}) custom-call(bf16[512,2048]{1,0:T(8,128)(2,1)} %get-tuple-element.41.refs_0_.refs_1_, bf16[2048,2048]{1,0:T(8,128)(2,1)} %refs_6_.5, bf16[512,2048]{1,0:T(8,128)(2,1)} %bitcast.74, f32[1,2048]{1,0:T(1,128)} %bitcast.77, ...), custom_call_target="tpu_custom_call" | custom-call | flops 219999993856 | bytes 1 | tf_op jit(solution)/shard_map/project_out/pallas_call | solution.py:44
  76.4 3.4 collective-permute-start.8
  83.3 2.2 collective-permute-done.8.refs_4_
  86.9 20.1 %down_back.1.refs_3_ = bf16[2048,1408]{1,0:T(8,128)(2,1)} custom-call(s32[1]{0:T(128)} %bitcast.5.refs_0_, bf16[512,2048]{1,0:T(8,128)(2,1)} %bitcast.4.refs_1_.refs_4_, bf16[512,2048]{1,0:T(8,128)(2,1)} %collective-permute-done.5.refs_4_.refs_2_, bf16[512,2048]{1,0:T(8,128)(2,1)} %hold.8.refs_3_, bf16[512,2048]{1,0:T(8,128)(2,1)} %copy-done.23, ...), custom_call_target="tpu_custom_call" | custom-call | flops 399999991808 | bytes 1 | tf_op jit(solution)/shard_map/down_back/pallas_call | solution.py:44
  107.0 21.3 %feed.2 = (bf16[1024,1408]{1,0:T(8,128)(2,1)}, bf16[1024,1408]{1,0:T(8,128)(2,1)}, bf16[1024,1408]{1,0:T(8,128)(2,1)}) custom-call(s32[1]{0:T(128)} %bitcast.5.refs_0_, bf16[512,2048]{1,0:T(8,128)(2,1)} %get-tuple-element.43.refs_0_.refs_6_.refs_1_, bf16[512,2048]{1,0:T(8,128)(2,1)} %collective-permute-done.6.refs_2_, bf16[2048,1408]{1,0:T(8,128)(2,1)} %down_back.1.refs_3_, ...), custom_call_target="tpu_custom_call" | custom-call | flops 420000006144 | bytes 1 | tf_op jit(solution)/shard_map/feed/pallas_call | solution.py:44
  130.0 2.9 collective-permute-done.13.refs_2_.refs_4_
  134.2 21.6 %feed.3 = (bf16[1024,1408]{1,0:T(8,128)(2,1)}, bf16[1024,1408]{1,0:T(8,128)(2,1)}, bf16[1024,1408]{1,0:T(8,128)(2,1)}) custom-call(s32[1]{0:T(128)} %bitcast.5.refs_0_, bf16[512,2048]{1,0:T(8,128)(2,1)} %hold.9.refs_1_.refs_3_, bf16[512,2048]{1,0:T(8,128)(2,1)} %copy-done.24, bf16[2048,1408]{1,0:T(8,128)(2,1)} %down_back.1.refs_3_, ...), custom_call_target="tpu_custom_call" | custom-call | flops 420000006144 | bytes 1 | tf_op jit(solution)/shard_map/feed/pallas_call | solution.py:44
  155.8 11.5 %up_send.1.refs_7_ = bf16[4,256,1408]{2,1,0:T(8,128)(2,1)} custom-call(s32[1]{0:T(128)S(6)} %sub.55.refs_0_, bf16[512,2048]{1,0:T(8,128)(2,1)} %get-tuple-element.43.refs_0_.refs_6_.refs_1_, bf16[512,2048]{1,0:T(8,128)(2,1)} %collective-permute-done.6.refs_2_, bf16[512,2048]{1,0:T(8,128)(2,1)} %hold.9.refs_1_.refs_3_, bf16[512,2048]{1,0:T(8,128)(2,1)} %copy-done.24, ...), custom_call_target="tpu_custom_call" | custom-call | flops 219999993856 | bytes 1 | tf_op jit(solution)/shard_map/up_send/pallas_call | solution.py:44
  168.1 19.0 %gate.1.refs_0_ = bf16[8,256,1408]{2,1,0:T(8,128)(2,1)} custom-call(s32[1]{0:T(128)} %constant.91.clone.1.refs_0_, bf16[512,2048]{1,0:T(8,128)(2,1)} %get-tuple-element.43.refs_0_.refs_6_.refs_1_, bf16[512,2048]{1,0:T(8,128)(2,1)} %collective-permute-done.6.refs_2_, bf16[512,2048]{1,0:T(8,128)(2,1)} %hold.9.refs_1_.refs_3_, bf16[512,2048]{1,0:T(8,128)(2,1)} %copy-done.24, ...), custom_call_target="tpu_custom_call" | custom-call | flops 380000010240 | bytes 1 | tf_op jit(solution)/shard_map/gate/pallas_call | solution.py:44
  187.2 21.4 %dn2_away.1.refs_7_ = bf16[2,512,2048]{2,1,0:T(8,128)(2,1)} custom-call(s32[1]{0:T(128)} %bitcast.5.refs_0_, bf16[1024,1408]{1,0:T(8,128)(2,1)} %hold.10.refs_1_, bf16[1024,1408]{1,0:T(8,128)(2,1)} %get-tuple-element.48.refs_6_.refs_2_, bf16[1024,1408]{1,0:T(8,128)(2,1)} %get-tuple-element.45.refs_0_.refs_6_.refs_5_.refs_3_, ...), custom_call_target="tpu_custom_call" | custom-call | flops 399999991808 | bytes 1 | tf_op jit(solution)/shard_map/dn2_away/pallas_call | solution.py:44
  209.6 11.2 %down_send.1.refs_8_ = bf16[1408,1024]{1,0:T(8,128)(2,1)} custom-call(s32[1]{0:T(128)S(6)} %sub.55.refs_0_, bf16[512,2048]{1,0:T(8,128)(2,1)} %bitcast.4.refs_1_.refs_4_, bf16[512,2048]{1,0:T(8,128)(2,1)} %collective-permute-done.5.refs_4_.refs_2_, bf16[512,2048]{1,0:T(8,128)(2,1)} %hold.8.refs_3_, bf16[512,2048]{1,0:T(8,128)(2,1)} %copy-done.23, ...), custom_call_target="tpu_custom_call" | custom-call | flops 219999993856 | bytes 1 | tf_op jit(solution)/shard_map/down_send/pallas_call | solution.py:44
  221.4 21.8 %dn2_near.1 = (bf16[512,2048]{1,0:T(8,128)(2,1)}, bf16[512,2048]{1,0:T(8,128)(2,1)}) custom-call(s32[1]{0:T(128)} %bitcast.5.refs_0_, bf16[1024,1408]{1,0:T(8,128)(2,1)} %hold.10.refs_1_, bf16[1024,1408]{1,0:T(8,128)(2,1)} %get-tuple-element.48.refs_6_.refs_2_, bf16[1024,1408]{1,0:T(8,128)(2,1)} %get-tuple-element.45.refs_0_.refs_6_.refs_5_.refs_3_, ...), custom_call_target="tpu_custom_call" | custom-call | flops 439999987712 | bytes 1 | tf_op jit(solution)/shard_map/dn2_near/pallas_call | solution.py:44
  244.1 11.5 %out_away.1.refs_8_ = bf16[2,512,2048]{2,1,0:T(8,128)(2,1)} custom-call(s32[1]{0:T(128)} %bitcast.5.refs_0_, bf16[1024,1408]{1,0:T(8,128)(2,1)} %get-tuple-element.44.refs_5_.refs_1_, bf16[1024,1408]{1,0:T(8,128)(2,1)} %get-tuple-element.46.refs_6_.refs_2_, bf16[5632,2048]{1,0:T(8,128)(2,1)} %refs_3_.6, bf16[512,2048]{1,0:T(8,128)(2,1)} %get-tuple-element.50.refs_4_), custom_call_target="tpu_custom_call" | custom-call | flops 219999993856 | bytes 1 | tf_op jit(solution)/shard_map/out_away/pallas_call | solution.py:44
  256.2 11.8 %up_keep.1.refs_5_ = bf16[4,256,1408]{2,1,0:T(8,128)(2,1)} custom-call(s32[1]{0:T(128)} %bitcast.6.refs_0_, bf16[512,2048]{1,0:T(8,128)(2,1)} %get-tuple-element.43.refs_0_.refs_6_.refs_1_, bf16[512,2048]{1,0:T(8,128)(2,1)} %collective-permute-done.6.refs_2_, bf16[512,2048]{1,0:T(8,128)(2,1)} %hold.9.refs_1_.refs_3_, bf16[512,2048]{1,0:T(8,128)(2,1)} %copy-done.24, ...), custom_call_target="tpu_custom_call" | custom-call | flops 240000008192 | bytes 1 | tf_op jit(solution)/shard_map/up_keep/pallas_call | solution.py:44
  268.1 13.1 %out_near.1 = (bf16[512,2048]{1,0:T(8,128)(2,1)}, bf16[512,2048]{1,0:T(8,128)(2,1)}) custom-call(s32[1]{0:T(128)} %bitcast.5.refs_0_, bf16[1024,1408]{1,0:T(8,128)(2,1)} %get-tuple-element.44.refs_5_.refs_1_, bf16[1024,1408]{1,0:T(8,128)(2,1)} %get-tuple-element.46.refs_6_.refs_2_, bf16[5632,2048]{1,0:T(8,128)(2,1)} %refs_3_.6, ...), custom_call_target="tpu_custom_call" | custom-call | flops 260000006144 | bytes 1 | tf_op jit(solution)/shard_map/out_near/pallas_call | solution.py:44
  282.0 8.0 %collective-permute-done.22.refs_1_ = bf16[512,2048]{1,0:T(8,128)(2,1)} collective-permute-done((bf16[512,2048]{1,0:T(8,128)(2,1)}, bf16[512,2048]{1,0:T(8,128)(2,1)}, u32[]{:S(2)}, u32[]{:S(2)}) %collective-permute-start.22) | collective-permute-done | bytes 2097184 | tf_op jit(solution)/shard_map/ppermute | solution.py:76
  290.1 14.5 %mid_back.1 = (bf16[512,2048]{1,0:T(8,128)(2,1)}, f32[1,2048]{1,0:T(1,128)}, bf16[512,2048]{1,0:T(8,128)(2,1)}) custom-call(bf16[512,2048]{1,0:T(8,128)(2,1)} %get-tuple-element.54.refs_0_, bf16[512,2048]{1,0:T(8,128)(2,1)} %collective-permute-done.22.refs_1_, f32[512,2048]{1,0:T(8,128)} %get-tuple-element.42.refs_2_.refs_0_, ...), custom_call_target="tpu_custom_call" | custom-call | flops 280000004096 | bytes 1 | tf_op jit(solution)/shard_map/mid_back/pallas_call | solution.py:44
  304.5 2.9 constant_dynamic-slice_fusion.4
  307.5 3.9 collective-permute-start.28
  311.8 23.1 %attend_back.1 = (bf16[512,2048]{1,0:T(8,128)(2,1)}, f32[2,768,256]{2,1,0:T(8,128)}) custom-call(bf16[512,2048]{1,0:T(8,128)(2,1)} %get-tuple-element.53.refs_0_, bf16[512,2048]{1,0:T(8,128)(2,1)} %get-tuple-element.41.refs_0_.refs_1_, bf16[512,2048]{1,0:T(8,128)(2,1)} %get-tuple-element.56.refs_2_, f32[2,2,256,8]{3,2,1,0:T(8,128)} %get-tuple-element.57.refs_3_, ...), custom_call_target="tpu_custom_call" | custom-call | flops 460000002048 | bytes 1 | tf_op jit(solution)/shard_map/attend_back/pallas_call | solution.py:44
  342.7 11.6 %down_keep.1.refs_3_ = bf16[1408,1024]{1,0:T(8,128)(2,1)} custom-call(s32[1]{0:T(128)} %bitcast.6.refs_0_, bf16[512,2048]{1,0:T(8,128)(2,1)} %bitcast.4.refs_1_.refs_4_, bf16[512,2048]{1,0:T(8,128)(2,1)} %collective-permute-done.5.refs_4_.refs_2_, bf16[512,2048]{1,0:T(8,128)(2,1)} %hold.8.refs_3_, bf16[512,2048]{1,0:T(8,128)(2,1)} %copy-done.23, ...), custom_call_target="tpu_custom_call" | custom-call | flops 240000008192 | bytes 1 | tf_op jit(solution)/shard_map/down_keep/pallas_call | solution.py:44
  355.6 5.2 %output.1.refs_9_.refs_0_ = bf16[512,2048]{1,0:T(8,128)(2,1)} custom-call(f32[512,2048]{1,0:T(8,128)} %get-tuple-element.42.refs_2_.refs_0_, bf16[512,2048]{1,0:T(8,128)(2,1)} %get-tuple-element.51.refs_1_, bf16[512,2048]{1,0:T(8,128)(2,1)} %collective-permute-done.20.refs_2_, bf16[1408,1024]{1,0:T(8,128)(2,1)} %down_keep.1.refs_3_), custom_call_target="tpu_custom_call" | custom-call | flops 99999997952 | bytes 1 | tf_op jit(solution)/shard_map/output/pallas_call | solution.py:44
  370.0 6.9 %w_out_send.1.refs_9_ = bf16[2048,256]{1,0:T(8,128)(2,1)} custom-call(s32[1]{0:T(128)S(6)} %sub.56.refs_0_, bf16[512,2048]{1,0:T(8,128)(2,1)} %get-tuple-element.41.refs_0_.refs_1_, bf16[512,2048]{1,0:T(8,128)(2,1)} %collective-permute-done.14.refs_8_.refs_2_, bf16[512,2048]{1,0:T(8,128)(2,1)} %collective-permute-done.15.refs_9_.refs_3_, ...), custom_call_target="tpu_custom_call" | custom-call | flops 140000002048 | bytes 1 | tf_op jit(solution)/shard_map/w_out_send/pallas_call | solution.py:44
  377.1 6.9 %w_query_send.1.refs_0_.refs_10_ = bf16[2048,256]{1,0:T(8,128)(2,1)} custom-call(s32[1]{0:T(128)S(6)} %sub.56.refs_0_, bf16[512,2048]{1,0:T(8,128)(2,1)} %get-tuple-element.39.refs_0_.refs_1_, bf16[512,2048]{1,0:T(8,128)(2,1)} %collective-permute-done.9.refs_6_.refs_2_, bf16[512,2048]{1,0:T(8,128)(2,1)} %collective-permute-done.10.refs_7_.refs_3_, ...), custom_call_target="tpu_custom_call" | custom-call | flops 140000002048 | bytes 1 | tf_op jit(solution)/shard_map/w_query_send/pallas_call | solution.py:44
  385.1 2.8 collective-permute-done.30.refs_1_
  390.6 14.2 %tokens_back.1 = (f32[512,2048]{1,0:T(8,128)}, f32[1,2048]{1,0:T(1,128)}) custom-call(bf16[512,2048]{1,0:T(8,128)(2,1)} %get-tuple-element.59.refs_8_.refs_0_, bf16[512,256]{1,0:T(8,128)(2,1)} %pad_maximum_fusion.4.refs_1_, bf16[2048,2048]{1,0:T(8,128)(2,1)} %refs_2_.3, bf16[2048,128]{1,0:T(8,128)(2,1)} %refs_3_.7, bf16[2048,128]{1,0:T(8,128)(2,1)} %refs_4_.5, ...), custom_call_target="tpu_custom_call" | custom-call | flops 280000004096 | bytes 1 | tf_op jit(solution)/shard_map/tokens_back/pallas_call | solution.py:44
  405.5 2.3 convolution_convert_fusion
  410.4 6.3 %all-to-all-start = ((bf16[8,4,64,384]{3,2,1,0:T(8,128)(2,1)}), bf16[8,4,64,384]{3,2,1,0:T(8,128)(2,1)}, u32[]{:S(2)}, u32[]{:S(2)}) async-start(bf16[8,4,64,384]{3,2,1,0:T(8,128)(2,1)} %bitcast.52), calls=%async_computation.3 | async-start | bytes 3145728 | tf_op jit(solution)/shard_map/all_to_all | solution.py:852
  418.7 3.5 collective-permute-start.34
  422.3 2.2 collective-permute-start.35
  424.5 7.2 %w_out_keep.1.refs_10_.refs_0_ = bf16[2048,256]{1,0:T(8,128)(2,1)} custom-call(s32[1]{0:T(128)} %bitcast.9.refs_0_, bf16[512,2048]{1,0:T(8,128)(2,1)} %get-tuple-element.41.refs_0_.refs_1_, bf16[512,2048]{1,0:T(8,128)(2,1)} %collective-permute-done.14.refs_8_.refs_2_, bf16[512,2048]{1,0:T(8,128)(2,1)} %collective-permute-done.15.refs_9_.refs_3_, ...), custom_call_target="tpu_custom_call" | custom-call | flops 140000002048 | bytes 1 | tf_op jit(solution)/shard_map/w_out_keep/pallas_call | solution.py:44
  431.7 7.2 %w_query_keep.1.refs_0_ = bf16[2048,256]{1,0:T(8,128)(2,1)} custom-call(s32[1]{0:T(128)} %bitcast.9.refs_0_, bf16[512,2048]{1,0:T(8,128)(2,1)} %get-tuple-element.39.refs_0_.refs_1_, bf16[512,2048]{1,0:T(8,128)(2,1)} %collective-permute-done.9.refs_6_.refs_2_, bf16[512,2048]{1,0:T(8,128)(2,1)} %collective-permute-done.10.refs_7_.refs_3_, ...), custom_call_target="tpu_custom_call" | custom-call | flops 140000002048 | bytes 1 | tf_op jit(solution)/shard_map/w_query_keep/pallas_call | solution.py:44
  442.9 5.7 %all-to-all-done.refs_1_ = bf16[8,4,64,384]{3,2,1,0:T(8,128)(2,1)} async-done(((bf16[8,4,64,384]{3,2,1,0:T(8,128)(2,1)}), bf16[8,4,64,384]{3,2,1,0:T(8,128)(2,1)}, u32[]{:S(2)}, u32[]{:S(2)}) %all-to-all-start) | async-done | bytes 1572896 | tf_op jit(solution)/shard_map/all_to_all | solution.py:852
  448.6 5.8 %all-to-all-start.3 = ((bf16[4,2,64,1408]{3,2,1,0:T(8,128)(2,1)}), bf16[4,2,64,1408]{3,2,1,0:T(8,128)(2,1)S(1)}, u32[]{:S(2)}, u32[]{:S(2)}) async-start(bf16[4,2,64,1408]{3,2,1,0:T(8,128)(2,1)} %maximum_bitcast_fusion), calls=%async_computation.8 | async-start | bytes 2883584 | tf_op jit(solution)/shard_map/all_to_all | solution.py:911
  459.8 14.9 %all-to-all-done.3.refs_0_ = bf16[4,2,64,1408]{3,2,1,0:T(8,128)(2,1)S(1)} async-done(((bf16[4,2,64,1408]{3,2,1,0:T(8,128)(2,1)}), bf16[4,2,64,1408]{3,2,1,0:T(8,128)(2,1)S(1)}, u32[]{:S(2)}, u32[]{:S(2)}) %all-to-all-start.3) | async-done | bytes 1441824 | tf_op jit(solution)/shard_map/all_to_all | solution.py:911
  474.7 5.3 %all-to-all-start.2 = ((bf16[8,64,256]{2,1,0:T(8,128)(2,1)}), bf16[8,64,256]{2,1,0:T(8,128)(2,1)S(1)}, u32[]{:S(2)}, u32[]{:S(2)}) async-start(bf16[8,64,256]{2,1,0:T(8,128)(2,1)} %bitcast.67), calls=%async_computation.7 | async-start | bytes 524288 | tf_op jit(solution)/shard_map/all_to_all | solution.py:872
  479.9 3.1 join.1
  487.0 8.8 %reduce-scatter.12.cloned.1.call-done = bf16[1,640,256]{2,1,0:T(8,128)(2,1)} async-done(((bf16[4,640,256]{2,1,0:T(8,128)(2,1)}), bf16[1,640,256]{2,1,0:T(8,128)(2,1)}) %reduce-scatter.12.cloned.1.call-update) | async-done | bytes 327696 | tf_op jit(solution)/shard_map/reduce_scatter | solution.py:866
  498.2 4.7 all-to-all-start.1
  505.0 2.4 all-to-all-done.1.refs_0_
  (185 shorter events, 72.4 us)
Async XLA Ops:
  7.2 335.6 %reduce-scatter.6.cloned.1.call-start = ((), (), s32[]{:S(2)}) async-start(), calls=%async_computation.9 | async-start | bytes 7208960 | tf_op jit(solution)/shard_map/reduce_scatter | solution.py:789
  7.9 8.8 %collective-permute-start.2 = (s32[2,256]{1,0:T(2,128)S(1)}, s32[2,256]{1,0:T(2,128)S(1)}, u32[]{:S(2)}, u32[]{:S(2)}) collective-permute-start(s32[2,256]{1,0:T(2,128)S(1)} %broadcast_add_fusion), channel_id=1, source_target_pairs={{0,24},{1,25},{2,26},{3,27},{4,28},{5,29},{6,30},{7,31}} | collective-permute-start | bytes 6152 | tf_op jit(solution)/shard_map/ppermute | solution.py:88
  13.1 3.6 collective-permute-start.1
  14.4 2.9 collective-permute-start
  26.8 8.4 %collective-permute-start.3 = (bf16[2,256,256]{2,1,0:T(8,128)(2,1)}, bf16[2,256,256]{2,1,0:T(8,128)(2,1)}, u32[]{:S(2)}, u32[]{:S(2)}) collective-permute-start(bf16[2,256,256]{2,1,0:T(8,128)(2,1)} %bitcast.68), channel_id=1, source_target_pairs={{0,8},{1,9},{2,10},{3,11},{4,12},{5,13},{6,14},{7,15},{8,16},{9,17... | collective-permute-start | bytes 786440 | tf_op jit(solution)/shard_map/ppermute | solution.py:88
  31.1 45.3 %collective-permute-start.7 = (bf16[512,2048]{1,0:T(8,128)(2,1)}, bf16[512,2048]{1,0:T(8,128)(2,1)}, u32[]{:S(2)}, u32[]{:S(2)}) collective-permute-start(bf16[512,2048]{1,0:T(8,128)(2,1)} %bitcast.4.refs_1_.refs_4_), channel_id=1, source_target_pairs={{0,2},{1,3},{2,0},{3,1},{4,6},{5,7},{6,4},{7,5},{8,10},{9,11},{10,... | collective-permute-start | bytes 6291464 | tf_op jit(solution)/shard_map/ppermute | solution.py:76
  32.3 32.6 %collective-permute-start.5 = (bf16[512,2048]{1,0:T(8,128)(2,1)}, bf16[512,2048]{1,0:T(8,128)(2,1)}, u32[]{:S(2)}, u32[]{:S(2)}) collective-permute-start(bf16[512,2048]{1,0:T(8,128)(2,1)} %bitcast.4.refs_1_.refs_4_), channel_id=1, source_target_pairs={{0,1},{1,0},{2,3},{3,2},{4,5},{5,4},{6,7},{7,6},{8,9},{9,8},{10,11... | collective-permute-start | bytes 6291464 | tf_op jit(solution)/shard_map/ppermute | solution.py:76
  35.0 47.6 %collective-permute-start.10 = (bf16[512,2048]{1,0:T(8,128)(2,1)}, bf16[512,2048]{1,0:T(8,128)(2,1)}, u32[]{:S(2)}, u32[]{:S(2)}) collective-permute-start(bf16[512,2048]{1,0:T(8,128)(2,1)} %get-tuple-element.39.refs_0_.refs_1_), channel_id=1, source_target_pairs={{0,4},{1,5},{2,6},{3,7},{4,0},{5,1},{6,2},{7,3},{8,12},{9,13},{10,... | collective-permute-start | bytes 6291464 | tf_op jit(solution)/shard_map/ppermute | solution.py:76
  35.2 14.0 %collective-permute-start.4 = (bf16[2,256,256]{2,1,0:T(8,128)(2,1)}, bf16[2,256,256]{2,1,0:T(8,128)(2,1)}, u32[]{:S(2)}, u32[]{:S(2)}) collective-permute-start(bf16[2,256,256]{2,1,0:T(8,128)(2,1)} %collective-permute-done.3), channel_id=1, source_target_pairs={{0,8},{1,9},{2,10},{3,11},{4,12},{5,13},{6,14},{7,15},{8,16},{9,17... | collective-permute-start | bytes 786440 | tf_op jit(solution)/shard_map/ppermute | solution.py:88
  76.4 9.2 %collective-permute-start.8 = (bf16[512,2048]{1,0:T(8,128)(2,1)}, bf16[512,2048]{1,0:T(8,128)(2,1)S(1)}, u32[]{:S(2)}, u32[]{:S(2)}) collective-permute-start(bf16[512,2048]{1,0:T(8,128)(2,1)} %hold.8.refs_3_), channel_id=1, source_target_pairs={{0,1},{1,0},{2,3},{3,2},{4,5},{5,4},{6,7},{7,6},{8,9},{9,8},{10,11... | collective-permute-start | bytes 6291464 | tf_op jit(solution)/shard_map/ppermute | solution.py:76
  79.7 27.3 %collective-permute-start.9 = (bf16[512,2048]{1,0:T(8,128)(2,1)}, bf16[512,2048]{1,0:T(8,128)(2,1)}, u32[]{:S(2)}, u32[]{:S(2)}) collective-permute-start(bf16[512,2048]{1,0:T(8,128)(2,1)} %get-tuple-element.39.refs_0_.refs_1_), channel_id=1, source_target_pairs={{0,1},{1,0},{2,3},{3,2},{4,5},{5,4},{6,7},{7,6},{8,9},{9,8},{10,11... | collective-permute-start | bytes 6291464 | tf_op jit(solution)/shard_map/ppermute | solution.py:76
  79.9 49.7 %collective-permute-start.15 = (bf16[512,2048]{1,0:T(8,128)(2,1)}, bf16[512,2048]{1,0:T(8,128)(2,1)}, u32[]{:S(2)}, u32[]{:S(2)}) collective-permute-start(bf16[512,2048]{1,0:T(8,128)(2,1)} %get-tuple-element.41.refs_0_.refs_1_), channel_id=1, source_target_pairs={{0,4},{1,5},{2,6},{3,7},{4,0},{5,1},{6,2},{7,3},{8,12},{9,13},{10,... | collective-permute-start | bytes 6291464 | tf_op jit(solution)/shard_map/ppermute | solution.py:76
  80.1 48.2 %collective-permute-start.12 = (bf16[512,2048]{1,0:T(8,128)(2,1)}, bf16[512,2048]{1,0:T(8,128)(2,1)}, u32[]{:S(2)}, u32[]{:S(2)}) collective-permute-start(bf16[512,2048]{1,0:T(8,128)(2,1)} %get-tuple-element.43.refs_0_.refs_6_.refs_1_), channel_id=1, source_target_pairs={{0,2},{1,3},{2,0},{3,1},{4,6},{5,7},{6,4},{7,5},{8,10},{9,11},{10,... | collective-permute-start | bytes 6291464 | tf_op jit(solution)/shard_map/ppermute | solution.py:76
  82.6 24.5 %collective-permute-start.6 = (bf16[512,2048]{1,0:T(8,128)(2,1)}, bf16[512,2048]{1,0:T(8,128)(2,1)}, u32[]{:S(2)}, u32[]{:S(2)}) collective-permute-start(bf16[512,2048]{1,0:T(8,128)(2,1)} %get-tuple-element.43.refs_0_.refs_6_.refs_1_), channel_id=1, source_target_pairs={{0,1},{1,0},{2,3},{3,2},{4,5},{5,4},{6,7},{7,6},{8,9},{9,8},{10,11... | collective-permute-start | bytes 6291464 | tf_op jit(solution)/shard_map/ppermute | solution.py:76
  85.6 21.5 %collective-permute-start.11 = (bf16[512,2048]{1,0:T(8,128)(2,1)}, bf16[512,2048]{1,0:T(8,128)(2,1)}, u32[]{:S(2)}, u32[]{:S(2)}) collective-permute-start(bf16[512,2048]{1,0:T(8,128)(2,1)} %collective-permute-done.10.refs_7_.refs_3_), channel_id=1, source_target_pairs={{0,1},{1,0},{2,3},{3,2},{4,5},{5,4},{6,7},{7,6},{8,9},{9,8},{10,11... | collective-permute-start | bytes 6291464 | tf_op jit(solution)/shard_map/ppermute | solution.py:76
  128.3 4.5 collective-permute-start.13
  129.5 26.3 %collective-permute-start.14 = (bf16[512,2048]{1,0:T(8,128)(2,1)}, bf16[512,2048]{1,0:T(8,128)(2,1)}, u32[]{:S(2)}, u32[]{:S(2)}) collective-permute-start(bf16[512,2048]{1,0:T(8,128)(2,1)} %get-tuple-element.41.refs_0_.refs_1_), channel_id=1, source_target_pairs={{0,1},{1,0},{2,3},{3,2},{4,5},{5,4},{6,7},{7,6},{8,9},{9,8},{10,11... | collective-permute-start | bytes 6291464 | tf_op jit(solution)/shard_map/ppermute | solution.py:76
  129.6 26.2 %collective-permute-start.16 = (bf16[512,2048]{1,0:T(8,128)(2,1)}, bf16[512,2048]{1,0:T(8,128)(2,1)}, u32[]{:S(2)}, u32[]{:S(2)}) collective-permute-start(bf16[512,2048]{1,0:T(8,128)(2,1)} %collective-permute-done.15.refs_9_.refs_3_), channel_id=1, source_target_pairs={{0,1},{1,0},{2,3},{3,2},{4,5},{5,4},{6,7},{7,6},{8,9},{9,8},{10,11... | collective-permute-start | bytes 6291464 | tf_op jit(solution)/shard_map/ppermute | solution.py:76
  167.3 88.9 %collective-permute-start.19 = (bf16[4,256,1408]{2,1,0:T(8,128)(2,1)}, bf16[4,256,1408]{2,1,0:T(8,128)(2,1)}, u32[]{:S(2)}, u32[]{:S(2)}) collective-permute-start(bf16[4,256,1408]{2,1,0:T(8,128)(2,1)} %up_send.1.refs_7_), channel_id=1, source_target_pairs={{0,4},{1,5},{2,6},{3,7},{4,0},{5,1},{6,2},{7,3},{8,12},{9,13},{10,... | collective-permute-start | bytes 8650760 | tf_op jit(solution)/shard_map/ppermute | solution.py:76
  187.1 181.9 %reduce-scatter.8.cloned.1.call-start = ((), (), s32[]{:S(2)}) async-start(), calls=%async_computation.10 | async-start | bytes 3604480 | tf_op jit(solution)/shard_map/reduce_scatter | solution.py:770
  208.6 12.8 %collective-permute-start.17 = (bf16[2,512,2048]{2,1,0:T(8,128)(2,1)}, bf16[2,512,2048]{2,1,0:T(8,128)(2,1)}, u32[]{:S(2)}, u32[]{:S(2)}) collective-permute-start(bf16[2,512,2048]{2,1,0:T(8,128)(2,1)} %dn2_away.1.refs_7_), channel_id=1, source_target_pairs={{0,1},{1,0},{2,3},{3,2},{4,5},{5,4},{6,7},{7,6},{8,9},{9,8},{10,11... | collective-permute-start | bytes 12582920 | tf_op jit(solution)/shard_map/ppermute | solution.py:76
  220.7 119.2 %collective-permute-start.21 = (bf16[1408,1024]{1,0:T(8,128)(2,1)}, bf16[1408,1024]{1,0:T(8,128)(2,1)}, u32[]{:S(2)}, u32[]{:S(2)}) collective-permute-start(bf16[1408,1024]{1,0:T(8,128)(2,1)} %down_send.1.refs_8_), channel_id=1, source_target_pairs={{0,4},{1,5},{2,6},{3,7},{4,0},{5,1},{6,2},{7,3},{8,12},{9,13},{10,... | collective-permute-start | bytes 8650760 | tf_op jit(solution)/shard_map/ppermute | solution.py:76
  243.2 46.8 %collective-permute-start.22 = (bf16[512,2048]{1,0:T(8,128)(2,1)}, bf16[512,2048]{1,0:T(8,128)(2,1)}, u32[]{:S(2)}, u32[]{:S(2)}) collective-permute-start(bf16[512,2048]{1,0:T(8,128)(2,1)} %get-tuple-element.50.refs_4_), channel_id=1, source_target_pairs={{0,2},{1,3},{2,0},{3,1},{4,6},{5,7},{6,4},{7,5},{8,10},{9,11},{10,... | collective-permute-start | bytes 6291464 | tf_op jit(solution)/shard_map/ppermute | solution.py:76
  255.5 12.6 %collective-permute-start.18 = (bf16[2,512,2048]{2,1,0:T(8,128)(2,1)}, bf16[2,512,2048]{2,1,0:T(8,128)(2,1)}, u32[]{:S(2)}, u32[]{:S(2)}) collective-permute-start(bf16[2,512,2048]{2,1,0:T(8,128)(2,1)} %out_away.1.refs_8_), channel_id=1, source_target_pairs={{0,1},{1,0},{2,3},{3,2},{4,5},{5,4},{6,7},{7,6},{8,9},{9,8},{10,11... | collective-permute-start | bytes 12582920 | tf_op jit(solution)/shard_map/ppermute | solution.py:76
  268.0 148.7 %reduce-scatter.10.cloned.1.call-start = ((), (), s32[]{:S(2)}) async-start(), calls=%async_computation.11 | async-start | bytes 3604480 | tf_op jit(solution)/shard_map/reduce_scatter | solution.py:819
  281.2 73.2 %collective-permute-start.20 = (bf16[512,2048]{1,0:T(8,128)(2,1)}, bf16[512,2048]{1,0:T(8,128)(2,1)}, u32[]{:S(2)}, u32[]{:S(2)}) collective-permute-start(bf16[512,2048]{1,0:T(8,128)(2,1)} %get-tuple-element.52.refs_7_), channel_id=1, source_target_pairs={{0,2},{1,3},{2,0},{3,1},{4,6},{5,7},{6,4},{7,5},{8,10},{9,11},{10,... | collective-permute-start | bytes 6291464 | tf_op jit(solution)/shard_map/ppermute | solution.py:76
  307.5 57.6 %collective-permute-start.28 = (bf16[512,512]{1,0:T(8,128)(2,1)}, bf16[512,512]{1,0:T(8,128)(2,1)}, u32[]{:S(2)}, u32[]{:S(2)}) collective-permute-start(bf16[512,512]{1,0:T(8,128)(2,1)} %get-tuple-element.73.refs_12_), channel_id=1, source_target_pairs={{0,5},{1,4},{2,7},{3,6},{4,1},{5,0},{6,3},{7,2},{8,13},{9,12},{10,... | collective-permute-start | bytes 1572872 | tf_op jit(solution)/shard_map/ppermute | solution.py:76
  311.3 55.0 %collective-permute-start.27 = (bf16[512,512]{1,0:T(8,128)(2,1)}, bf16[512,512]{1,0:T(8,128)(2,1)}, u32[]{:S(2)}, u32[]{:S(2)}) collective-permute-start(bf16[512,512]{1,0:T(8,128)(2,1)} %get-tuple-element.74.refs_11_), channel_id=1, source_target_pairs={{0,4},{1,5},{2,6},{3,7},{4,0},{5,1},{6,2},{7,3},{8,12},{9,13},{10,... | collective-permute-start | bytes 1572872 | tf_op jit(solution)/shard_map/ppermute | solution.py:76
  311.5 29.7 %collective-permute-start.23 = (bf16[512,512]{1,0:T(8,128)(2,1)}, bf16[512,512]{1,0:T(8,128)(2,1)}, u32[]{:S(2)}, u32[]{:S(2)}) collective-permute-start(bf16[512,512]{1,0:T(8,128)(2,1)} %get-tuple-element.75.refs_10_), channel_id=1, source_target_pairs={{0,1},{1,0},{2,3},{3,2},{4,5},{5,4},{6,7},{7,6},{8,9},{9,8},{10,11... | collective-permute-start | bytes 1572872 | tf_op jit(solution)/shard_map/ppermute | solution.py:76
  311.8 23.1 %copy-start.20 = (f32[1,2048]{1,0:T(1,128)S(1)}, f32[1,2048]{1,0:T(1,128)}, u32[]{:S(2)}) copy-start(f32[1,2048]{1,0:T(1,128)} %get-tuple-element.64) | copy-start | bytes 24580
  339.9 20.9 %collective-permute-start.29 = (bf16[2,256,256]{2,1,0:T(8,128)(2,1)}, bf16[2,256,256]{2,1,0:T(8,128)(2,1)}, u32[]{:S(2)}, u32[]{:S(2)}) collective-permute-start(bf16[2,256,256]{2,1,0:T(8,128)(2,1)} %slice.69), channel_id=1, source_target_pairs={{8,0},{9,1},{10,2},{11,3},{12,4},{13,5},{14,6},{15,7},{16,8},{17,9... | collective-permute-start | bytes 786440 | tf_op jit(solution)/shard_map/ppermute | solution.py:88
  341.2 26.6 %collective-permute-start.26 = (bf16[512,512]{1,0:T(8,128)(2,1)}, bf16[512,512]{1,0:T(8,128)(2,1)}, u32[]{:S(2)}, u32[]{:S(2)}) collective-permute-start(bf16[512,512]{1,0:T(8,128)(2,1)} %get-tuple-element.69), channel_id=1, source_target_pairs={{0,5},{1,4},{2,7},{3,6},{4,1},{5,0},{6,3},{7,2},{8,13},{9,12},{10,... | collective-permute-start | bytes 1572872 | tf_op jit(solution)/shard_map/ppermute | solution.py:76
  355.4 13.6 %collective-permute-start.25 = (bf16[512,512]{1,0:T(8,128)(2,1)S(1)}, bf16[512,512]{1,0:T(8,128)(2,1)S(1)}, u32[]{:S(2)}, u32[]{:S(2)}) collective-permute-start(bf16[512,512]{1,0:T(8,128)(2,1)S(1)} %copy-done.15), channel_id=1, source_target_pairs={{0,4},{1,5},{2,6},{3,7},{4,0},{5,1},{6,2},{7,3},{8,12},{9,13},{10,... | collective-permute-start | bytes 1572872 | tf_op jit(solution)/shard_map/ppermute | solution.py:76
  361.9 7.1 %collective-permute-start.24 = (bf16[512,512]{1,0:T(8,128)(2,1)S(1)}, bf16[512,512]{1,0:T(8,128)(2,1)S(1)}, u32[]{:S(2)}, u32[]{:S(2)}) collective-permute-start(bf16[512,512]{1,0:T(8,128)(2,1)S(1)} %copy-done.14), channel_id=1, source_target_pairs={{0,1},{1,0},{2,3},{3,2},{4,5},{5,4},{6,7},{7,6},{8,9},{9,8},{10,11... | collective-permute-start | bytes 1572872 | tf_op jit(solution)/shard_map/ppermute | solution.py:76
  365.1 22.8 %collective-permute-start.30 = (bf16[2,256,256]{2,1,0:T(8,128)(2,1)}, bf16[2,256,256]{2,1,0:T(8,128)(2,1)}, u32[]{:S(2)}, u32[]{:S(2)}) collective-permute-start(bf16[2,256,256]{2,1,0:T(8,128)(2,1)} %add_convert_fusion), channel_id=1, source_target_pairs={{8,0},{9,1},{10,2},{11,3},{12,4},{13,5},{14,6},{15,7},{16,8},{17,9... | collective-permute-start | bytes 786440 | tf_op jit(solution)/shard_map/ppermute | solution.py:88
  366.4 72.5 %collective-permute-start.33 = (bf16[256,1408]{1,0:T(8,128)(2,1)}, bf16[256,1408]{1,0:T(8,128)(2,1)}, u32[]{:S(2)}, u32[]{:S(2)}) collective-permute-start(bf16[256,1408]{1,0:T(8,128)(2,1)} %dynamic-slice_bitcast_fusion), channel_id=1, source_target_pairs={{0,4},{1,5},{2,6},{3,7},{4,0},{5,1},{6,2},{7,3},{8,12},{9,13},{10,... | collective-permute-start | bytes 2162696 | tf_op jit(solution)/shard_map/ppermute | solution.py:76
  376.9 47.6 %collective-permute-start.32 = (bf16[2048,256]{1,0:T(8,128)(2,1)}, bf16[2048,256]{1,0:T(8,128)(2,1)}, u32[]{:S(2)}, u32[]{:S(2)}) collective-permute-start(bf16[2048,256]{1,0:T(8,128)(2,1)} %w_out_send.1.refs_9_), channel_id=1, source_target_pairs={{0,2},{1,3},{2,0},{3,1},{4,6},{5,7},{6,4},{7,5},{8,10},{9,11},{10,... | collective-permute-start | bytes 3145736 | tf_op jit(solution)/shard_map/ppermute | solution.py:76
  383.9 47.8 %collective-permute-start.31 = (bf16[2048,256]{1,0:T(8,128)(2,1)}, bf16[2048,256]{1,0:T(8,128)(2,1)}, u32[]{:S(2)}, u32[]{:S(2)}) collective-permute-start(bf16[2048,256]{1,0:T(8,128)(2,1)} %w_query_send.1.refs_0_.refs_10_), channel_id=1, source_target_pairs={{0,2},{1,3},{2,0},{3,1},{4,6},{5,7},{6,4},{7,5},{8,10},{9,11},{10,... | collective-permute-start | bytes 3145736 | tf_op jit(solution)/shard_map/ppermute | solution.py:76
  390.6 14.9 %copy-start.11 = (bf16[512,128]{1,0:T(8,128)(2,1)S(1)}, bf16[512,128]{1,0:T(8,128)(2,1)}, u32[]{:S(2)}) copy-start(bf16[512,128]{1,0:T(8,128)(2,1)} %copy-done.10) | copy-start | bytes 393220
  390.6 14.9 %copy-start.13 = (bf16[512,128]{1,0:T(8,128)(2,1)S(1)}, bf16[512,128]{1,0:T(8,128)(2,1)}, u32[]{:S(2)}) copy-start(bf16[512,128]{1,0:T(8,128)(2,1)} %copy-done.12) | copy-start | bytes 393220
  410.4 38.2 %all-to-all-start = ((bf16[8,4,64,384]{3,2,1,0:T(8,128)(2,1)}), bf16[8,4,64,384]{3,2,1,0:T(8,128)(2,1)}, u32[]{:S(2)}, u32[]{:S(2)}) async-start(bf16[8,4,64,384]{3,2,1,0:T(8,128)(2,1)} %bitcast.52), calls=%async_computation.3 | async-start | bytes 3145728 | tf_op jit(solution)/shard_map/all_to_all | solution.py:852
  416.7 58.0 %reduce-scatter.14.cloned.1.call-start = ((), (), s32[]{:S(2)}) async-start(), calls=%async_computation.13 | async-start | bytes 1310720 | tf_op jit(solution)/shard_map/reduce_scatter | solution.py:854
  418.7 38.6 %collective-permute-start.34 = (bf16[176,1024]{1,0:T(8,128)(2,1)}, bf16[176,1024]{1,0:T(8,128)(2,1)}, u32[]{:S(2)}, u32[]{:S(2)}) collective-permute-start(bf16[176,1024]{1,0:T(8,128)(2,1)} %get-tuple-element.79), channel_id=1, source_target_pairs={{0,0},{1,16},{2,8},{3,24},{4,1},{5,17},{6,9},{7,25},{8,2},{9,18},{... | collective-permute-start | bytes 1081352 | tf_op jit(solution)/shard_map/ppermute | solution.py:886
  422.3 35.1 %collective-permute-start.35 = (bf16[176,1024]{1,0:T(8,128)(2,1)}, bf16[176,1024]{1,0:T(8,128)(2,1)}, u32[]{:S(2)}, u32[]{:S(2)}) collective-permute-start(bf16[176,1024]{1,0:T(8,128)(2,1)} %get-tuple-element.80), channel_id=1, source_target_pairs={{0,1},{1,17},{2,9},{3,25},{4,0},{5,16},{6,8},{7,24},{8,3},{9,19},{... | collective-permute-start | bytes 1081352 | tf_op jit(solution)/shard_map/ppermute | solution.py:886
  448.6 26.1 %all-to-all-start.3 = ((bf16[4,2,64,1408]{3,2,1,0:T(8,128)(2,1)}), bf16[4,2,64,1408]{3,2,1,0:T(8,128)(2,1)S(1)}, u32[]{:S(2)}, u32[]{:S(2)}) async-start(bf16[4,2,64,1408]{3,2,1,0:T(8,128)(2,1)} %maximum_bitcast_fusion), calls=%async_computation.8 | async-start | bytes 2883584 | tf_op jit(solution)/shard_map/all_to_all | solution.py:911
  454.4 41.5 %reduce-scatter.12.cloned.1.call-start = ((), (), s32[]{:S(2)}) async-start(), calls=%async_computation.12 | async-start | bytes 1638400 | tf_op jit(solution)/shard_map/reduce_scatter | solution.py:866
  474.7 9.9 %all-to-all-start.2 = ((bf16[8,64,256]{2,1,0:T(8,128)(2,1)}), bf16[8,64,256]{2,1,0:T(8,128)(2,1)S(1)}, u32[]{:S(2)}, u32[]{:S(2)}) async-start(bf16[8,64,256]{2,1,0:T(8,128)(2,1)} %bitcast.67), calls=%async_computation.7 | async-start | bytes 524288 | tf_op jit(solution)/shard_map/all_to_all | solution.py:872
  498.2 9.2 %all-to-all-start.1 = ((bf16[8,64,256]{2,1,0:T(8,128)(2,1)}), bf16[8,64,256]{2,1,0:T(8,128)(2,1)S(1)}, u32[]{:S(2)}, u32[]{:S(2)}) async-start(bf16[8,64,256]{2,1,0:T(8,128)(2,1)} %bitcast.18), calls=%async_computation.5 | async-start | bytes 524288 | tf_op jit(solution)/shard_map/all_to_all | solution.py:872
  (24 other events, 53.7 us)
Sparse Core Ops, SparseCore 0:
  187.3 100.3 reduce-scatter.5
  289.9 58.6 reduce-scatter.7
  354.5 61.1 reduce-scatter.9
  431.8 31.6 reduce-scatter.13
  465.8 29.9 reduce-scatter.11

commit v4 on v3

--- a/solution.py
+++ b/solution.py
@@ -243,26 +243,26 @@
     return out
 
 
-def norm_keys(tokens, gain, w_key, w_value, cosine, sine):
+def norm_keys(tokens, gain, w_key, w_value):
     T, D = tokens.shape
     block = 128
     hd = w_key.shape[1]
 
-    def kernel(x_ref, g_ref, wk_ref, wv_ref, c_ref, s_ref, n_ref, inv_ref, kv_ref):
+    def kernel(x_ref, g_ref, wk_ref, wv_ref, n_ref, inv_ref, kv_ref):
         x = x_ref[...].astype(f32)
         inv = lax.rsqrt(jnp.mean(x * x, axis=1, keepdims=True) + eps)
         normed = (x * inv * g_ref[...]).astype(bf16)
         n_ref[...] = normed
         inv_ref[...] = inv
-        kv_ref[:, :hd] = turn(dot(normed, wk_ref[...], 1, 0), c_ref[...], s_ref[...]).astype(bf16)
-        kv_ref[:, hd:] = dot(normed, wv_ref[...], 1, 0, bf16)
+        kv_ref[:, :hd] = dot(normed, wk_ref[...], 1, 0)
+        kv_ref[:, hd:] = dot(normed, wv_ref[...], 1, 0)
 
     row = lambda w: pl.BlockSpec((block, w), lambda i: (i, 0))
     return call(
-        kernel, "norm_keys", (tokens, gain.reshape(1, D), w_key, w_value, cosine, sine), grid=(T // block,),
-        in_specs=[row(D), pl.BlockSpec((1, D), lambda i: (0, 0)), whole(w_key), whole(w_value), row(hd), row(hd)],
+        kernel, "norm_keys", (tokens, gain.reshape(1, D), w_key, w_value), grid=(T // block,),
+        in_specs=[row(D), pl.BlockSpec((1, D), lambda i: (0, 0)), whole(w_key), whole(w_value)],
         out_specs=[row(D), row(1), row(2 * hd)],
-        out_shape=[shape((T, D)), shape((T, 1), f32), shape((T, 2 * hd))],
+        out_shape=[shape((T, D)), shape((T, 1), f32), shape((T, 2 * hd), f32)],
         vmem=56,
     )
 
@@ -726,7 +726,9 @@
     cosine = jnp.concatenate([cos_half, cos_half], axis=1)
     sine = jnp.concatenate([-sin_half, sin_half], axis=1)
 
-    normed, inv1, kv = norm_keys(rows, norm1_gain, w_key, w_value, cosine, sine)
+    normed, inv1, kv = norm_keys(rows, norm1_gain, w_key, w_value)
+    key_swapped = jnp.concatenate([kv[:, half:hd], kv[:, :half]], axis=1)
+    kv = jnp.concatenate([kv[:, :hd] * cosine + key_swapped * sine, kv[:, hd:]], axis=1).astype(bf16)
     kv = kv.reshape(groups, L, 2 * hd)
     blocks = [kv]
     for _ in range(hops):

time: 525 us -> 525 us (level)
    unnamed x57 -> x69, local copies, waits for them, and re-layouts: 11 us -> 11.5 us
  transfers between devices with their start and end apart: 45 -> 45, of which waited for: 12 -> 12; matrix products, arithmetic and copies ran while one was open for 6% -> 7% of each run, Pallas kernels for 60% -> 61%
where the time goes in v4:
time: 525 us; the launch traced here: 517 us
  Pallas kernels  327 us (62%)
  starting transfers between devices  68.3 us (13%)
  waiting for transfers between devices  54.6 us (10%)
  local copies, waits for them, and re-layouts  27.6 us (5%)
  other arithmetic  22.3 us (4%)
  between operations  14.6 us (3%)
    pallas_call x35, Pallas kernels, call(): pl.pallas_call(body, grid_spec=pltpu.PrefetchScalarGridSpec(num_scalar_pr...  327 us
    ppermute x27, starting transfers between devices, flip(): return lax.ppermute(value, AXES, pairs)  22.4 us
    ppermute x7, starting transfers between devices, shift(): return lax.ppermute(value, AXES, pairs)  18.9 us
    ppermute x27, waiting for transfers between devices, flip(): return lax.ppermute(value, AXES, pairs)  16 us
    all_to_all x1, waiting for transfers between devices, finish_quarter(): return lax.all_to_all(r, 'batch', 0, 0, tiled=True, axis_index_groups=fours)  14.7 us
    unnamed x69, local copies, waits for them, and re-layouts  11.5 us
  transfers between devices with their start and end apart: 45, of which 12 were waited for; matrix products, arithmetic and copies ran while one was open for 7% of the time, Pallas kernels for 61%

profile of v4, /device:TPU:5, one launch (start us, length us, event | category | flops | bytes accessed | tf_op | source)
XLA Modules:
  0.0 516.8 jit_solution(2106247018398019798)
XLA Ops:
  7.9 5.2 %collective-permute-start.2 = (s32[2,256]{1,0:T(2,128)S(1)}, s32[2,256]{1,0:T(2,128)S(1)}, u32[]{:S(2)}, u32[]{:S(2)}) collective-permute-start(s32[2,256]{1,0:T(2,128)S(1)} %broadcast_add_fusion), channel_id=1, source_target_pairs={{0,24},{1,25},{2,26},{3,27},{4,28},{5,29},{6,30},{7,31}} | collective-permute-start | bytes 6152 | tf_op jit(solution)/shard_map/ppermute | solution.py:88
  14.4 2.2 collective-permute-start
  16.7 5.0 norm_keys.1
  28.5 2.6 collective-permute-start.3
  35.0 5.1 collective-permute-start.4
  40.2 9.2 %query.1.refs_0_ = f32[512,2048]{1,0:T(8,128)} custom-call(bf16[512,2048]{1,0:T(8,128)(2,1)} %get-tuple-element.39.refs_0_.refs_1_, bf16[2048,2048]{1,0:T(8,128)(2,1)} %refs_2_.3, bf16[2,256,256]{2,1,0:T(8,128)(2,1)} %copy-done.21), custom_call_target="tpu_custom_call" | custom-call | flops 179999997952 | bytes 1 | tf_op jit(solution)/shard_map/query/pallas_call | solution.py:44
  50.2 2.0 maximum_maximum_fusion.refs_4_.refs_5_.refs_7_.refs_8_
  52.2 13.8 %attend.1 = (bf16[512,2048]{1,0:T(8,128)(2,1)}, bf16[512,2048]{1,0:T(8,128)(2,1)}, f32[2,2,256,8]{3,2,1,0:T(8,128)}) custom-call(f32[512,2048]{1,0:T(8,128)} %query.1.refs_0_, f32[512,128]{1,0:T(8,128)} %get-tuple-element.87.refs_1_.refs_4_, f32[512,128]{1,0:T(8,128)} %get-tuple-element.70.refs_2_.refs_5_, s32[512,1]{1,0:T(8,128)} %bitcast.70, ...), custom_call_target="tpu_custom_call" | custom-call | flops 280000004096 | bytes 1 | tf_op jit(solution)/shard_map/attend/pallas_call | solution.py:44
  66.0 11.5 %project_out.1 = (f32[512,2048]{1,0:T(8,128)}, bf16[512,2048]{1,0:T(8,128)(2,1)}, f32[512,1]{1,0:T(8,128)}) custom-call(bf16[512,2048]{1,0:T(8,128)(2,1)} %get-tuple-element.41.refs_0_.refs_1_, bf16[2048,2048]{1,0:T(8,128)(2,1)} %refs_6_.5, bf16[512,2048]{1,0:T(8,128)(2,1)} %bitcast.76, f32[1,2048]{1,0:T(1,128)} %bitcast.79, ...), custom_call_target="tpu_custom_call" | custom-call | flops 219999993856 | bytes 1 | tf_op jit(solution)/shard_map/project_out/pallas_call | solution.py:44
  77.5 2.2 collective-permute-start.8
  82.2 3.7 collective-permute-done.8.refs_4_
  87.2 20.1 %down_back.1.refs_3_ = bf16[2048,1408]{1,0:T(8,128)(2,1)} custom-call(s32[1]{0:T(128)} %bitcast.6.refs_0_, bf16[512,2048]{1,0:T(8,128)(2,1)} %bitcast.5.refs_1_.refs_4_, bf16[512,2048]{1,0:T(8,128)(2,1)} %collective-permute-done.5.refs_4_.refs_2_, bf16[512,2048]{1,0:T(8,128)(2,1)} %hold.8.refs_3_, bf16[512,2048]{1,0:T(8,128)(2,1)} %copy-done.29, ...), custom_call_target="tpu_custom_call" | custom-call | flops 399999991808 | bytes 1 | tf_op jit(solution)/shard_map/down_back/pallas_call | solution.py:44
  107.3 21.3 %feed.2 = (bf16[1024,1408]{1,0:T(8,128)(2,1)}, bf16[1024,1408]{1,0:T(8,128)(2,1)}, bf16[1024,1408]{1,0:T(8,128)(2,1)}) custom-call(s32[1]{0:T(128)} %bitcast.6.refs_0_, bf16[512,2048]{1,0:T(8,128)(2,1)} %get-tuple-element.43.refs_0_.refs_6_.refs_1_, bf16[512,2048]{1,0:T(8,128)(2,1)} %collective-permute-done.6.refs_2_, bf16[2048,1408]{1,0:T(8,128)(2,1)} %down_back.1.refs_3_, ...), custom_call_target="tpu_custom_call" | custom-call | flops 420000006144 | bytes 1 | tf_op jit(solution)/shard_map/feed/pallas_call | solution.py:44
  130.4 2.9 collective-permute-done.13.refs_2_.refs_4_
  134.6 21.6 %feed.3 = (bf16[1024,1408]{1,0:T(8,128)(2,1)}, bf16[1024,1408]{1,0:T(8,128)(2,1)}, bf16[1024,1408]{1,0:T(8,128)(2,1)}) custom-call(s32[1]{0:T(128)} %bitcast.6.refs_0_, bf16[512,2048]{1,0:T(8,128)(2,1)} %hold.9.refs_1_.refs_3_, bf16[512,2048]{1,0:T(8,128)(2,1)} %copy-done.30, bf16[2048,1408]{1,0:T(8,128)(2,1)} %down_back.1.refs_3_, ...), custom_call_target="tpu_custom_call" | custom-call | flops 420000006144 | bytes 1 | tf_op jit(solution)/shard_map/feed/pallas_call | solution.py:44
  156.2 11.5 %up_send.1.refs_7_ = bf16[4,256,1408]{2,1,0:T(8,128)(2,1)} custom-call(s32[1]{0:T(128)S(6)} %sub.55.refs_0_, bf16[512,2048]{1,0:T(8,128)(2,1)} %get-tuple-element.43.refs_0_.refs_6_.refs_1_, bf16[512,2048]{1,0:T(8,128)(2,1)} %collective-permute-done.6.refs_2_, bf16[512,2048]{1,0:T(8,128)(2,1)} %hold.9.refs_1_.refs_3_, bf16[512,2048]{1,0:T(8,128)(2,1)} %copy-done.30, ...), custom_call_target="tpu_custom_call" | custom-call | flops 219999993856 | bytes 1 | tf_op jit(solution)/shard_map/up_send/pallas_call | solution.py:44
  168.0 19.0 %gate.1.refs_0_ = bf16[8,256,1408]{2,1,0:T(8,128)(2,1)} custom-call(s32[1]{0:T(128)} %constant.91.clone.1.refs_0_, bf16[512,2048]{1,0:T(8,128)(2,1)} %get-tuple-element.43.refs_0_.refs_6_.refs_1_, bf16[512,2048]{1,0:T(8,128)(2,1)} %collective-permute-done.6.refs_2_, bf16[512,2048]{1,0:T(8,128)(2,1)} %hold.9.refs_1_.refs_3_, bf16[512,2048]{1,0:T(8,128)(2,1)} %copy-done.30, ...), custom_call_target="tpu_custom_call" | custom-call | flops 380000010240 | bytes 1 | tf_op jit(solution)/shard_map/gate/pallas_call | solution.py:44
  187.1 21.5 %dn2_away.1.refs_7_ = bf16[2,512,2048]{2,1,0:T(8,128)(2,1)} custom-call(s32[1]{0:T(128)} %bitcast.6.refs_0_, bf16[1024,1408]{1,0:T(8,128)(2,1)} %hold.10.refs_1_, bf16[1024,1408]{1,0:T(8,128)(2,1)} %get-tuple-element.48.refs_6_.refs_2_, bf16[1024,1408]{1,0:T(8,128)(2,1)} %get-tuple-element.45.refs_0_.refs_6_.refs_5_.refs_3_, ...), custom_call_target="tpu_custom_call" | custom-call | flops 399999991808 | bytes 1 | tf_op jit(solution)/shard_map/dn2_away/pallas_call | solution.py:44
  209.4 11.1 %down_send.1.refs_8_ = bf16[1408,1024]{1,0:T(8,128)(2,1)} custom-call(s32[1]{0:T(128)S(6)} %sub.55.refs_0_, bf16[512,2048]{1,0:T(8,128)(2,1)} %bitcast.5.refs_1_.refs_4_, bf16[512,2048]{1,0:T(8,128)(2,1)} %collective-permute-done.5.refs_4_.refs_2_, bf16[512,2048]{1,0:T(8,128)(2,1)} %hold.8.refs_3_, bf16[512,2048]{1,0:T(8,128)(2,1)} %copy-done.29, ...), custom_call_target="tpu_custom_call" | custom-call | flops 219999993856 | bytes 1 | tf_op jit(solution)/shard_map/down_send/pallas_call | solution.py:44
  221.6 21.8 %dn2_near.1 = (bf16[512,2048]{1,0:T(8,128)(2,1)}, bf16[512,2048]{1,0:T(8,128)(2,1)}) custom-call(s32[1]{0:T(128)} %bitcast.6.refs_0_, bf16[1024,1408]{1,0:T(8,128)(2,1)} %hold.10.refs_1_, bf16[1024,1408]{1,0:T(8,128)(2,1)} %get-tuple-element.48.refs_6_.refs_2_, bf16[1024,1408]{1,0:T(8,128)(2,1)} %get-tuple-element.45.refs_0_.refs_6_.refs_5_.refs_3_, ...), custom_call_target="tpu_custom_call" | custom-call | flops 439999987712 | bytes 1 | tf_op jit(solution)/shard_map/dn2_near/pallas_call | solution.py:44
  244.2 11.5 %out_away.1.refs_8_ = bf16[2,512,2048]{2,1,0:T(8,128)(2,1)} custom-call(s32[1]{0:T(128)} %bitcast.6.refs_0_, bf16[1024,1408]{1,0:T(8,128)(2,1)} %get-tuple-element.44.refs_5_.refs_1_, bf16[1024,1408]{1,0:T(8,128)(2,1)} %get-tuple-element.46.refs_6_.refs_2_, bf16[5632,2048]{1,0:T(8,128)(2,1)} %refs_3_.6, bf16[512,2048]{1,0:T(8,128)(2,1)} %get-tuple-element.50.refs_4_), custom_call_target="tpu_custom_call" | custom-call | flops 219999993856 | bytes 1 | tf_op jit(solution)/shard_map/out_away/pallas_call | solution.py:44
  256.4 11.8 %up_keep.1.refs_5_ = bf16[4,256,1408]{2,1,0:T(8,128)(2,1)} custom-call(s32[1]{0:T(128)} %bitcast.7.refs_0_, bf16[512,2048]{1,0:T(8,128)(2,1)} %get-tuple-element.43.refs_0_.refs_6_.refs_1_, bf16[512,2048]{1,0:T(8,128)(2,1)} %collective-permute-done.6.refs_2_, bf16[512,2048]{1,0:T(8,128)(2,1)} %hold.9.refs_1_.refs_3_, bf16[512,2048]{1,0:T(8,128)(2,1)} %copy-done.30, ...), custom_call_target="tpu_custom_call" | custom-call | flops 240000008192 | bytes 1 | tf_op jit(solution)/shard_map/up_keep/pallas_call | solution.py:44
  268.3 13.1 %out_near.1 = (bf16[512,2048]{1,0:T(8,128)(2,1)}, bf16[512,2048]{1,0:T(8,128)(2,1)}) custom-call(s32[1]{0:T(128)} %bitcast.6.refs_0_, bf16[1024,1408]{1,0:T(8,128)(2,1)} %get-tuple-element.44.refs_5_.refs_1_, bf16[1024,1408]{1,0:T(8,128)(2,1)} %get-tuple-element.46.refs_6_.refs_2_, bf16[5632,2048]{1,0:T(8,128)(2,1)} %refs_3_.6, ...), custom_call_target="tpu_custom_call" | custom-call | flops 260000006144 | bytes 1 | tf_op jit(solution)/shard_map/out_near/pallas_call | solution.py:44
  282.3 7.9 %collective-permute-done.22.refs_1_ = bf16[512,2048]{1,0:T(8,128)(2,1)} collective-permute-done((bf16[512,2048]{1,0:T(8,128)(2,1)}, bf16[512,2048]{1,0:T(8,128)(2,1)}, u32[]{:S(2)}, u32[]{:S(2)}) %collective-permute-start.22) | collective-permute-done | bytes 2097184 | tf_op jit(solution)/shard_map/ppermute | solution.py:76
  290.2 14.5 %mid_back.1 = (bf16[512,2048]{1,0:T(8,128)(2,1)}, f32[1,2048]{1,0:T(1,128)}, bf16[512,2048]{1,0:T(8,128)(2,1)}) custom-call(bf16[512,2048]{1,0:T(8,128)(2,1)} %get-tuple-element.54.refs_0_, bf16[512,2048]{1,0:T(8,128)(2,1)} %collective-permute-done.22.refs_1_, f32[512,2048]{1,0:T(8,128)} %get-tuple-element.42.refs_2_.refs_0_, ...), custom_call_target="tpu_custom_call" | custom-call | flops 280000004096 | bytes 1 | tf_op jit(solution)/shard_map/mid_back/pallas_call | solution.py:44
  304.7 2.9 constant_dynamic-slice_fusion.4
  307.5 3.5 collective-permute-start.28
  312.1 23.1 %attend_back.1 = (bf16[512,2048]{1,0:T(8,128)(2,1)}, f32[2,768,256]{2,1,0:T(8,128)}) custom-call(bf16[512,2048]{1,0:T(8,128)(2,1)} %get-tuple-element.53.refs_0_, bf16[512,2048]{1,0:T(8,128)(2,1)} %get-tuple-element.41.refs_0_.refs_1_, bf16[512,2048]{1,0:T(8,128)(2,1)} %get-tuple-element.56.refs_2_, f32[2,2,256,8]{3,2,1,0:T(8,128)} %get-tuple-element.57.refs_3_, ...), custom_call_target="tpu_custom_call" | custom-call | flops 460000002048 | bytes 1 | tf_op jit(solution)/shard_map/attend_back/pallas_call | solution.py:44
  342.4 11.6 %down_keep.1.refs_3_ = bf16[1408,1024]{1,0:T(8,128)(2,1)} custom-call(s32[1]{0:T(128)} %bitcast.7.refs_0_, bf16[512,2048]{1,0:T(8,128)(2,1)} %bitcast.5.refs_1_.refs_4_, bf16[512,2048]{1,0:T(8,128)(2,1)} %collective-permute-done.5.refs_4_.refs_2_, bf16[512,2048]{1,0:T(8,128)(2,1)} %hold.8.refs_3_, bf16[512,2048]{1,0:T(8,128)(2,1)} %copy-done.29, ...), custom_call_target="tpu_custom_call" | custom-call | flops 240000008192 | bytes 1 | tf_op jit(solution)/shard_map/down_keep/pallas_call | solution.py:44
  356.1 5.2 %output.1.refs_9_.refs_0_ = bf16[512,2048]{1,0:T(8,128)(2,1)} custom-call(f32[512,2048]{1,0:T(8,128)} %get-tuple-element.42.refs_2_.refs_0_, bf16[512,2048]{1,0:T(8,128)(2,1)} %get-tuple-element.51.refs_1_, bf16[512,2048]{1,0:T(8,128)(2,1)} %collective-permute-done.20.refs_2_, bf16[1408,1024]{1,0:T(8,128)(2,1)} %down_keep.1.refs_3_), custom_call_target="tpu_custom_call" | custom-call | flops 99999997952 | bytes 1 | tf_op jit(solution)/shard_map/output/pallas_call | solution.py:44
  369.7 6.9 %w_out_send.1.refs_9_ = bf16[2048,256]{1,0:T(8,128)(2,1)} custom-call(s32[1]{0:T(128)S(6)} %sub.56.refs_0_, bf16[512,2048]{1,0:T(8,128)(2,1)} %get-tuple-element.41.refs_0_.refs_1_, bf16[512,2048]{1,0:T(8,128)(2,1)} %collective-permute-done.14.refs_8_.refs_2_, bf16[512,2048]{1,0:T(8,128)(2,1)} %collective-permute-done.15.refs_9_.refs_3_, ...), custom_call_target="tpu_custom_call" | custom-call | flops 140000002048 | bytes 1 | tf_op jit(solution)/shard_map/w_out_send/pallas_call | solution.py:44
  376.8 6.9 %w_query_send.1.refs_0_.refs_10_ = bf16[2048,256]{1,0:T(8,128)(2,1)} custom-call(s32[1]{0:T(128)S(6)} %sub.56.refs_0_, bf16[512,2048]{1,0:T(8,128)(2,1)} %get-tuple-element.39.refs_0_.refs_1_, bf16[512,2048]{1,0:T(8,128)(2,1)} %collective-permute-done.9.refs_6_.refs_2_, bf16[512,2048]{1,0:T(8,128)(2,1)} %collective-permute-done.10.refs_7_.refs_3_, ...), custom_call_target="tpu_custom_call" | custom-call | flops 140000002048 | bytes 1 | tf_op jit(solution)/shard_map/w_query_send/pallas_call | solution.py:44
  384.8 3.6 collective-permute-done.30.refs_1_
  391.1 14.2 %tokens_back.1 = (f32[512,2048]{1,0:T(8,128)}, f32[1,2048]{1,0:T(1,128)}) custom-call(bf16[512,2048]{1,0:T(8,128)(2,1)} %get-tuple-element.59.refs_8_.refs_0_, bf16[512,256]{1,0:T(8,128)(2,1)} %pad_maximum_fusion.4.refs_1_, bf16[2048,2048]{1,0:T(8,128)(2,1)} %refs_2_.3, bf16[2048,128]{1,0:T(8,128)(2,1)} %refs_3_.7, bf16[2048,128]{1,0:T(8,128)(2,1)} %refs_4_.5, ...), custom_call_target="tpu_custom_call" | custom-call | flops 280000004096 | bytes 1 | tf_op jit(solution)/shard_map/tokens_back/pallas_call | solution.py:44
  406.0 2.3 convolution_convert_fusion
  410.9 5.5 %all-to-all-start = ((bf16[8,4,64,384]{3,2,1,0:T(8,128)(2,1)}), bf16[8,4,64,384]{3,2,1,0:T(8,128)(2,1)}, u32[]{:S(2)}, u32[]{:S(2)}) async-start(bf16[8,4,64,384]{3,2,1,0:T(8,128)(2,1)} %bitcast.53), calls=%async_computation.3 | async-start | bytes 3145728 | tf_op jit(solution)/shard_map/all_to_all | solution.py:854
  416.3 2.0 dynamic-slice_bitcast_fusion.2
  418.4 3.8 collective-permute-start.34
  424.1 7.2 %w_out_keep.1.refs_10_.refs_0_ = bf16[2048,256]{1,0:T(8,128)(2,1)} custom-call(s32[1]{0:T(128)} %bitcast.10.refs_0_, bf16[512,2048]{1,0:T(8,128)(2,1)} %get-tuple-element.41.refs_0_.refs_1_, bf16[512,2048]{1,0:T(8,128)(2,1)} %collective-permute-done.14.refs_8_.refs_2_, bf16[512,2048]{1,0:T(8,128)(2,1)} %collective-permute-done.15.refs_9_.refs_3_, ...), custom_call_target="tpu_custom_call" | custom-call | flops 140000002048 | bytes 1 | tf_op jit(solution)/shard_map/w_out_keep/pallas_call | solution.py:44
  431.3 7.2 %w_query_keep.1.refs_0_ = bf16[2048,256]{1,0:T(8,128)(2,1)} custom-call(s32[1]{0:T(128)} %bitcast.10.refs_0_, bf16[512,2048]{1,0:T(8,128)(2,1)} %get-tuple-element.39.refs_0_.refs_1_, bf16[512,2048]{1,0:T(8,128)(2,1)} %collective-permute-done.9.refs_6_.refs_2_, bf16[512,2048]{1,0:T(8,128)(2,1)} %collective-permute-done.10.refs_7_.refs_3_, ...), custom_call_target="tpu_custom_call" | custom-call | flops 140000002048 | bytes 1 | tf_op jit(solution)/shard_map/w_query_keep/pallas_call | solution.py:44
  442.5 6.1 %all-to-all-done.refs_1_ = bf16[8,4,64,384]{3,2,1,0:T(8,128)(2,1)} async-done(((bf16[8,4,64,384]{3,2,1,0:T(8,128)(2,1)}), bf16[8,4,64,384]{3,2,1,0:T(8,128)(2,1)}, u32[]{:S(2)}, u32[]{:S(2)}) %all-to-all-start) | async-done | bytes 1572896 | tf_op jit(solution)/shard_map/all_to_all | solution.py:854
  448.6 5.7 %all-to-all-start.3 = ((bf16[4,2,64,1408]{3,2,1,0:T(8,128)(2,1)}), bf16[4,2,64,1408]{3,2,1,0:T(8,128)(2,1)S(1)}, u32[]{:S(2)}, u32[]{:S(2)}) async-start(bf16[4,2,64,1408]{3,2,1,0:T(8,128)(2,1)} %maximum_bitcast_fusion), calls=%async_computation.8 | async-start | bytes 2883584 | tf_op jit(solution)/shard_map/all_to_all | solution.py:913
  459.7 14.7 %all-to-all-done.3.refs_0_ = bf16[4,2,64,1408]{3,2,1,0:T(8,128)(2,1)S(1)} async-done(((bf16[4,2,64,1408]{3,2,1,0:T(8,128)(2,1)}), bf16[4,2,64,1408]{3,2,1,0:T(8,128)(2,1)S(1)}, u32[]{:S(2)}, u32[]{:S(2)}) %all-to-all-start.3) | async-done | bytes 1441824 | tf_op jit(solution)/shard_map/all_to_all | solution.py:913
  474.4 5.3 %all-to-all-start.2 = ((bf16[8,64,256]{2,1,0:T(8,128)(2,1)}), bf16[8,64,256]{2,1,0:T(8,128)(2,1)S(1)}, u32[]{:S(2)}, u32[]{:S(2)}) async-start(bf16[8,64,256]{2,1,0:T(8,128)(2,1)} %bitcast.72), calls=%async_computation.7 | async-start | bytes 524288 | tf_op jit(solution)/shard_map/all_to_all | solution.py:874
  479.7 3.1 join.1
  486.8 9.2 %reduce-scatter.12.cloned.1.call-done = bf16[1,640,256]{2,1,0:T(8,128)(2,1)} async-done(((bf16[4,640,256]{2,1,0:T(8,128)(2,1)}), bf16[1,640,256]{2,1,0:T(8,128)(2,1)}) %reduce-scatter.12.cloned.1.call-update) | async-done | bytes 327696 | tf_op jit(solution)/shard_map/reduce_scatter | solution.py:868
  498.4 4.7 all-to-all-start.1
  505.1 2.4 all-to-all-done.1.refs_0_
  (200 shorter events, 73.3 us)
Async XLA Ops:
  7.2 335.3 %reduce-scatter.6.cloned.1.call-start = ((), (), s32[]{:S(2)}) async-start(), calls=%async_computation.9 | async-start | bytes 7208960 | tf_op jit(solution)/shard_map/reduce_scatter | solution.py:791
  7.9 16.0 %collective-permute-start.2 = (s32[2,256]{1,0:T(2,128)S(1)}, s32[2,256]{1,0:T(2,128)S(1)}, u32[]{:S(2)}, u32[]{:S(2)}) collective-permute-start(s32[2,256]{1,0:T(2,128)S(1)} %broadcast_add_fusion), channel_id=1, source_target_pairs={{0,24},{1,25},{2,26},{3,27},{4,28},{5,29},{6,30},{7,31}} | collective-permute-start | bytes 6152 | tf_op jit(solution)/shard_map/ppermute | solution.py:88
  13.1 10.8 %collective-permute-start.1 = (s32[2,256]{1,0:T(2,128)S(1)}, s32[2,256]{1,0:T(2,128)S(1)}, u32[]{:S(2)}, u32[]{:S(2)}) collective-permute-start(s32[2,256]{1,0:T(2,128)S(1)} %broadcast_add_fusion), channel_id=1, source_target_pairs={{0,16},{1,17},{2,18},{3,19},{4,20},{5,21},{6,22},{7,23},{8,24},{9,... | collective-permute-start | bytes 6152 | tf_op jit(solution)/shard_map/ppermute | solution.py:88
  14.4 9.5 %collective-permute-start = (s32[2,256]{1,0:T(2,128)S(1)}, s32[2,256]{1,0:T(2,128)S(1)}, u32[]{:S(2)}, u32[]{:S(2)}) collective-permute-start(s32[2,256]{1,0:T(2,128)S(1)} %broadcast_add_fusion), channel_id=1, source_target_pairs={{0,8},{1,9},{2,10},{3,11},{4,12},{5,13},{6,14},{7,15},{8,16},{9,17... | collective-permute-start | bytes 6152 | tf_op jit(solution)/shard_map/ppermute | solution.py:88
  28.5 6.6 %collective-permute-start.3 = (bf16[2,256,256]{2,1,0:T(8,128)(2,1)S(1)}, bf16[2,256,256]{2,1,0:T(8,128)(2,1)}, u32[]{:S(2)}, u32[]{:S(2)}) collective-permute-start(bf16[2,256,256]{2,1,0:T(8,128)(2,1)S(1)} %pad_maximum_fusion.3.refs_2_), channel_id=1, source_target_pairs={{0,8},{1,9},{2,10},{3,11},{4,12},{5,13},{6,14},{7,15},{8,16},{9,17... | collective-permute-start | bytes 786440 | tf_op jit(solution)/shard_map/ppermute | solution.py:88
  31.1 46.4 %collective-permute-start.7 = (bf16[512,2048]{1,0:T(8,128)(2,1)}, bf16[512,2048]{1,0:T(8,128)(2,1)}, u32[]{:S(2)}, u32[]{:S(2)}) collective-permute-start(bf16[512,2048]{1,0:T(8,128)(2,1)} %bitcast.5.refs_1_.refs_4_), channel_id=1, source_target_pairs={{0,2},{1,3},{2,0},{3,1},{4,6},{5,7},{6,4},{7,5},{8,10},{9,11},{10,... | collective-permute-start | bytes 6291464 | tf_op jit(solution)/shard_map/ppermute | solution.py:76
  32.3 33.6 %collective-permute-start.5 = (bf16[512,2048]{1,0:T(8,128)(2,1)}, bf16[512,2048]{1,0:T(8,128)(2,1)}, u32[]{:S(2)}, u32[]{:S(2)}) collective-permute-start(bf16[512,2048]{1,0:T(8,128)(2,1)} %bitcast.5.refs_1_.refs_4_), channel_id=1, source_target_pairs={{0,1},{1,0},{2,3},{3,2},{4,5},{5,4},{6,7},{7,6},{8,9},{9,8},{10,11... | collective-permute-start | bytes 6291464 | tf_op jit(solution)/shard_map/ppermute | solution.py:76
  33.8 47.6 %collective-permute-start.10 = (bf16[512,2048]{1,0:T(8,128)(2,1)}, bf16[512,2048]{1,0:T(8,128)(2,1)}, u32[]{:S(2)}, u32[]{:S(2)}) collective-permute-start(bf16[512,2048]{1,0:T(8,128)(2,1)} %get-tuple-element.39.refs_0_.refs_1_), channel_id=1, source_target_pairs={{0,4},{1,5},{2,6},{3,7},{4,0},{5,1},{6,2},{7,3},{8,12},{9,13},{10,... | collective-permute-start | bytes 6291464 | tf_op jit(solution)/shard_map/ppermute | solution.py:76
  35.0 15.1 %collective-permute-start.4 = (bf16[2,256,256]{2,1,0:T(8,128)(2,1)}, bf16[2,256,256]{2,1,0:T(8,128)(2,1)}, u32[]{:S(2)}, u32[]{:S(2)}) collective-permute-start(bf16[2,256,256]{2,1,0:T(8,128)(2,1)} %collective-permute-done.3), channel_id=1, source_target_pairs={{0,8},{1,9},{2,10},{3,11},{4,12},{5,13},{6,14},{7,15},{8,16},{9,17... | collective-permute-start | bytes 786440 | tf_op jit(solution)/shard_map/ppermute | solution.py:88
  77.5 8.4 %collective-permute-start.8 = (bf16[512,2048]{1,0:T(8,128)(2,1)}, bf16[512,2048]{1,0:T(8,128)(2,1)S(1)}, u32[]{:S(2)}, u32[]{:S(2)}) collective-permute-start(bf16[512,2048]{1,0:T(8,128)(2,1)} %hold.8.refs_3_), channel_id=1, source_target_pairs={{0,1},{1,0},{2,3},{3,2},{4,5},{5,4},{6,7},{7,6},{8,9},{9,8},{10,11... | collective-permute-start | bytes 6291464 | tf_op jit(solution)/shard_map/ppermute | solution.py:76
  79.7 27.6 %collective-permute-start.9 = (bf16[512,2048]{1,0:T(8,128)(2,1)}, bf16[512,2048]{1,0:T(8,128)(2,1)}, u32[]{:S(2)}, u32[]{:S(2)}) collective-permute-start(bf16[512,2048]{1,0:T(8,128)(2,1)} %get-tuple-element.39.refs_0_.refs_1_), channel_id=1, source_target_pairs={{0,1},{1,0},{2,3},{3,2},{4,5},{5,4},{6,7},{7,6},{8,9},{9,8},{10,11... | collective-permute-start | bytes 6291464 | tf_op jit(solution)/shard_map/ppermute | solution.py:76
  79.7 50.2 %collective-permute-start.15 = (bf16[512,2048]{1,0:T(8,128)(2,1)}, bf16[512,2048]{1,0:T(8,128)(2,1)}, u32[]{:S(2)}, u32[]{:S(2)}) collective-permute-start(bf16[512,2048]{1,0:T(8,128)(2,1)} %get-tuple-element.41.refs_0_.refs_1_), channel_id=1, source_target_pairs={{0,4},{1,5},{2,6},{3,7},{4,0},{5,1},{6,2},{7,3},{8,12},{9,13},{10,... | collective-permute-start | bytes 6291464 | tf_op jit(solution)/shard_map/ppermute | solution.py:76
  80.0 48.7 %collective-permute-start.12 = (bf16[512,2048]{1,0:T(8,128)(2,1)}, bf16[512,2048]{1,0:T(8,128)(2,1)}, u32[]{:S(2)}, u32[]{:S(2)}) collective-permute-start(bf16[512,2048]{1,0:T(8,128)(2,1)} %get-tuple-element.43.refs_0_.refs_6_.refs_1_), channel_id=1, source_target_pairs={{0,2},{1,3},{2,0},{3,1},{4,6},{5,7},{6,4},{7,5},{8,10},{9,11},{10,... | collective-permute-start | bytes 6291464 | tf_op jit(solution)/shard_map/ppermute | solution.py:76
  81.4 25.9 %collective-permute-start.6 = (bf16[512,2048]{1,0:T(8,128)(2,1)}, bf16[512,2048]{1,0:T(8,128)(2,1)}, u32[]{:S(2)}, u32[]{:S(2)}) collective-permute-start(bf16[512,2048]{1,0:T(8,128)(2,1)} %get-tuple-element.43.refs_0_.refs_6_.refs_1_), channel_id=1, source_target_pairs={{0,1},{1,0},{2,3},{3,2},{4,5},{5,4},{6,7},{7,6},{8,9},{9,8},{10,11... | collective-permute-start | bytes 6291464 | tf_op jit(solution)/shard_map/ppermute | solution.py:76
  85.9 21.4 %collective-permute-start.11 = (bf16[512,2048]{1,0:T(8,128)(2,1)}, bf16[512,2048]{1,0:T(8,128)(2,1)}, u32[]{:S(2)}, u32[]{:S(2)}) collective-permute-start(bf16[512,2048]{1,0:T(8,128)(2,1)} %collective-permute-done.10.refs_7_.refs_3_), channel_id=1, source_target_pairs={{0,1},{1,0},{2,3},{3,2},{4,5},{5,4},{6,7},{7,6},{8,9},{9,8},{10,11... | collective-permute-start | bytes 6291464 | tf_op jit(solution)/shard_map/ppermute | solution.py:76
  128.6 4.7 collective-permute-start.13
  129.9 26.3 %collective-permute-start.14 = (bf16[512,2048]{1,0:T(8,128)(2,1)}, bf16[512,2048]{1,0:T(8,128)(2,1)}, u32[]{:S(2)}, u32[]{:S(2)}) collective-permute-start(bf16[512,2048]{1,0:T(8,128)(2,1)} %get-tuple-element.41.refs_0_.refs_1_), channel_id=1, source_target_pairs={{0,1},{1,0},{2,3},{3,2},{4,5},{5,4},{6,7},{7,6},{8,9},{9,8},{10,11... | collective-permute-start | bytes 6291464 | tf_op jit(solution)/shard_map/ppermute | solution.py:76
  130.0 26.2 %collective-permute-start.16 = (bf16[512,2048]{1,0:T(8,128)(2,1)}, bf16[512,2048]{1,0:T(8,128)(2,1)}, u32[]{:S(2)}, u32[]{:S(2)}) collective-permute-start(bf16[512,2048]{1,0:T(8,128)(2,1)} %collective-permute-done.15.refs_9_.refs_3_), channel_id=1, source_target_pairs={{0,1},{1,0},{2,3},{3,2},{4,5},{5,4},{6,7},{7,6},{8,9},{9,8},{10,11... | collective-permute-start | bytes 6291464 | tf_op jit(solution)/shard_map/ppermute | solution.py:76
  167.7 88.7 %collective-permute-start.19 = (bf16[4,256,1408]{2,1,0:T(8,128)(2,1)}, bf16[4,256,1408]{2,1,0:T(8,128)(2,1)}, u32[]{:S(2)}, u32[]{:S(2)}) collective-permute-start(bf16[4,256,1408]{2,1,0:T(8,128)(2,1)} %up_send.1.refs_7_), channel_id=1, source_target_pairs={{0,4},{1,5},{2,6},{3,7},{4,0},{5,1},{6,2},{7,3},{8,12},{9,13},{10,... | collective-permute-start | bytes 8650760 | tf_op jit(solution)/shard_map/ppermute | solution.py:76
  187.0 181.7 %reduce-scatter.8.cloned.1.call-start = ((), (), s32[]{:S(2)}) async-start(), calls=%async_computation.10 | async-start | bytes 3604480 | tf_op jit(solution)/shard_map/reduce_scatter | solution.py:772
  208.5 13.1 %collective-permute-start.17 = (bf16[2,512,2048]{2,1,0:T(8,128)(2,1)}, bf16[2,512,2048]{2,1,0:T(8,128)(2,1)}, u32[]{:S(2)}, u32[]{:S(2)}) collective-permute-start(bf16[2,512,2048]{2,1,0:T(8,128)(2,1)} %dn2_away.1.refs_7_), channel_id=1, source_target_pairs={{0,1},{1,0},{2,3},{3,2},{4,5},{5,4},{6,7},{7,6},{8,9},{9,8},{10,11... | collective-permute-start | bytes 12582920 | tf_op jit(solution)/shard_map/ppermute | solution.py:76
  220.5 119.7 %collective-permute-start.21 = (bf16[1408,1024]{1,0:T(8,128)(2,1)}, bf16[1408,1024]{1,0:T(8,128)(2,1)}, u32[]{:S(2)}, u32[]{:S(2)}) collective-permute-start(bf16[1408,1024]{1,0:T(8,128)(2,1)} %down_send.1.refs_8_), channel_id=1, source_target_pairs={{0,4},{1,5},{2,6},{3,7},{4,0},{5,1},{6,2},{7,3},{8,12},{9,13},{10,... | collective-permute-start | bytes 8650760 | tf_op jit(solution)/shard_map/ppermute | solution.py:76
  243.4 46.8 %collective-permute-start.22 = (bf16[512,2048]{1,0:T(8,128)(2,1)}, bf16[512,2048]{1,0:T(8,128)(2,1)}, u32[]{:S(2)}, u32[]{:S(2)}) collective-permute-start(bf16[512,2048]{1,0:T(8,128)(2,1)} %get-tuple-element.50.refs_4_), channel_id=1, source_target_pairs={{0,2},{1,3},{2,0},{3,1},{4,6},{5,7},{6,4},{7,5},{8,10},{9,11},{10,... | collective-permute-start | bytes 6291464 | tf_op jit(solution)/shard_map/ppermute | solution.py:76
  255.7 12.6 %collective-permute-start.18 = (bf16[2,512,2048]{2,1,0:T(8,128)(2,1)}, bf16[2,512,2048]{2,1,0:T(8,128)(2,1)}, u32[]{:S(2)}, u32[]{:S(2)}) collective-permute-start(bf16[2,512,2048]{2,1,0:T(8,128)(2,1)} %out_away.1.refs_8_), channel_id=1, source_target_pairs={{0,1},{1,0},{2,3},{3,2},{4,5},{5,4},{6,7},{7,6},{8,9},{9,8},{10,11... | collective-permute-start | bytes 12582920 | tf_op jit(solution)/shard_map/ppermute | solution.py:76
  268.2 148.1 %reduce-scatter.10.cloned.1.call-start = ((), (), s32[]{:S(2)}) async-start(), calls=%async_computation.11 | async-start | bytes 3604480 | tf_op jit(solution)/shard_map/reduce_scatter | solution.py:821
  281.4 72.7 %collective-permute-start.20 = (bf16[512,2048]{1,0:T(8,128)(2,1)}, bf16[512,2048]{1,0:T(8,128)(2,1)}, u32[]{:S(2)}, u32[]{:S(2)}) collective-permute-start(bf16[512,2048]{1,0:T(8,128)(2,1)} %get-tuple-element.52.refs_7_), channel_id=1, source_target_pairs={{0,2},{1,3},{2,0},{3,1},{4,6},{5,7},{6,4},{7,5},{8,10},{9,11},{10,... | collective-permute-start | bytes 6291464 | tf_op jit(solution)/shard_map/ppermute | solution.py:76
  307.5 58.0 %collective-permute-start.28 = (bf16[512,512]{1,0:T(8,128)(2,1)}, bf16[512,512]{1,0:T(8,128)(2,1)}, u32[]{:S(2)}, u32[]{:S(2)}) collective-permute-start(bf16[512,512]{1,0:T(8,128)(2,1)} %get-tuple-element.75.refs_12_), channel_id=1, source_target_pairs={{0,5},{1,4},{2,7},{3,6},{4,1},{5,0},{6,3},{7,2},{8,13},{9,12},{10,... | collective-permute-start | bytes 1572872 | tf_op jit(solution)/shard_map/ppermute | solution.py:76
  311.1 55.8 %collective-permute-start.27 = (bf16[512,512]{1,0:T(8,128)(2,1)}, bf16[512,512]{1,0:T(8,128)(2,1)}, u32[]{:S(2)}, u32[]{:S(2)}) collective-permute-start(bf16[512,512]{1,0:T(8,128)(2,1)} %get-tuple-element.76.refs_11_), channel_id=1, source_target_pairs={{0,4},{1,5},{2,6},{3,7},{4,0},{5,1},{6,2},{7,3},{8,12},{9,13},{10,... | collective-permute-start | bytes 1572872 | tf_op jit(solution)/shard_map/ppermute | solution.py:76
  312.1 29.5 %collective-permute-start.23 = (bf16[512,512]{1,0:T(8,128)(2,1)}, bf16[512,512]{1,0:T(8,128)(2,1)}, u32[]{:S(2)}, u32[]{:S(2)}) collective-permute-start(bf16[512,512]{1,0:T(8,128)(2,1)} %get-tuple-element.77.refs_10_), channel_id=1, source_target_pairs={{0,1},{1,0},{2,3},{3,2},{4,5},{5,4},{6,7},{7,6},{8,9},{9,8},{10,11... | collective-permute-start | bytes 1572872 | tf_op jit(solution)/shard_map/ppermute | solution.py:76
  312.1 23.1 %copy-start.25 = (f32[1,2048]{1,0:T(1,128)S(1)}, f32[1,2048]{1,0:T(1,128)}, u32[]{:S(2)}) copy-start(f32[1,2048]{1,0:T(1,128)} %get-tuple-element.64) | copy-start | bytes 24580
  340.3 21.1 %collective-permute-start.29 = (bf16[2,256,256]{2,1,0:T(8,128)(2,1)}, bf16[2,256,256]{2,1,0:T(8,128)(2,1)}, u32[]{:S(2)}, u32[]{:S(2)}) collective-permute-start(bf16[2,256,256]{2,1,0:T(8,128)(2,1)} %slice.87), channel_id=1, source_target_pairs={{8,0},{9,1},{10,2},{11,3},{12,4},{13,5},{14,6},{15,7},{16,8},{17,9... | collective-permute-start | bytes 786440 | tf_op jit(solution)/shard_map/ppermute | solution.py:88
  341.6 25.9 %collective-permute-start.26 = (bf16[512,512]{1,0:T(8,128)(2,1)}, bf16[512,512]{1,0:T(8,128)(2,1)}, u32[]{:S(2)}, u32[]{:S(2)}) collective-permute-start(bf16[512,512]{1,0:T(8,128)(2,1)} %get-tuple-element.71), channel_id=1, source_target_pairs={{0,5},{1,4},{2,7},{3,6},{4,1},{5,0},{6,3},{7,2},{8,13},{9,12},{10,... | collective-permute-start | bytes 1572872 | tf_op jit(solution)/shard_map/ppermute | solution.py:76
  355.1 13.6 %collective-permute-start.25 = (bf16[512,512]{1,0:T(8,128)(2,1)S(1)}, bf16[512,512]{1,0:T(8,128)(2,1)S(1)}, u32[]{:S(2)}, u32[]{:S(2)}) collective-permute-start(bf16[512,512]{1,0:T(8,128)(2,1)S(1)} %copy-done.20), channel_id=1, source_target_pairs={{0,4},{1,5},{2,6},{3,7},{4,0},{5,1},{6,2},{7,3},{8,12},{9,13},{10,... | collective-permute-start | bytes 1572872 | tf_op jit(solution)/shard_map/ppermute | solution.py:76
  362.4 6.3 %collective-permute-start.24 = (bf16[512,512]{1,0:T(8,128)(2,1)S(1)}, bf16[512,512]{1,0:T(8,128)(2,1)S(1)}, u32[]{:S(2)}, u32[]{:S(2)}) collective-permute-start(bf16[512,512]{1,0:T(8,128)(2,1)S(1)} %copy-done.19), channel_id=1, source_target_pairs={{0,1},{1,0},{2,3},{3,2},{4,5},{5,4},{6,7},{7,6},{8,9},{9,8},{10,11... | collective-permute-start | bytes 1572872 | tf_op jit(solution)/shard_map/ppermute | solution.py:76
  365.6 22.9 %collective-permute-start.30 = (bf16[2,256,256]{2,1,0:T(8,128)(2,1)}, bf16[2,256,256]{2,1,0:T(8,128)(2,1)}, u32[]{:S(2)}, u32[]{:S(2)}) collective-permute-start(bf16[2,256,256]{2,1,0:T(8,128)(2,1)} %add_convert_fusion), channel_id=1, source_target_pairs={{8,0},{9,1},{10,2},{11,3},{12,4},{13,5},{14,6},{15,7},{16,8},{17,9... | collective-permute-start | bytes 786440 | tf_op jit(solution)/shard_map/ppermute | solution.py:88
  366.9 71.7 %collective-permute-start.33 = (bf16[256,1408]{1,0:T(8,128)(2,1)}, bf16[256,1408]{1,0:T(8,128)(2,1)}, u32[]{:S(2)}, u32[]{:S(2)}) collective-permute-start(bf16[256,1408]{1,0:T(8,128)(2,1)} %dynamic-slice_bitcast_fusion), channel_id=1, source_target_pairs={{0,4},{1,5},{2,6},{3,7},{4,0},{5,1},{6,2},{7,3},{8,12},{9,13},{10,... | collective-permute-start | bytes 2162696 | tf_op jit(solution)/shard_map/ppermute | solution.py:76
  376.5 47.6 %collective-permute-start.32 = (bf16[2048,256]{1,0:T(8,128)(2,1)}, bf16[2048,256]{1,0:T(8,128)(2,1)}, u32[]{:S(2)}, u32[]{:S(2)}) collective-permute-start(bf16[2048,256]{1,0:T(8,128)(2,1)} %w_out_send.1.refs_9_), channel_id=1, source_target_pairs={{0,2},{1,3},{2,0},{3,1},{4,6},{5,7},{6,4},{7,5},{8,10},{9,11},{10,... | collective-permute-start | bytes 3145736 | tf_op jit(solution)/shard_map/ppermute | solution.py:76
  383.7 47.6 %collective-permute-start.31 = (bf16[2048,256]{1,0:T(8,128)(2,1)}, bf16[2048,256]{1,0:T(8,128)(2,1)}, u32[]{:S(2)}, u32[]{:S(2)}) collective-permute-start(bf16[2048,256]{1,0:T(8,128)(2,1)} %w_query_send.1.refs_0_.refs_10_), channel_id=1, source_target_pairs={{0,2},{1,3},{2,0},{3,1},{4,6},{5,7},{6,4},{7,5},{8,10},{9,11},{10,... | collective-permute-start | bytes 3145736 | tf_op jit(solution)/shard_map/ppermute | solution.py:76
  391.1 14.9 %copy-start.16 = (bf16[512,128]{1,0:T(8,128)(2,1)S(1)}, bf16[512,128]{1,0:T(8,128)(2,1)}, u32[]{:S(2)}) copy-start(bf16[512,128]{1,0:T(8,128)(2,1)} %copy-done.15) | copy-start | bytes 393220
  391.1 14.9 %copy-start.18 = (bf16[512,128]{1,0:T(8,128)(2,1)S(1)}, bf16[512,128]{1,0:T(8,128)(2,1)}, u32[]{:S(2)}) copy-start(bf16[512,128]{1,0:T(8,128)(2,1)} %copy-done.17) | copy-start | bytes 393220
  410.9 37.8 %all-to-all-start = ((bf16[8,4,64,384]{3,2,1,0:T(8,128)(2,1)}), bf16[8,4,64,384]{3,2,1,0:T(8,128)(2,1)}, u32[]{:S(2)}, u32[]{:S(2)}) async-start(bf16[8,4,64,384]{3,2,1,0:T(8,128)(2,1)} %bitcast.53), calls=%async_computation.3 | async-start | bytes 3145728 | tf_op jit(solution)/shard_map/all_to_all | solution.py:854
  416.3 58.1 %reduce-scatter.14.cloned.1.call-start = ((), (), s32[]{:S(2)}) async-start(), calls=%async_computation.13 | async-start | bytes 1310720 | tf_op jit(solution)/shard_map/reduce_scatter | solution.py:856
  418.4 39.0 %collective-permute-start.34 = (bf16[176,1024]{1,0:T(8,128)(2,1)}, bf16[176,1024]{1,0:T(8,128)(2,1)}, u32[]{:S(2)}, u32[]{:S(2)}) collective-permute-start(bf16[176,1024]{1,0:T(8,128)(2,1)} %get-tuple-element.81), channel_id=1, source_target_pairs={{0,0},{1,16},{2,8},{3,24},{4,1},{5,17},{6,9},{7,25},{8,2},{9,18},{... | collective-permute-start | bytes 1081352 | tf_op jit(solution)/shard_map/ppermute | solution.py:888
  422.2 35.1 %collective-permute-start.35 = (bf16[176,1024]{1,0:T(8,128)(2,1)}, bf16[176,1024]{1,0:T(8,128)(2,1)}, u32[]{:S(2)}, u32[]{:S(2)}) collective-permute-start(bf16[176,1024]{1,0:T(8,128)(2,1)} %get-tuple-element.82), channel_id=1, source_target_pairs={{0,1},{1,17},{2,9},{3,25},{4,0},{5,16},{6,8},{7,24},{8,3},{9,19},{... | collective-permute-start | bytes 1081352 | tf_op jit(solution)/shard_map/ppermute | solution.py:888
  448.6 25.8 %all-to-all-start.3 = ((bf16[4,2,64,1408]{3,2,1,0:T(8,128)(2,1)}), bf16[4,2,64,1408]{3,2,1,0:T(8,128)(2,1)S(1)}, u32[]{:S(2)}, u32[]{:S(2)}) async-start(bf16[4,2,64,1408]{3,2,1,0:T(8,128)(2,1)} %maximum_bitcast_fusion), calls=%async_computation.8 | async-start | bytes 2883584 | tf_op jit(solution)/shard_map/all_to_all | solution.py:913
  454.3 41.7 %reduce-scatter.12.cloned.1.call-start = ((), (), s32[]{:S(2)}) async-start(), calls=%async_computation.12 | async-start | bytes 1638400 | tf_op jit(solution)/shard_map/reduce_scatter | solution.py:868
  474.4 9.9 %all-to-all-start.2 = ((bf16[8,64,256]{2,1,0:T(8,128)(2,1)}), bf16[8,64,256]{2,1,0:T(8,128)(2,1)S(1)}, u32[]{:S(2)}, u32[]{:S(2)}) async-start(bf16[8,64,256]{2,1,0:T(8,128)(2,1)} %bitcast.72), calls=%async_computation.7 | async-start | bytes 524288 | tf_op jit(solution)/shard_map/all_to_all | solution.py:874
  498.4 9.2 %all-to-all-start.1 = ((bf16[8,64,256]{2,1,0:T(8,128)(2,1)}), bf16[8,64,256]{2,1,0:T(8,128)(2,1)S(1)}, u32[]{:S(2)}, u32[]{:S(2)}) async-start(bf16[8,64,256]{2,1,0:T(8,128)(2,1)} %bitcast.19), calls=%async_computation.5 | async-start | bytes 524288 | tf_op jit(solution)/shard_map/all_to_all | solution.py:874
  (30 other events, 99.4 us)
Sparse Core Ops, SparseCore 0:
  187.1 100.2 reduce-scatter.5
  289.8 58.7 reduce-scatter.7
  354.2 61.3 reduce-scatter.9
  431.5 31.7 reduce-scatter.13
  465.5 30.4 reduce-scatter.11
